TPU v7x, 128 devices: a whole 4x4x4 slice. The times are simulated.
128 devices in a mesh: dp: 4 (over y_hi, core), ctx: 32 (over y_lo, z, x).
Axes of the slice: x: 4, y: 4 (y_hi: 2, y_lo: 2; y = y_hi * 2 + y_lo), z: 4, core: 2. Of those that a mesh axis runs over, the one named last changes fastest.
Arguments:
- gate_values: bfloat16 [4, 4096, 4096], P('dp', 'ctx'), may hold values from -6 to 6
- conv_input: bfloat16 [4, 4096, 4096], P('dp', 'ctx'), may hold values from -6 to 6
- cotangent: bfloat16 [4, 4096, 4096], P('dp', 'ctx'), may hold values from -6 to 6
- filters: bfloat16 [256, 4096], P('ctx'), may hold values from -1.4 to 1.4
- direct_scale: float32 [4096], P('ctx'), may hold values from -1 to 1
Outputs:
- gate_grad: bfloat16 [4, 4096, 4096], P('dp', 'ctx')
- input_grad: bfloat16 [4, 4096, 4096], P('dp', 'ctx')
- filter_grad: float32 [256, 4096], P('ctx', 'dp')
All inputs are finite; a program needn't handle non-finite values.
Results may differ from a plain program's by a relative error of at most 0.012.
Values may be sent and summed in bfloat16 or wider, within the bound.
No kernel may reach another device: no remote copies, remote signals or barrier semaphores. Data moves between devices by JAX's collectives and lax.ppermute only.
A program may use at most 128 MiB of HBM per device.

v0:
```python
import math

import jax
import jax.numpy as jnp
import numpy as np
from jax import lax
from jax.experimental import pallas as pl
from jax.experimental.pallas import tpu as pltpu
from jax.sharding import PartitionSpec as P

GROUP_WIDTH = 16
OUTER = 32
INNER = 128
POINTS = 8192
LANES = 128
F32 = jnp.float32
BF16 = jnp.bfloat16


def turns(numerator, denominator):
    angle = 2.0 * np.pi * (np.asarray(numerator) % denominator) / denominator
    return np.cos(angle), np.sin(angle)


def build_tables(grad_scale):
    eye = np.eye(8)
    slab = np.arange(OUTER)[:, None, None]
    outer = np.arange(OUTER)[None, :, None]
    step = np.arange(8)[None, None, :]
    cos_part, sin_part = turns(slab * (128 * outer + step), POINTS)
    first = np.concatenate([cos_part, -sin_part], 0)
    first[0] = 1.0
    first[OUTER] = (1.0 - 2.0 * (np.arange(OUTER) % 2))[:, None]
    table_one = np.einsum("rns,st->rtns", first, eye).reshape(512, 256)
    table_last = table_one.T * (2.0 / POINTS)

    index = np.arange(INNER)
    cos_two, sin_two = turns(index[:, None] * index[None, :], INNER)
    table_two = np.block([[cos_two, sin_two], [-sin_two, cos_two]])
    half = np.arange(64)
    cos_low, sin_low = turns(half[:, None] * index[None, :], INNER)
    cos_mid, sin_mid = turns((32 + 64 * half[:, None]) * index[None, :], POINTS)
    zero = np.zeros((64, INNER))
    sin_low = -sin_low
    sin_low[0] = 1.0 - 2.0 * (index % 2)
    table_two_zero = np.block(
        [[cos_low, zero], [zero, cos_mid], [sin_low, zero], [zero, -sin_mid]]
    )
    weight = np.ones((256, 1))
    weight[0] = 0.5
    weight[128] = 0.5
    table_three = table_two.T
    table_three_zero = (table_two_zero * weight).T

    cos_q, sin_q = turns(np.arange(OUTER)[:, None] * 8 * np.arange(16)[None, :], POINTS)
    scalars = np.concatenate([cos_q.reshape(-1), sin_q.reshape(-1)])

    member = np.zeros((8, 256, LANES))
    for pair in range(8):
        for side in range(2):
            for channel in range(LANES):
                lane = (2 * pair + side) * 8 + channel // GROUP_WIDTH
                member[pair, side * LANES + channel, lane] = 1.0
    slab_lane = np.repeat(np.arange(OUTER), 8)
    group_lane = np.tile(np.arange(8), OUTER)
    turn_cos, turn_sin = turns(index[:, None] * slab_lane[None, :], POINTS)
    last_cos, last_sin = turns(slab_lane[:, None] * np.arange(OUTER)[None, :], 64)
    last_sin = -last_sin
    last_sin[slab_lane == 0] = 1.0 - 2.0 * (np.arange(OUTER) % 2)
    parts = np.stack([last_cos, last_sin])
    same = group_lane[:, None] == np.arange(8)[None, :]
    table_grad = np.einsum("pln,lg->plgn", parts, same)
    table_grad = table_grad.reshape(2, 256, 8, 4, 8).transpose(0, 1, 3, 2, 4)
    table_grad = table_grad.reshape(512, 256) * (2.0 * grad_scale)

    def low(values):
        return jnp.asarray(values, BF16)

    def wide(values):
        return jnp.asarray(values, F32)

    return dict(
        one=low(table_one),
        last=low(table_last),
        two=low(table_two),
        two_zero=low(table_two_zero),
        three=low(table_three),
        three_zero=low(table_three_zero),
        scalars=wide(scalars),
        member=low(member),
        turn_cos=wide(turn_cos),
        turn_sin=wide(turn_sin),
        grad=low(table_grad),
    )


def dot(left, right):
    return jnp.dot(left, right, preferred_element_type=F32)


def halves(values):
    values = values.astype(F32)
    rows = values.shape[0] * 8
    return jnp.concatenate(
        [values[:, :8].reshape(rows, LANES), values[:, 8:].reshape(rows, LANES)], 1
    )


def outer_stage(v_ref, one_ref, w_ref, u_ref):
    @pl.loop(0, 8)
    def _(p):
        row = pl.multiple_of(p * 16, 16)
        first = dot(one_ref[...], halves(v_ref[:, pl.ds(row, 16), :]).astype(BF16))
        for j in range(OUTER):
            real, imag = [], []
            for h in range(2):
                c = w_ref[j * 16 + 2 * p + h]
                s = w_ref[512 + j * 16 + 2 * p + h]
                fr = first[8 * j : 8 * j + 8, LANES * h : LANES * h + LANES]
                fi = first[256 + 8 * j : 264 + 8 * j, LANES * h : LANES * h + LANES]
                real.append(fr * c + fi * s)
                imag.append(fi * c - fr * s)
            u_ref[j, pl.ds(row, 16), :] = jnp.concatenate(real, 0).astype(BF16)
            u_ref[OUTER + j, pl.ds(row, 16), :] = jnp.concatenate(imag, 0).astype(BF16)


def load_pair(u_ref, j):
    return jnp.concatenate(
        [
            jnp.concatenate([u_ref[j], u_ref[j + 1]], 1),
            jnp.concatenate([u_ref[OUTER + j], u_ref[OUTER + j + 1]], 1),
        ],
        0,
    )


def load_one(u_ref, j):
    return jnp.concatenate([u_ref[j], u_ref[OUTER + j]], 0)


def load_spec(ref, j, count):
    if count == 1:
        return ref[j].astype(F32), ref[OUTER + j].astype(F32)
    return (
        jnp.concatenate([ref[j], ref[j + 1]], 1).astype(F32),
        jnp.concatenate([ref[OUTER + j], ref[OUTER + j + 1]], 1).astype(F32),
    )


def store_spec(ref, j, count, real, imag):
    for h in range(count):
        ref[j + h] = real[:, LANES * h : LANES * h + LANES].astype(ref.dtype)
        ref[OUTER + j + h] = imag[:, LANES * h : LANES * h + LANES].astype(ref.dtype)


def times(ar, ai, br, bi, conjugate, packed):
    cross = ai * bi
    if conjugate:
        real, imag = ar * br + cross, ar * bi - ai * br
    else:
        real, imag = ar * br - cross, ar * bi + ai * br
    if packed:
        edge = lax.broadcasted_iota(jnp.int32, ar.shape, 0) == 0
        real = jnp.where(edge, ar * br, real)
        imag = jnp.where(edge, cross, imag)
    return real, imag


def turn_back(u_ref, w_ref, j, count, back):
    for h in range(count):
        for q in range(0, 16, 2):
            real, imag = [], []
            for k in (q, q + 1):
                c = w_ref[(j + h) * 16 + k]
                s = w_ref[512 + (j + h) * 16 + k]
                br = back[8 * k : 8 * k + 8, LANES * h : LANES * h + LANES]
                bi = back[128 + 8 * k : 136 + 8 * k, LANES * h : LANES * h + LANES]
                real.append(br * c - bi * s)
                imag.append(br * s + bi * c)
            u_ref[j + h, 8 * q : 8 * q + 16, :] = jnp.concatenate(real, 0).astype(BF16)
            u_ref[OUTER + j + h, 8 * q : 8 * q + 16, :] = jnp.concatenate(imag, 0).astype(BF16)


def last_stage(u_ref, v_ref, gain_ref, last_ref, out_ref):
    @pl.loop(0, 8)
    def _(p):
        row = pl.multiple_of(p * 16, 16)
        lines = dot(last_ref[...], halves(u_ref[:, pl.ds(row, 16), :]).astype(BF16))
        gain = gain_ref[...]
        given = v_ref[:, pl.ds(row, 16), :].astype(F32)
        low = lines[:, :LANES].reshape(OUTER, 8, LANES) + gain * given[:, :8]
        high = lines[:, LANES:].reshape(OUTER, 8, LANES) + gain * given[:, 8:]
        out_ref[:, pl.ds(row, 16), :] = jnp.concatenate([low, high], 1).astype(BF16)


def slabs(body):
    body(0, 1, True)
    body(1, 1, False)

    @pl.loop(1, OUTER // 2)
    def _(m):
        body(2 * m, 2, False)


def filter_kernel(w_ref, v_ref, one_ref, two_ref, two_zero_ref, spec_ref, u_ref):
    outer_stage(v_ref, one_ref, w_ref, u_ref)

    def body(j, count, packed):
        held = load_one(u_ref, j) if count == 1 else load_pair(u_ref, j)
        spec = dot((two_zero_ref if packed else two_ref)[...], held)
        store_spec(spec_ref, j, count, spec[:128], spec[128:])

    slabs(body)


def input_kernel(
    w_ref, v_ref, h_ref, gain_ref, one_ref, two_ref, two_zero_ref, three_ref, three_zero_ref,
    last_ref, out_ref, spec_ref, u_ref,
):
    outer_stage(v_ref, one_ref, w_ref, u_ref)

    def body(j, count, packed):
        held = load_one(u_ref, j) if count == 1 else load_pair(u_ref, j)
        spec = dot((two_zero_ref if packed else two_ref)[...], held)
        xr, xi = spec[:128], spec[128:]
        store_spec(spec_ref, j, count, xr, xi)
        hr, hi = load_spec(h_ref, j, count)
        pr, pi = times(hr, hi, xr, xi, False, packed)
        product = jnp.concatenate([pr, pi], 0).astype(BF16)
        back = dot((three_zero_ref if packed else three_ref)[...], product)
        turn_back(u_ref, w_ref, j, count, back)

    slabs(body)
    last_stage(u_ref, v_ref, gain_ref, last_ref, out_ref)


def gradient_kernel(
    w_ref, v_ref, h_ref, x_ref, gain_ref, one_ref, two_ref, two_zero_ref, three_ref,
    three_zero_ref, last_ref, member_ref, turn_cos_ref, turn_sin_ref, grad_ref,
    out_ref, filter_ref, u_ref, sum_ref,
):
    outer_stage(v_ref, one_ref, w_ref, u_ref)
    sum_ref[...] = jnp.zeros_like(sum_ref)

    def body(j, count, packed):
        held = load_one(u_ref, j) if count == 1 else load_pair(u_ref, j)
        spec = dot((two_zero_ref if packed else two_ref)[...], held)
        gr, gi = spec[:128], spec[128:]
        hr, hi = load_spec(h_ref, j, count)
        pr, pi = times(hr, hi, gr, gi, True, packed)
        product = jnp.concatenate([pr, pi], 0).astype(BF16)
        back = dot((three_zero_ref if packed else three_ref)[...], product)
        turn_back(u_ref, w_ref, j, count, back)
        xr, xi = load_spec(x_ref, j, count)
        fr, fi = times(xr, xi, gr, gi, True, packed)
        both = jnp.concatenate([fr, fi], 0)
        high = both.astype(BF16)
        rest = (both - high.astype(F32)).astype(BF16)
        pair = (j // 2) % 8
        if count == 1:
            member = member_ref[pair, pl.ds(LANES * j, LANES), :]
        else:
            member = member_ref[pair]
        sum_ref[j // 16] += dot(high, member) + dot(rest, member)

    slabs(body)
    last_stage(u_ref, v_ref, gain_ref, last_ref, out_ref)

    total = jnp.concatenate([sum_ref[0], sum_ref[1]], 1).astype(BF16)
    back = dot(three_ref[...], total)
    back_zero = dot(three_zero_ref[...], total)
    packed = lax.broadcasted_iota(jnp.int32, back.shape, 1) < 8
    back = jnp.where(packed, back_zero, back)
    br, bi = back[:128], back[128:]
    c, s = turn_cos_ref[...], turn_sin_ref[...]
    turned = jnp.concatenate([br * c - bi * s, br * s + bi * c], 1).astype(BF16)
    filter_ref[...] = dot(turned, grad_ref[...]).T


SMEM_SPEC = pl.BlockSpec(memory_space=pltpu.SMEM)
VMEM_SPEC = pl.BlockSpec(memory_space=pltpu.VMEM)
PARAMS = pltpu.CompilerParams(vmem_limit_bytes=48 * 1024 * 1024)
BLOCK = jax.ShapeDtypeStruct((OUTER, INNER, LANES), BF16)
SPEC = jax.ShapeDtypeStruct((2 * OUTER, INNER, LANES), F32)
HELD = pltpu.VMEM((2 * OUTER, INNER, LANES), BF16)


def call(kernel, operands, outs, scratch, flops):
    return pl.pallas_call(
        kernel,
        out_shape=outs,
        in_specs=[SMEM_SPEC] + [VMEM_SPEC] * (len(operands) - 1),
        out_specs=jax.tree.map(lambda _: VMEM_SPEC, outs),
        scratch_shapes=scratch,
        compiler_params=PARAMS,
        cost_estimate=pl.CostEstimate(flops=flops, bytes_accessed=16 << 20, transcendentals=0),
    )(*operands)


def filter_spectrum(tables, spread):
    t = tables
    return call(
        filter_kernel,
        (t["scalars"], spread, t["one"], t["two"], t["two_zero"]),
        SPEC, [HELD], 2 << 30,
    )


def input_path(tables, moved, kernel_spec, gains):
    t = tables
    return call(
        input_kernel,
        (t["scalars"], moved, kernel_spec, gains, t["one"], t["two"], t["two_zero"],
         t["three"], t["three_zero"], t["last"]),
        (BLOCK, SPEC), [HELD], 4 << 30,
    )


def gradient_path(tables, moved, kernel_spec, input_spec, gains):
    t = tables
    return call(
        gradient_kernel,
        (t["scalars"], moved, kernel_spec, input_spec, gains, t["one"], t["two"], t["two_zero"],
         t["three"], t["three_zero"], t["last"], t["member"], t["turn_cos"], t["turn_sin"],
         t["grad"]),
        (BLOCK, jax.ShapeDtypeStruct((256, LANES), F32)),
        [HELD, pltpu.VMEM((2, 256, LANES), F32)],
        6 << 30,
    )


def spread_filters(filters):
    groups = filters.shape[0]
    member = np.repeat(np.eye(groups), LANES // groups, axis=1)
    return jnp.einsum(
        "gt,gc->tc", filters, jnp.asarray(member, BF16), preferred_element_type=F32
    ).astype(BF16).reshape(OUTER, INNER, LANES)


def exchange(blocks):
    return lax.all_to_all(blocks, "ctx", split_axis=0, concat_axis=0, tiled=True)


def by_channel(rows):
    return jnp.transpose(rows.reshape(INNER, OUTER, LANES), (1, 0, 2))


def by_position(blocks):
    return jnp.transpose(blocks, (1, 0, 2)).reshape(INNER, OUTER * LANES)


def on_device(gate_values, conv_input, cotangent, filters, direct_scale):
    replica_count = lax.axis_size("dp")
    grad_scale = 1.0 / (POINTS * math.sqrt(GROUP_WIDTH * replica_count * POINTS // 2))
    tables = build_tables(grad_scale)
    gains = direct_scale[None, :]
    moved_input = exchange(by_channel(conv_input[0]))
    gated = (cotangent[0].astype(F32) * gate_values[0].astype(F32)).astype(BF16)
    moved_grad = exchange(by_channel(gated))
    kernel_spec = filter_spectrum(tables, spread_filters(filters))
    mixed, input_spec = input_path(tables, moved_input, kernel_spec, gains)
    back_mixed = exchange(mixed)
    in_grad, filter_part = gradient_path(tables, moved_grad, kernel_spec, input_spec, gains)
    back_input = exchange(in_grad)
    filter_grad = lax.psum_scatter(
        filter_part.reshape(replica_count, -1, LANES), "dp", scatter_dimension=0, tiled=True
    ).reshape(filters.shape[0], -1)
    gate_grad = (cotangent[0].astype(F32) * by_position(back_mixed).astype(F32)).astype(BF16)
    return gate_grad[None], by_position(back_input)[None], filter_grad


def solution(mesh):
    placed = (
        P("dp", "ctx", None),
        P("dp", "ctx", None),
        P("dp", "ctx", None),
        P("ctx", None),
        P("ctx"),
    )
    return jax.shard_map(
        on_device,
        mesh=mesh,
        in_specs=placed,
        out_specs=(P("dp", "ctx", None), P("dp", "ctx", None), P("ctx", "dp")),
        check_vma=False,
    )
```

profile of v0, /device:TPU:0, one launch (start us, length us, event | category | flops | bytes accessed | tf_op | source)
XLA Modules:
  0.0 163.5 jit_solution(3429903594607857685)
XLA Ops:
  7.2 0.0 copy-start
  7.2 1.6 %copy.22 = bf16[1,128,4096]{1,2,0:T(8,128)(2,1)S(1)} copy(bf16[1,128,4096]{2,1,0:T(8,128)(2,1)} %param.18) | data formatting | bytes 2097152 | tf_op args[1]
  8.8 0.0 copy-start.16
  8.8 1.3 copy.23
  10.2 9.3 %all-to-all-start = ((bf16[32,128,128]{2,1,0:T(8,128)(2,1)}), bf16[32,128,128]{2,1,0:T(8,128)(2,1)S(1)}, u32[]{:S(2)}, u32[]{:S(2)}) async-start(bf16[32,128,128]{2,1,0:T(8,128)(2,1)} %bitcast.1), calls=%async_computation | async-start | bytes 2097152 | tf_op jit(solution)/shard_map/all_to_all | solution.py:341
  19.4 0.0 copy-done
  19.4 0.0 copy-done.16
  19.4 0.0 copy-start.3
  19.5 0.0 copy-start.6
  19.5 0.0 copy-start.7
  19.5 0.0 copy-start.12
  19.5 1.4 fusion
  20.9 1.6 copy.24
  22.6 0.0 copy-done.3
  22.6 0.0 copy-done.6
  22.6 0.0 copy-done.7
  22.6 0.0 copy-done.12
  22.6 0.0 copy-start.1
  22.6 0.0 copy-start.4
  22.6 0.0 copy-start.8
  22.6 0.0 copy-start.9
  22.6 5.6 %shard_map.184.h_ref = f32[64,128,128]{2,1,0:T(8,128)S(1)} custom-call(f32[1024]{0:T(1024)S(1)} %copy-done.12, bf16[32,128,128]{2,1,0:T(8,128)(2,1)S(1)} %bitcast.17, bf16[512,256]{1,0:T(8,128)(2,1)S(1)} %copy-done.3, bf16[256,256]{1,0:T(8,128)(2,1)S(1)} %copy-done.6, bf16[256,256]{1,0:T(8,128)(2,1)S(1)} %copy-done.7), custom_call_target="tpu_custom_call" | custom-call | flops 2147483648 | bytes 16777216 | tf_op jit(solution)/shard_map/pallas_call | solution.py:289
  28.3 0.0 copy-start.13
  28.3 1.9 %copy-done.13 = f32[64,128,128]{2,1,0:T(8,128)} copy-done((f32[64,128,128]{2,1,0:T(8,128)}, f32[64,128,128]{2,1,0:T(8,128)S(1)}, u32[]{:S(2)}) %copy-start.13) | copy-done | bytes 4194328
  30.2 6.3 %all-to-all-done.v_ref = bf16[32,128,128]{2,1,0:T(8,128)(2,1)S(1)} async-done(((bf16[32,128,128]{2,1,0:T(8,128)(2,1)}), bf16[32,128,128]{2,1,0:T(8,128)(2,1)S(1)}, u32[]{:S(2)}, u32[]{:S(2)}) %all-to-all-start) | async-done | bytes 1048608 | tf_op jit(solution)/shard_map/all_to_all | solution.py:341
  36.5 0.0 copy-done.1
  36.5 0.0 copy-done.4
  36.5 0.0 copy-done.8
  36.5 0.0 copy-done.9
  36.5 15.1 %shard_map.185 = (bf16[32,128,128]{2,1,0:T(8,128)(2,1)}, f32[64,128,128]{2,1,0:T(8,128)}) custom-call(f32[1024]{0:T(1024)S(1)} %copy-done.12, bf16[32,128,128]{2,1,0:T(8,128)(2,1)S(1)} %all-to-all-done.v_ref, f32[64,128,128]{2,1,0:T(8,128)} %copy-done.13, f32[1,128]{1,0:T(1,128)S(1)} %bitcast.18, bf16[512,256]{1,0:T(8,128)(2,1)S(1)} %copy-done.3, ...), custom_call_target="tpu_custom_call" | custom-call | flops 4294967296 | bytes 16777216 | tf_op jit(solution)/shard_map/pallas_call | solution.py:289
  51.6 0.0 copy-start.15
  51.6 4.3 %all-to-all-start.1 = ((bf16[32,128,128]{2,1,0:T(8,128)(2,1)}), bf16[32,128,128]{2,1,0:T(8,128)(2,1)S(1)}, u32[]{:S(2)}, u32[]{:S(2)}) async-start(bf16[32,128,128]{2,1,0:T(8,128)(2,1)} %get-tuple-element.7), calls=%async_computation.1 | async-start | bytes 2097152 | tf_op jit(solution)/shard_map/all_to_all | solution.py:341
  55.9 0.0 copy-done.15
  56.0 1.3 copy.21
  57.3 2.3 %copy.26 = bf16[1,128,4096]{1,2,0:T(8,128)(2,1)} copy(bf16[1,128,4096]{2,1,0:T(8,128)(2,1)} %param.17) | data formatting | bytes 2097152 | tf_op args[0]
  59.5 12.6 %all-to-all-done.1 = bf16[32,128,128]{2,1,0:T(8,128)(2,1)S(1)} async-done(((bf16[32,128,128]{2,1,0:T(8,128)(2,1)}), bf16[32,128,128]{2,1,0:T(8,128)(2,1)S(1)}, u32[]{:S(2)}, u32[]{:S(2)}) %all-to-all-start.1) | async-done | bytes 1048608 | tf_op jit(solution)/shard_map/all_to_all | solution.py:341
  72.1 1.6 convert_bitcast_fusion
  73.7 1.9 %copy.25 = f32[128,32,128]{0,2,1:T(8,128)S(1)} copy(f32[128,32,128]{2,0,1:T(8,128)} %convert_bitcast_fusion) | data formatting | bytes 4194304 | tf_op jit(solution)/shard_map/convert_element_type | solution.py:368
  75.7 3.3 %fusion.2 = (bf16[1,128,4096]{1,2,0:T(8,128)(2,1)}, bf16[1,128,4096]{1,2,0:T(8,128)(2,1)}) fusion(bf16[1,128,4096]{1,2,0:T(8,128)(2,1)} %copy.21, bf16[1,128,4096]{1,2,0:T(8,128)(2,1)} %copy.26, f32[128,32,128]{0,2,1:T(8,128)S(1)} %copy.25), kind=kLoop, calls=%fused_computation.5 | loop fusion | flops 3145728 | bytes 6291456 | tf_op jit(solution)/shard_map/convert_element_type | solution.py:358
  78.9 0.0 copy-start.2
  78.9 0.0 copy-start.5
  78.9 0.0 copy-start.10
  78.9 0.0 copy-start.11
  78.9 1.7 %copy.27 = bf16[128,32,128]{2,0,1:T(8,128)(2,1)S(1)} copy(bf16[128,32,128]{0,2,1:T(8,128)(2,1)} %bitcast.24) | data formatting | bytes 2097152 | tf_op jit(solution)/shard_map/convert_element_type | solution.py:358
  80.7 19.9 %all_to_all.20.v_ref = bf16[32,128,128]{2,1,0:T(8,128)(2,1)S(1)} all-to-all(bf16[32,128,128]{2,1,0:T(8,128)(2,1)S(1)} %bitcast.21), channel_id=1, replica_groups=mesh['dp'=4,'ctx'=32] {'ctx'}, dimensions={0} | all-to-all | bytes 2097152 | tf_op jit(solution)/shard_map/all_to_all | solution.py:341
  100.5 0.0 copy-done.2
  100.5 0.0 copy-done.5
  100.5 0.0 copy-done.10
  100.5 0.0 copy-done.11
  100.6 17.2 %shard_map.186 = (bf16[32,128,128]{2,1,0:T(8,128)(2,1)}, f32[256,128]{1,0:T(8,128)}) custom-call(f32[1024]{0:T(1024)S(1)} %copy-done.12, bf16[32,128,128]{2,1,0:T(8,128)(2,1)S(1)} %all_to_all.20.v_ref, f32[64,128,128]{2,1,0:T(8,128)} %copy-done.13, f32[64,128,128]{2,1,0:T(8,128)} %get-tuple-element.8.x_ref, f32[1,128]{1,0:T(1,128)S(1)} %bitcast.19, ...), custom_call_target="tpu_custom_call" | custom-call | flops 6442450944 | bytes 16777216 | tf_op jit(solution)/shard_map/pallas_call | solution.py:289
  117.7 0.0 copy-start.14
  117.7 4.3 %all-to-all-start.3 = ((bf16[32,128,128]{2,1,0:T(8,128)(2,1)}), bf16[32,128,128]{2,1,0:T(8,128)(2,1)S(1)}, u32[]{:S(2)}, u32[]{:S(2)}) async-start(bf16[32,128,128]{2,1,0:T(8,128)(2,1)} %get-tuple-element.9), calls=%async_computation.3 | async-start | bytes 2097152 | tf_op jit(solution)/shard_map/all_to_all | solution.py:341
  122.0 0.0 reduce-scatter.2.cloned.1.call-start
  122.1 0.7 reduce-scatter.2.cloned.1.call-update
  122.8 0.0 copy-done.14
  122.8 1.3 copy.29
  124.1 29.2 %reduce-scatter.2.cloned.1.call-done = f32[1,64,128]{2,1,0:T(8,128)} async-done(((f32[4,64,128]{2,1,0:T(8,128)}), f32[1,64,128]{2,1,0:T(8,128)}) %reduce-scatter.2.cloned.1.call-update) | async-done | bytes 32784 | tf_op jit(solution)/shard_map/reduce_scatter | solution.py:365
  153.2 1.4 reshape.37
  154.6 0.0 all-to-all-done.3
  154.6 0.7 copy.28
  155.3 1.3 copy.30
Async XLA Ops:
  7.2 12.3 %copy-start = (bf16[8,4096]{1,0:T(8,128)(2,1)S(1)}, bf16[8,4096]{1,0:T(8,128)(2,1)}, u32[]{:S(2)}) copy-start(bf16[8,4096]{1,0:T(8,128)(2,1)} %param.20) | copy-start | bytes 196612
  8.8 10.6 %copy-start.16 = (bf16[8,128]{1,0:T(8,128)(2,1)S(1)}, bf16[8,128]{1,0:T(8,128)(2,1)}, u32[]{:S(2)}) copy-start(bf16[8,128]{1,0:T(8,128)(2,1)} %constant.35.clone) | copy-start | bytes 6148
  10.2 26.3 %all-to-all-start = ((bf16[32,128,128]{2,1,0:T(8,128)(2,1)}), bf16[32,128,128]{2,1,0:T(8,128)(2,1)S(1)}, u32[]{:S(2)}, u32[]{:S(2)}) async-start(bf16[32,128,128]{2,1,0:T(8,128)(2,1)} %bitcast.1), calls=%async_computation | async-start | bytes 2097152 | tf_op jit(solution)/shard_map/all_to_all | solution.py:341
  19.4 3.1 %copy-start.3 = (bf16[512,256]{1,0:T(8,128)(2,1)S(1)}, bf16[512,256]{1,0:T(8,128)(2,1)}, u32[]{:S(2)}) copy-start(bf16[512,256]{1,0:T(8,128)(2,1)} %constant.24.clone.one_ref) | copy-start | bytes 786436
  19.5 3.1 %copy-start.6 = (bf16[256,256]{1,0:T(8,128)(2,1)S(1)}, bf16[256,256]{1,0:T(8,128)(2,1)}, u32[]{:S(2)}) copy-start(bf16[256,256]{1,0:T(8,128)(2,1)} %constant.26.clone.two_ref) | copy-start | bytes 393220
  19.5 3.1 %copy-start.7 = (bf16[256,256]{1,0:T(8,128)(2,1)S(1)}, bf16[256,256]{1,0:T(8,128)(2,1)}, u32[]{:S(2)}) copy-start(bf16[256,256]{1,0:T(8,128)(2,1)} %constant.27.clone.two_zero_ref) | copy-start | bytes 393220
  19.5 3.1 %copy-start.12 = (f32[1024]{0:T(1024)S(1)}, f32[1024]{0:T(1024)}, u32[]{:S(2)}) copy-start(f32[1024]{0:T(1024)} %constant.30.clone.w_ref) | copy-start | bytes 12292
  22.6 13.9 %copy-start.1 = (f32[128]{0:T(128)S(1)}, f32[128]{0:T(128)}, u32[]{:S(2)}) copy-start(f32[128]{0:T(128)} %param.21) | copy-start | bytes 1540
  22.6 13.9 %copy-start.4 = (bf16[256,512]{1,0:T(8,128)(2,1)S(1)}, bf16[256,512]{1,0:T(8,128)(2,1)}, u32[]{:S(2)}) copy-start(bf16[256,512]{1,0:T(8,128)(2,1)} %constant.25.clone.last_ref) | copy-start | bytes 786436
  22.6 13.9 %copy-start.8 = (bf16[256,256]{1,0:T(8,128)(2,1)S(1)}, bf16[256,256]{1,0:T(8,128)(2,1)}, u32[]{:S(2)}) copy-start(bf16[256,256]{1,0:T(8,128)(2,1)} %constant.28.clone.three_ref) | copy-start | bytes 393220
  22.6 13.9 %copy-start.9 = (bf16[256,256]{1,0:T(8,128)(2,1)S(1)}, bf16[256,256]{1,0:T(8,128)(2,1)}, u32[]{:S(2)}) copy-start(bf16[256,256]{1,0:T(8,128)(2,1)} %constant.29.clone.three_zero_ref) | copy-start | bytes 393220
  28.3 1.9 %copy-start.13 = (f32[64,128,128]{2,1,0:T(8,128)}, f32[64,128,128]{2,1,0:T(8,128)S(1)}, u32[]{:S(2)}) copy-start(f32[64,128,128]{2,1,0:T(8,128)S(1)} %shard_map.184.h_ref) | copy-start | bytes 12582916
  51.6 4.3 %copy-start.15 = (bf16[1,128,4096]{2,1,0:T(8,128)(2,1)S(1)}, bf16[1,128,4096]{2,1,0:T(8,128)(2,1)}, u32[]{:S(2)}) copy-start(bf16[1,128,4096]{2,1,0:T(8,128)(2,1)} %param.19) | copy-start | bytes 3145732
  51.6 20.5 %all-to-all-start.1 = ((bf16[32,128,128]{2,1,0:T(8,128)(2,1)}), bf16[32,128,128]{2,1,0:T(8,128)(2,1)S(1)}, u32[]{:S(2)}, u32[]{:S(2)}) async-start(bf16[32,128,128]{2,1,0:T(8,128)(2,1)} %get-tuple-element.7), calls=%async_computation.1 | async-start | bytes 2097152 | tf_op jit(solution)/shard_map/all_to_all | solution.py:341
  78.9 21.6 %copy-start.2 = (bf16[8,256,128]{2,1,0:T(8,128)(2,1)S(1)}, bf16[8,256,128]{2,1,0:T(8,128)(2,1)}, u32[]{:S(2)}) copy-start(bf16[8,256,128]{2,1,0:T(8,128)(2,1)} %constant.31.clone.member_ref) | copy-start | bytes 1572868
  78.9 21.6 %copy-start.5 = (bf16[512,256]{1,0:T(8,128)(2,1)S(1)}, bf16[512,256]{1,0:T(8,128)(2,1)}, u32[]{:S(2)}) copy-start(bf16[512,256]{1,0:T(8,128)(2,1)} %constant.34.clone.grad_ref) | copy-start | bytes 786436
  78.9 21.6 %copy-start.10 = (f32[128,256]{1,0:T(8,128)S(1)}, f32[128,256]{1,0:T(8,128)}, u32[]{:S(2)}) copy-start(f32[128,256]{1,0:T(8,128)} %constant.32.clone.turn_cos_ref) | copy-start | bytes 393220
  78.9 21.6 %copy-start.11 = (f32[128,256]{1,0:T(8,128)S(1)}, f32[128,256]{1,0:T(8,128)}, u32[]{:S(2)}) copy-start(f32[128,256]{1,0:T(8,128)} %constant.33.clone.turn_sin_ref) | copy-start | bytes 393220
  117.7 5.0 %copy-start.14 = (bf16[1,128,4096]{1,2,0:T(8,128)(2,1)S(1)}, bf16[1,128,4096]{1,2,0:T(8,128)(2,1)}, u32[]{:S(2)}) copy-start(bf16[1,128,4096]{1,2,0:T(8,128)(2,1)} %get-tuple-element.15) | copy-start | bytes 3145732
  117.7 36.9 %all-to-all-start.3 = ((bf16[32,128,128]{2,1,0:T(8,128)(2,1)}), bf16[32,128,128]{2,1,0:T(8,128)(2,1)S(1)}, u32[]{:S(2)}, u32[]{:S(2)}) async-start(bf16[32,128,128]{2,1,0:T(8,128)(2,1)} %get-tuple-element.9), calls=%async_computation.3 | async-start | bytes 2097152 | tf_op jit(solution)/shard_map/all_to_all | solution.py:341
  122.0 31.2 %reduce-scatter.2.cloned.1.call-start = ((), (), s32[]{:S(2)}) async-start(), calls=%async_computation.5 | async-start | bytes 163840 | tf_op jit(solution)/shard_map/reduce_scatter | solution.py:365
Sparse Core Ops, SparseCore 0:
  125.4 27.8 reduce-scatter.1
where the time goes:
time: 164 us; the launch traced here: 163 us
  waiting for transfers between devices  48.7 us (30%)
  Pallas kernels  37.9 us (23%)
  blocking collectives  19.9 us (12%)
  local copies, waits for them, and re-layouts  18.4 us (11%)
  starting transfers between devices  17.9 us (11%)
  between operations  14.3 us (9%)
  other arithmetic  4.9 us (3%)
    pallas_call x3, Pallas kernels, call(): pl.pallas_call(kernel, out_shape=outs, in_specs=[SMEM_SPEC] + [VMEM_SPEC]...  37.9 us
    reduce_scatter x1, waiting for transfers between devices, on_device(): lax.psum_scatter(filter_part.reshape(replica_count, -1, LANES), 'dp', sca...  29.2 us
    all_to_all x1, blocking collectives, exchange(): lax.all_to_all(blocks, 'ctx', split_axis=0, concat_axis=0, tiled=True)  19.9 us
    all_to_all x3, waiting for transfers between devices, exchange(): lax.all_to_all(blocks, 'ctx', split_axis=0, concat_axis=0, tiled=True)  18.9 us
    all_to_all x3, starting transfers between devices, exchange(): lax.all_to_all(blocks, 'ctx', split_axis=0, concat_axis=0, tiled=True)  17.9 us
    unnamed x39, local copies, waits for them, and re-layouts  9.86 us
  transfers between devices with their start and end apart: 4, of which 3 were waited for; matrix products, arithmetic and copies ran while one was open for 6% of the time, Pallas kernels for 3%

commit v1 on v0

v1 whole, which is shorter than its diff:
```python
import math

import jax
import jax.numpy as jnp
import numpy as np
from jax import lax
from jax.experimental import pallas as pl
from jax.experimental.pallas import tpu as pltpu
from jax.sharding import PartitionSpec as P

GROUP_WIDTH = 16
OUTER = 32
INNER = 128
POINTS = 8192
LANES = 128
PAIR = 2 * LANES
F32 = jnp.float32
BF16 = jnp.bfloat16


def turns(numerator, denominator):
    angle = 2.0 * np.pi * (np.asarray(numerator) % denominator) / denominator
    return np.cos(angle), np.sin(angle)


def build_tables(grad_scale):
    eye = np.eye(8)
    slab = np.arange(OUTER)[:, None, None]
    outer = np.arange(OUTER)[None, :, None]
    step = np.arange(INNER)[None, None, :]
    cos_part, sin_part = turns(slab * (128 * outer + step), POINTS)
    first = np.concatenate([cos_part, -sin_part], 0)
    first[0] = 1.0
    first[OUTER] = (1.0 - 2.0 * (np.arange(OUTER) % 2))[:, None]
    table_one = np.einsum("rnqs,st->qrtns", first.reshape(64, OUTER, 16, 8), eye)
    table_one = table_one.reshape(16, 512, 256)
    table_last = table_one.transpose(0, 2, 1) * (2.0 / POINTS)

    index = np.arange(INNER)
    cos_two, sin_two = turns(index[:, None] * index[None, :], INNER)
    table_two = np.block([[cos_two, sin_two], [-sin_two, cos_two]])
    half = np.arange(64)
    cos_low, sin_low = turns(half[:, None] * index[None, :], INNER)
    cos_mid, sin_mid = turns((32 + 64 * half[:, None]) * index[None, :], POINTS)
    zero = np.zeros((64, INNER))
    sin_low = -sin_low
    sin_low[0] = 1.0 - 2.0 * (index % 2)
    table_two_zero = np.block(
        [[cos_low, zero], [zero, cos_mid], [sin_low, zero], [zero, -sin_mid]]
    )
    weight = np.ones((256, 1))
    weight[0] = 0.5
    weight[128] = 0.5
    table_three = table_two.T
    table_three_zero = (table_two_zero * weight).T

    member = np.zeros((8, 256, LANES))
    for pair in range(8):
        for side in range(2):
            for channel in range(LANES):
                lane = (2 * pair + side) * 8 + channel // GROUP_WIDTH
                member[pair, side * LANES + channel, lane] = 1.0
    slab_lane = np.repeat(np.arange(OUTER), 8)
    group_lane = np.tile(np.arange(8), OUTER)
    turn_cos, turn_sin = turns(index[:, None] * slab_lane[None, :], POINTS)
    last_cos, last_sin = turns(slab_lane[:, None] * np.arange(OUTER)[None, :], 64)
    last_sin = -last_sin
    last_sin[slab_lane == 0] = 1.0 - 2.0 * (np.arange(OUTER) % 2)
    parts = np.stack([last_cos, last_sin])
    same = group_lane[:, None] == np.arange(8)[None, :]
    table_grad = np.einsum("pln,lg->plgn", parts, same)
    table_grad = table_grad.reshape(2, 256, 8, 4, 8).transpose(0, 1, 3, 2, 4)
    table_grad = table_grad.reshape(512, 256) * (2.0 * grad_scale)

    def low(values):
        return jnp.asarray(values, BF16)

    def wide(values):
        return jnp.asarray(values, F32)

    return dict(
        one=low(table_one),
        last=low(table_last),
        two=low(table_two),
        two_zero=low(table_two_zero),
        three=low(table_three),
        three_zero=low(table_three_zero),
        member=low(member),
        turn_cos=wide(turn_cos),
        turn_sin=wide(turn_sin),
        grad=low(table_grad),
    )


def dot(left, right):
    return jnp.dot(left, right, preferred_element_type=F32)


def outer_stage(load, one_ref, u_ref):
    @pl.loop(0, 8)
    def _(p):
        row = pl.multiple_of(p * 16, 16)
        given = load(row)
        lanes = given.shape[2]
        out = []
        for h in range(2):
            held = given[:, 8 * h : 8 * h + 8].reshape(256, lanes).astype(BF16)
            out.append(dot(one_ref[2 * p + h], held).reshape(64, 8, lanes))
        u_ref[:, pl.ds(row, 16), :] = jnp.concatenate(out, 1).astype(BF16)


def slab_matrix(u_ref, start, count):
    real = [u_ref[start + k] for k in range(count)]
    imag = [u_ref[OUTER + start + k] for k in range(count)]
    return jnp.concatenate([jnp.concatenate(real, 1), jnp.concatenate(imag, 1)], 0)


def times(ar, ai, br, bi, conjugate, packed):
    cross = ai * bi
    if conjugate:
        real, imag = ar * br + cross, ar * bi - ai * br
    else:
        real, imag = ar * br - cross, ar * bi + ai * br
    if packed:
        edge = lax.broadcasted_iota(jnp.int32, ar.shape, 0) == 0
        real = jnp.where(edge, ar * br, real)
        imag = jnp.where(edge, cross, imag)
    return real, imag


def slabs(body, count):
    body(0, 1, True)
    body(1, count - 1, False)

    @pl.loop(1, OUTER // count)
    def _(m):
        body(count * m, count, False)


def filter_kernel(v_ref, one_ref, two_ref, two_zero_ref, spec_ref, u_ref):
    outer_stage(lambda row: v_ref[:, pl.ds(row, 16), :].astype(F32), one_ref, u_ref)

    def body(start, count, packed):
        spec = dot((two_zero_ref if packed else two_ref)[...], slab_matrix(u_ref, start, count))
        for k in range(count):
            spec_ref[start + k] = spec[:INNER, LANES * k : LANES * k + LANES]
            spec_ref[OUTER + start + k] = spec[INNER:, LANES * k : LANES * k + LANES]

    slabs(body, 4)


def main_kernel(
    v_ref, h_ref, gain_ref, one_ref, two_ref, two_zero_ref, three_ref, three_zero_ref, last_ref,
    out_ref, u_ref, back_ref,
):
    def load(row):
        both = v_ref[:, :, pl.ds(row, 16), :].astype(F32)
        return jnp.concatenate([both[:, 0], both[:, 1]], 2)

    outer_stage(load, one_ref, u_ref)

    def body(start, count, packed):
        spec = dot((two_zero_ref if packed else two_ref)[...], slab_matrix(u_ref, start, count))
        top, bottom = [], []
        for k in range(count):
            real = spec[:INNER, PAIR * k : PAIR * k + PAIR]
            imag = spec[INNER:, PAIR * k : PAIR * k + PAIR]
            hr, hi = h_ref[start + k], h_ref[OUTER + start + k]
            pr, pi = times(hr, hi, real[:, :LANES], imag[:, :LANES], False, packed)
            ar, ai = times(hr, hi, real[:, LANES:], imag[:, LANES:], True, packed)
            top += [pr, ar]
            bottom += [pi, ai]
        product = jnp.concatenate(
            [jnp.concatenate(top, 1), jnp.concatenate(bottom, 1)], 0
        ).astype(BF16)
        back = dot((three_zero_ref if packed else three_ref)[...], product)
        for k in range(count):
            u_ref[start + k] = spec[:INNER, PAIR * k : PAIR * k + PAIR].astype(BF16)
            u_ref[OUTER + start + k] = spec[INNER:, PAIR * k : PAIR * k + PAIR].astype(BF16)
            back_ref[start + k] = back[:INNER, PAIR * k : PAIR * k + PAIR]
            back_ref[OUTER + start + k] = back[INNER:, PAIR * k : PAIR * k + PAIR]

    slabs(body, 4)

    @pl.loop(0, 8)
    def _(p):
        row = pl.multiple_of(p * 16, 16)
        gain = gain_ref[...]
        given = v_ref[:, :, pl.ds(row, 16), :].astype(F32)
        out = [[], []]
        for h in range(2):
            held = back_ref[:, pl.ds(row + 8 * h, 8), :].reshape(512, PAIR).astype(BF16)
            lines = dot(last_ref[2 * p + h], held).reshape(OUTER, 8, PAIR)
            for a in range(2):
                out[a].append(
                    lines[:, :, LANES * a : LANES * a + LANES]
                    + gain * given[:, a, 8 * h : 8 * h + 8]
                )
        for a in range(2):
            out_ref[:, a, pl.ds(row, 16), :] = jnp.concatenate(out[a], 1).astype(BF16)


def filter_grad_kernel(
    spec_ref, two_ref, member_ref, three_ref, three_zero_ref, turn_cos_ref, turn_sin_ref, grad_ref,
    filter_ref, sum_ref,
):
    sum_ref[...] = jnp.zeros_like(sum_ref)

    def body(start, count, packed):
        for k in range(count):
            real = spec_ref[start + k].astype(F32)
            imag = spec_ref[OUTER + start + k].astype(F32)
            fr, fi = times(
                real[:, :LANES], imag[:, :LANES], real[:, LANES:], imag[:, LANES:], True, packed
            )
            both = jnp.concatenate([fr, fi], 0)
            high = both.astype(BF16)
            rest = (both - high.astype(F32)).astype(BF16)
            slab = start + k
            member = member_ref[(slab // 2) % 8, pl.ds(LANES * (slab % 2), LANES), :]
            sum_ref[slab // 16] += dot(high, member) + dot(rest, member)

    slabs(body, 4)
    total = jnp.concatenate([sum_ref[0], sum_ref[1]], 1).astype(BF16)
    back = dot(three_ref[...], total)
    back_zero = dot(three_zero_ref[...], total)
    packed = lax.broadcasted_iota(jnp.int32, back.shape, 1) < 8
    back = jnp.where(packed, back_zero, back)
    br, bi = back[:INNER], back[INNER:]
    c, s = turn_cos_ref[...], turn_sin_ref[...]
    turned = jnp.concatenate([br * c - bi * s, br * s + bi * c], 1).astype(BF16)
    filter_ref[...] = dot(turned, grad_ref[...]).T


def gather_kernel(gate_ref, input_ref, cotan_ref, out_ref):
    for k in range(out_ref.shape[0]):
        cut = slice(LANES * k, LANES * k + LANES)
        out_ref[k, 0] = input_ref[:, cut]
        product = cotan_ref[:, cut].astype(F32) * gate_ref[:, cut].astype(F32)
        out_ref[k, 1] = product.astype(BF16)


def spread_kernel(back_ref, cotan_ref, gate_grad_ref, input_grad_ref):
    for k in range(back_ref.shape[0]):
        cut = slice(LANES * k, LANES * k + LANES)
        product = cotan_ref[:, cut].astype(F32) * back_ref[k, 0].astype(F32)
        gate_grad_ref[:, cut] = product.astype(BF16)
        input_grad_ref[:, cut] = back_ref[k, 1]


STEPS = 8
ROWS_BLOCK = pl.BlockSpec((INNER, OUTER // STEPS * LANES), lambda i: (0, i))
MOVED_BLOCK = pl.BlockSpec((OUTER // STEPS, 2, INNER, LANES), lambda i: (i, 0, 0, 0))
MOVED = jax.ShapeDtypeStruct((OUTER, 2, INNER, LANES), BF16)
ROWS = jax.ShapeDtypeStruct((INNER, OUTER * LANES), BF16)
HELD = jax.ShapeDtypeStruct((2 * OUTER, INNER, PAIR), BF16)


def gather(gate, given, cotan):
    return pl.pallas_call(
        gather_kernel,
        grid=(STEPS,),
        out_shape=MOVED,
        in_specs=[ROWS_BLOCK] * 3,
        out_specs=MOVED_BLOCK,
        compiler_params=pltpu.CompilerParams(vmem_limit_bytes=8 << 20),
    )(gate, given, cotan)


def spread(back, cotan):
    return pl.pallas_call(
        spread_kernel,
        grid=(STEPS,),
        out_shape=(ROWS, ROWS),
        in_specs=[MOVED_BLOCK, ROWS_BLOCK],
        out_specs=(ROWS_BLOCK, ROWS_BLOCK),
        compiler_params=pltpu.CompilerParams(vmem_limit_bytes=8 << 20),
    )(back, cotan)


def call(kernel, operands, outs, scratch, flops, limit):
    space = pl.BlockSpec(memory_space=pltpu.VMEM)
    return pl.pallas_call(
        kernel,
        out_shape=outs,
        in_specs=[space] * len(operands),
        out_specs=jax.tree.map(lambda _: space, outs),
        scratch_shapes=scratch,
        compiler_params=pltpu.CompilerParams(vmem_limit_bytes=limit),
        cost_estimate=pl.CostEstimate(flops=flops, bytes_accessed=16 << 20, transcendentals=0),
    )(*operands)


def filter_spectrum(t, laid):
    return call(
        filter_kernel,
        (laid, t["one"], t["two"], t["two_zero"]),
        jax.ShapeDtypeStruct((2 * OUTER, INNER, LANES), F32),
        [pltpu.VMEM((2 * OUTER, INNER, LANES), BF16)],
        4 << 30, 24 << 20,
    )


def main_path(t, moved, kernel_spec, gains):
    return call(
        main_kernel,
        (moved, kernel_spec, gains, t["one"], t["two"], t["two_zero"], t["three"],
         t["three_zero"], t["last"]),
        (MOVED, HELD),
        [pltpu.VMEM((2 * OUTER, INNER, PAIR), F32)],
        6 << 30, 40 << 20,
    )


def filter_gradient(t, spec):
    return call(
        filter_grad_kernel,
        (spec, t["two"], t["member"], t["three"], t["three_zero"], t["turn_cos"], t["turn_sin"],
         t["grad"]),
        jax.ShapeDtypeStruct((PAIR, LANES), F32),
        [pltpu.VMEM((2, PAIR, LANES), F32)],
        2 << 30, 16 << 20,
    )


def lay_filters(filters):
    groups = filters.shape[0]
    member = np.repeat(np.eye(groups), LANES // groups, axis=1)
    return jnp.einsum(
        "gt,gc->tc", filters, jnp.asarray(member, BF16), preferred_element_type=F32
    ).astype(BF16).reshape(OUTER, INNER, LANES)


def exchange(blocks):
    return lax.all_to_all(blocks, "ctx", split_axis=0, concat_axis=0, tiled=True)


def sum_over_sequences(parts):
    count = lax.axis_size("dp")
    place = lax.axis_index("dp")

    def share(owner):
        return lax.dynamic_index_in_dim(parts, owner, 0, keepdims=False)

    total = share(place)
    for hop in range(1, count):
        total = total + lax.ppermute(
            share((place + hop) % count), "dp", [(i, (i + hop) % count) for i in range(count)]
        )
    return total


def unit(moved_input, moved_grad, filters, gains):
    t = build_tables(1.0 / (8192 * 512))
    moved = jnp.stack([moved_input, moved_grad], 1)
    out, spec = main_path(t, moved, filter_spectrum(t, lay_filters(filters)), gains)
    return out[:, 0], out[:, 1], filter_gradient(t, spec)


def on_device(gate_values, conv_input, cotangent, filters, direct_scale):
    replica_count = lax.axis_size("dp")
    grad_scale = 1.0 / (POINTS * math.sqrt(GROUP_WIDTH * replica_count * POINTS // 2))
    t = build_tables(grad_scale)
    moved = exchange(gather(gate_values[0], conv_input[0], cotangent[0]))
    kernel_spec = filter_spectrum(t, lay_filters(filters))
    out, spec = main_path(t, moved, kernel_spec, direct_scale[None, :])
    back = exchange(out)
    filter_part = filter_gradient(t, spec)
    filter_grad = sum_over_sequences(filter_part.reshape(replica_count, -1, LANES))
    filter_grad = filter_grad.reshape(filters.shape[0], -1)
    gate_grad, input_grad = spread(back, cotangent[0])
    return gate_grad[None], input_grad[None], filter_grad


def solution(mesh):
    placed = (
        P("dp", "ctx", None),
        P("dp", "ctx", None),
        P("dp", "ctx", None),
        P("ctx", None),
        P("ctx"),
    )
    return jax.shard_map(
        on_device,
        mesh=mesh,
        in_specs=placed,
        out_specs=(P("dp", "ctx", None), P("dp", "ctx", None), P("ctx", "dp")),
        check_vma=False,
    )
```

time: 164 us -> 103 us (0.63)
  blocking collectives: 19.9 us -> 0 us
  waiting for transfers between devices: 48.7 us -> 32.4 us
  between operations: 14.3 us -> 0.87 us
  Pallas kernels: 37.9 us -> 27.8 us
  other arithmetic: 4.9 us -> 0.01 us
  local copies, waits for them, and re-layouts: 18.4 us -> 22.5 us
    reduce_scatter x1 -> x0, waiting for transfers between devices: 29.2 us -> none  [on_device(): lax.psum_scatter(filter_part.reshape(replica_count, -1, LANES), 'dp', sca...]
    all_to_all x1 -> x0, blocking collectives: 19.9 us -> none  [exchange(): lax.all_to_all(blocks, 'ctx', split_axis=0, concat_axis=0, tiled=True)]
    unnamed x39 -> x46, local copies, waits for them, and re-layouts: 9.86 us -> 21.2 us
    pallas_call x3 -> x5, Pallas kernels: 37.9 us -> 27.8 us  [the longest x3 21.3 us: call(): pl.pallas_call(kernel, out_shape=outs, in_specs=[space] * len(operands),...]
    ppermute x0 -> x3, waiting for transfers between devices: none -> 8.7 us  [sum_over_sequences(): lax.ppermute(share((place + hop) % count), 'dp', [(i, (i + hop) % count)...]
    convert_element_type x2 -> x0, other arithmetic: 4.9 us -> none  [the longest x1 3.27 us: on_device(): gated = (cotangent[0].astype(F32) * gate_values[0].astype(F32)).astype(BF16)]
    all_to_all x3 -> x2, waiting for transfers between devices: 18.9 us -> 23.7 us  [exchange(): lax.all_to_all(blocks, 'ctx', split_axis=0, concat_axis=0, tiled=True)]
    convert_element_type x3 -> x1, local copies, waits for them, and re-layouts: 5.23 us -> 0.66 us  [lay_filters(): return jnp.einsum('gt,gc->tc', filters, jnp.asarray(member, BF16), prefer...]
  transfers between devices with their start and end apart: 4 -> 5, of which waited for: 3 -> 5; matrix products, arithmetic and copies ran while one was open for 6% -> 2% of each run, Pallas kernels for 3% -> 7%
where the time goes in v1:
time: 103 us; the launch traced here: 101 us
  waiting for transfers between devices  32.4 us (31%)
  Pallas kernels  27.8 us (27%)
  local copies, waits for them, and re-layouts  22.5 us (22%)
  starting transfers between devices  17.5 us (17%)
    all_to_all x2, waiting for transfers between devices, exchange(): lax.all_to_all(blocks, 'ctx', split_axis=0, concat_axis=0, tiled=True)  23.7 us
    pallas_call x3, Pallas kernels, call(): pl.pallas_call(kernel, out_shape=outs, in_specs=[space] * len(operands),...  21.3 us
    unnamed x46, local copies, waits for them, and re-layouts  21.2 us
    all_to_all x2, starting transfers between devices, exchange(): lax.all_to_all(blocks, 'ctx', split_axis=0, concat_axis=0, tiled=True)  14.3 us
    ppermute x3, waiting for transfers between devices, sum_over_sequences(): lax.ppermute(share((place + hop) % count), 'dp', [(i, (i + hop) % count)...  8.7 us
    pallas_call x1, Pallas kernels, gather(): pl.pallas_call(gather_kernel, grid=(STEPS,), out_shape=MOVED, in_specs=[R...  3.32 us
    ppermute x3, starting transfers between devices, sum_over_sequences(): lax.ppermute(share((place + hop) % count), 'dp', [(i, (i + hop) % count)...  3.21 us
    pallas_call x1, Pallas kernels, spread(): pl.pallas_call(spread_kernel, grid=(STEPS,), out_shape=(ROWS, ROWS), in_s...  3.1 us
  transfers between devices with their start and end apart: 5, of which 5 were waited for; matrix products, arithmetic and copies ran while one was open for 2% of the time, Pallas kernels for 7%

profile of v1, /device:TPU:0, one launch (start us, length us, event | category | flops | bytes accessed | tf_op | source)
XLA Modules:
  0.0 101.5 jit_solution(12320358875844724101)
XLA Ops:
  0.6 0.0 copy-start
  0.6 0.0 copy-start.1
  0.7 1.2 %copy-done.1 = bf16[1,128,4096]{2,1,0:T(8,128)(2,1)S(1)} copy-done((bf16[1,128,4096]{2,1,0:T(8,128)(2,1)S(1)}, bf16[1,128,4096]{2,1,0:T(8,128)(2,1)}, u32[]{:S(2)}) %copy-start.1) | copy-done | bytes 1048600
  1.9 0.0 copy-start.4
  1.9 1.2 %copy-done.4 = bf16[1,128,4096]{2,1,0:T(8,128)(2,1)S(1)} copy-done((bf16[1,128,4096]{2,1,0:T(8,128)(2,1)S(1)}, bf16[1,128,4096]{2,1,0:T(8,128)(2,1)}, u32[]{:S(2)}) %copy-start.4) | copy-done | bytes 1048600
  3.1 0.0 copy-start.5
  3.1 1.2 %copy-done.5 = bf16[1,128,4096]{2,1,0:T(8,128)(2,1)S(1)} copy-done((bf16[1,128,4096]{2,1,0:T(8,128)(2,1)S(1)}, bf16[1,128,4096]{2,1,0:T(8,128)(2,1)}, u32[]{:S(2)}) %copy-start.5) | copy-done | bytes 1048600
  4.4 3.3 %shard_map.175 = bf16[32,2,128,128]{3,2,1,0:T(8,128)(2,1)} custom-call(bf16[128,4096]{1,0:T(8,128)(2,1)S(1)} %bitcast.26, bf16[128,4096]{1,0:T(8,128)(2,1)S(1)} %bitcast.27, bf16[128,4096]{1,0:T(8,128)(2,1)S(1)} %bitcast.24), custom_call_target="tpu_custom_call" | custom-call | tf_op jit(solution)/shard_map/pallas_call | solution.py:260
  7.7 0.0 copy-start.22
  7.7 9.5 %all-to-all-start = ((bf16[32,2,128,128]{3,2,1,0:T(8,128)(2,1)}), bf16[32,2,128,128]{3,2,1,0:T(8,128)(2,1)}, u32[]{:S(2)}, u32[]{:S(2)}) async-start(bf16[32,2,128,128]{3,2,1,0:T(8,128)(2,1)} %shard_map.175), calls=%async_computation | async-start | bytes 4194304 | tf_op jit(solution)/shard_map/all_to_all | solution.py:335
  17.2 0.0 copy-done
  17.2 0.0 copy-done.22
  17.2 0.0 copy-start.10
  17.2 0.0 copy-start.17
  17.2 0.5 fusion
  17.7 0.7 copy.19
  18.4 0.0 copy-done.10
  18.4 0.0 copy-done.17
  18.4 0.0 copy-start.7
  18.4 2.2 %copy-done.7 = bf16[16,512,256]{2,1,0:T(8,128)(2,1)S(1)} copy-done((bf16[16,512,256]{2,1,0:T(8,128)(2,1)S(1)}, bf16[16,512,256]{2,1,0:T(8,128)(2,1)}, u32[]{:S(2)}) %copy-start.7) | copy-done | bytes 4194328
  20.6 0.0 copy-start.6
  20.6 0.0 copy-start.11
  20.6 0.0 copy-start.13
  20.6 4.3 %shard_map.176.h_ref = f32[64,128,128]{2,1,0:T(8,128)S(1)} custom-call(bf16[32,128,128]{2,1,0:T(8,128)(2,1)S(1)} %bitcast.28, bf16[16,512,256]{2,1,0:T(8,128)(2,1)S(1)} %copy-done.7, bf16[256,256]{1,0:T(8,128)(2,1)S(1)} %copy-done.10, bf16[256,256]{1,0:T(8,128)(2,1)S(1)} %copy-done.17), custom_call_target="tpu_custom_call" | custom-call | flops 4294967296 | bytes 16777216 | tf_op jit(solution)/shard_map/pallas_call | solution.py:283
  24.9 0.0 copy-start.20
  24.9 2.0 %copy-done.20 = f32[64,128,128]{2,1,0:T(8,128)} copy-done((f32[64,128,128]{2,1,0:T(8,128)}, f32[64,128,128]{2,1,0:T(8,128)S(1)}, u32[]{:S(2)}) %copy-start.20) | copy-done | bytes 4194328
  26.8 18.8 %all-to-all-done.v_ref = bf16[32,2,128,128]{3,2,1,0:T(8,128)(2,1)} async-done(((bf16[32,2,128,128]{3,2,1,0:T(8,128)(2,1)}), bf16[32,2,128,128]{3,2,1,0:T(8,128)(2,1)}, u32[]{:S(2)}, u32[]{:S(2)}) %all-to-all-start) | async-done | bytes 2097184 | tf_op jit(solution)/shard_map/all_to_all | solution.py:335
  45.6 0.0 copy-done.6
  45.6 0.0 copy-done.11
  45.6 0.0 copy-done.13
  45.6 0.0 copy-start.21
  45.6 2.2 %copy-done.21 = f32[64,128,128]{2,1,0:T(8,128)S(1)} copy-done((f32[64,128,128]{2,1,0:T(8,128)S(1)}, f32[64,128,128]{2,1,0:T(8,128)}, u32[]{:S(2)}) %copy-start.21) | copy-done | bytes 4194328
  47.8 13.8 %shard_map.177 = (bf16[32,2,128,128]{3,2,1,0:T(8,128)(2,1)S(1)}, bf16[64,128,256]{2,1,0:T(8,128)(2,1)S(1)}) custom-call(bf16[32,2,128,128]{3,2,1,0:T(8,128)(2,1)} %all-to-all-done.v_ref, f32[64,128,128]{2,1,0:T(8,128)S(1)} %copy-done.21, f32[1,128]{1,0:T(1,128)S(1)} %bitcast.31, bf16[16,512,256]{2,1,0:T(8,128)(2,1)} %constant.64.clone.one_ref, ...), custom_call_target="tpu_custom_call" | custom-call | flops 6442450944 | bytes 16777216 | tf_op jit(solution)/shard_map/pallas_call | solution.py:283
  61.6 0.0 copy-start.3
  61.7 1.4 %copy-done.3 = bf16[32,2,128,128]{3,2,1,0:T(8,128)(2,1)} copy-done((bf16[32,2,128,128]{3,2,1,0:T(8,128)(2,1)}, bf16[32,2,128,128]{3,2,1,0:T(8,128)(2,1)S(1)}, u32[]{:S(2)}) %copy-start.3) | copy-done | bytes 2097176
  63.0 0.0 copy-start.18
  63.0 2.0 %copy-done.18 = bf16[64,128,256]{2,1,0:T(8,128)(2,1)} copy-done((bf16[64,128,256]{2,1,0:T(8,128)(2,1)}, bf16[64,128,256]{2,1,0:T(8,128)(2,1)S(1)}, u32[]{:S(2)}) %copy-start.18) | copy-done | bytes 4194328
  65.0 4.8 %all-to-all-start.1 = ((bf16[32,2,128,128]{3,2,1,0:T(8,128)(2,1)}), bf16[32,2,128,128]{3,2,1,0:T(8,128)(2,1)S(1)}, u32[]{:S(2)}, u32[]{:S(2)}) async-start(bf16[32,2,128,128]{3,2,1,0:T(8,128)(2,1)} %copy-done.3), calls=%async_computation.1 | async-start | bytes 4194304 | tf_op jit(solution)/shard_map/all_to_all | solution.py:335
  69.8 0.0 copy-start.8
  69.8 1.0 %copy-done.8 = bf16[8,256,128]{2,1,0:T(8,128)(2,1)S(1)} copy-done((bf16[8,256,128]{2,1,0:T(8,128)(2,1)S(1)}, bf16[8,256,128]{2,1,0:T(8,128)(2,1)}, u32[]{:S(2)}) %copy-start.8) | copy-done | bytes 524312
  70.8 0.0 copy-start.9
  70.8 0.9 copy-done.9
  71.8 0.0 copy-start.12
  71.8 0.9 copy-done.12
  72.7 0.0 copy-start.14
  72.7 0.9 copy-done.14
  73.6 0.0 copy-start.15
  73.6 0.9 copy-done.15
  74.5 0.0 copy-start.16
  74.5 0.9 copy-done.16
  75.4 0.0 copy-start.19
  75.4 2.2 %copy-done.19 = bf16[64,128,256]{2,1,0:T(8,128)(2,1)S(1)} copy-done((bf16[64,128,256]{2,1,0:T(8,128)(2,1)S(1)}, bf16[64,128,256]{2,1,0:T(8,128)(2,1)}, u32[]{:S(2)}) %copy-start.19) | copy-done | bytes 4194328
  77.6 0.0 copy-start.2
  77.6 3.2 %shard_map.179 = f32[256,128]{1,0:T(8,128)S(1)} custom-call(bf16[64,128,256]{2,1,0:T(8,128)(2,1)S(1)} %copy-done.19, bf16[256,256]{1,0:T(8,128)(2,1)S(1)} %copy-done.10, bf16[8,256,128]{2,1,0:T(8,128)(2,1)S(1)} %copy-done.8, bf16[256,256]{1,0:T(8,128)(2,1)S(1)} %copy-done.12, bf16[256,256]{1,0:T(8,128)(2,1)S(1)} %copy-done.14, f32[128,256]{1,0:T(8,128)S(1)} %copy-done.15, ...), custom_call_target="tpu_custom_call" | custom-call | flops 2147483648 | bytes 16777216 | tf_op jit(solution)/shard_map/pallas_call | solution.py:283
  80.9 2.3 %collective-permute-start.2 = (f32[64,128]{1,0:T(8,128)S(1)}, f32[64,128]{1,0:T(8,128)S(1)}, u32[]{:S(2)}, u32[]{:S(2)}) collective-permute-start(f32[64,128]{1,0:T(8,128)S(1)} %get-tuple-element.12), channel_id=1, source_target_pairs={{0,96},{32,0},{64,32},{96,64},{1,97},{33,1},{65,33},{97,65},{2,98}... | collective-permute-start | bytes 98312 | tf_op jit(solution)/shard_map/ppermute | solution.py:347
  83.2 0.7 collective-permute-start.1
  83.9 0.2 collective-permute-start
  84.1 0.7 collective-permute-done.2
  84.8 6.3 %collective-permute-done.1 = f32[64,128]{1,0:T(8,128)S(1)} collective-permute-done((f32[64,128]{1,0:T(8,128)S(1)}, f32[64,128]{1,0:T(8,128)S(1)}, u32[]{:S(2)}, u32[]{:S(2)}) %collective-permute-start.1) | collective-permute-done | bytes 32800 | tf_op jit(solution)/shard_map/ppermute | solution.py:347
  91.1 1.7 %collective-permute-done = f32[64,128]{1,0:T(8,128)S(1)} collective-permute-done((f32[64,128]{1,0:T(8,128)S(1)}, f32[64,128]{1,0:T(8,128)S(1)}, u32[]{:S(2)}, u32[]{:S(2)}) %collective-permute-start) | collective-permute-done | bytes 32800 | tf_op jit(solution)/shard_map/ppermute | solution.py:347
  92.8 0.6 reshape.17
  93.4 4.9 %all-to-all-done.1.back_ref = bf16[32,2,128,128]{3,2,1,0:T(8,128)(2,1)S(1)} async-done(((bf16[32,2,128,128]{3,2,1,0:T(8,128)(2,1)}), bf16[32,2,128,128]{3,2,1,0:T(8,128)(2,1)S(1)}, u32[]{:S(2)}, u32[]{:S(2)}) %all-to-all-start.1) | async-done | bytes 2097184 | tf_op jit(solution)/shard_map/all_to_all | solution.py:335
  98.4 0.0 copy-done.2
  98.4 3.1 %shard_map.178 = (bf16[128,4096]{1,0:T(8,128)(2,1)}, bf16[128,4096]{1,0:T(8,128)(2,1)}) custom-call(bf16[32,2,128,128]{3,2,1,0:T(8,128)(2,1)S(1)} %all-to-all-done.1.back_ref, bf16[128,4096]{1,0:T(8,128)(2,1)S(1)} %bitcast.25), custom_call_target="tpu_custom_call" | custom-call | tf_op jit(solution)/shard_map/pallas_call | solution.py:271
  (2 shorter events, 0.0 us)
Async XLA Ops:
  0.6 16.6 %copy-start = (bf16[8,4096]{1,0:T(8,128)(2,1)S(1)}, bf16[8,4096]{1,0:T(8,128)(2,1)}, u32[]{:S(2)}) copy-start(bf16[8,4096]{1,0:T(8,128)(2,1)} %param.19) | copy-start | bytes 196612
  0.6 1.3 %copy-start.1 = (bf16[1,128,4096]{2,1,0:T(8,128)(2,1)S(1)}, bf16[1,128,4096]{2,1,0:T(8,128)(2,1)}, u32[]{:S(2)}) copy-start(bf16[1,128,4096]{2,1,0:T(8,128)(2,1)} %param.18) | copy-start | bytes 3145732
  1.9 1.2 %copy-start.4 = (bf16[1,128,4096]{2,1,0:T(8,128)(2,1)S(1)}, bf16[1,128,4096]{2,1,0:T(8,128)(2,1)}, u32[]{:S(2)}) copy-start(bf16[1,128,4096]{2,1,0:T(8,128)(2,1)} %param.16) | copy-start | bytes 3145732
  3.1 1.2 %copy-start.5 = (bf16[1,128,4096]{2,1,0:T(8,128)(2,1)S(1)}, bf16[1,128,4096]{2,1,0:T(8,128)(2,1)}, u32[]{:S(2)}) copy-start(bf16[1,128,4096]{2,1,0:T(8,128)(2,1)} %param.17) | copy-start | bytes 3145732
  7.7 9.5 %copy-start.22 = (bf16[8,128]{1,0:T(8,128)(2,1)S(1)}, bf16[8,128]{1,0:T(8,128)(2,1)}, u32[]{:S(2)}) copy-start(bf16[8,128]{1,0:T(8,128)(2,1)} %constant.74.clone) | copy-start | bytes 6148
  7.7 37.9 %all-to-all-start = ((bf16[32,2,128,128]{3,2,1,0:T(8,128)(2,1)}), bf16[32,2,128,128]{3,2,1,0:T(8,128)(2,1)}, u32[]{:S(2)}, u32[]{:S(2)}) async-start(bf16[32,2,128,128]{3,2,1,0:T(8,128)(2,1)} %shard_map.175), calls=%async_computation | async-start | bytes 4194304 | tf_op jit(solution)/shard_map/all_to_all | solution.py:335
  17.2 1.2 %copy-start.10 = (bf16[256,256]{1,0:T(8,128)(2,1)S(1)}, bf16[256,256]{1,0:T(8,128)(2,1)}, u32[]{:S(2)}) copy-start(bf16[256,256]{1,0:T(8,128)(2,1)} %constant.66.clone.two_ref) | copy-start | bytes 393220
  17.2 1.2 %copy-start.17 = (bf16[256,256]{1,0:T(8,128)(2,1)S(1)}, bf16[256,256]{1,0:T(8,128)(2,1)}, u32[]{:S(2)}) copy-start(bf16[256,256]{1,0:T(8,128)(2,1)} %constant.67.clone.two_zero_ref) | copy-start | bytes 393220
  18.4 2.2 %copy-start.7 = (bf16[16,512,256]{2,1,0:T(8,128)(2,1)S(1)}, bf16[16,512,256]{2,1,0:T(8,128)(2,1)}, u32[]{:S(2)}) copy-start(bf16[16,512,256]{2,1,0:T(8,128)(2,1)} %constant.64.clone.one_ref) | copy-start | bytes 12582916
  20.6 25.0 %copy-start.6 = (f32[128]{0:T(128)S(1)}, f32[128]{0:T(128)}, u32[]{:S(2)}) copy-start(f32[128]{0:T(128)} %param.20) | copy-start | bytes 1540
  20.6 25.0 %copy-start.11 = (bf16[256,256]{1,0:T(8,128)(2,1)S(1)}, bf16[256,256]{1,0:T(8,128)(2,1)}, u32[]{:S(2)}) copy-start(bf16[256,256]{1,0:T(8,128)(2,1)} %constant.68.clone.three_ref) | copy-start | bytes 393220
  20.6 25.0 %copy-start.13 = (bf16[256,256]{1,0:T(8,128)(2,1)S(1)}, bf16[256,256]{1,0:T(8,128)(2,1)}, u32[]{:S(2)}) copy-start(bf16[256,256]{1,0:T(8,128)(2,1)} %constant.69.clone.three_zero_ref) | copy-start | bytes 393220
  24.9 2.0 %copy-start.20 = (f32[64,128,128]{2,1,0:T(8,128)}, f32[64,128,128]{2,1,0:T(8,128)S(1)}, u32[]{:S(2)}) copy-start(f32[64,128,128]{2,1,0:T(8,128)S(1)} %shard_map.176.h_ref) | copy-start | bytes 12582916
  45.6 2.2 %copy-start.21 = (f32[64,128,128]{2,1,0:T(8,128)S(1)}, f32[64,128,128]{2,1,0:T(8,128)}, u32[]{:S(2)}) copy-start(f32[64,128,128]{2,1,0:T(8,128)} %copy-done.20) | copy-start | bytes 12582916
  61.6 1.4 %copy-start.3 = (bf16[32,2,128,128]{3,2,1,0:T(8,128)(2,1)}, bf16[32,2,128,128]{3,2,1,0:T(8,128)(2,1)S(1)}, u32[]{:S(2)}) copy-start(bf16[32,2,128,128]{3,2,1,0:T(8,128)(2,1)S(1)} %get-tuple-element.7) | copy-start | bytes 6291460
  63.0 2.0 %copy-start.18 = (bf16[64,128,256]{2,1,0:T(8,128)(2,1)}, bf16[64,128,256]{2,1,0:T(8,128)(2,1)S(1)}, u32[]{:S(2)}) copy-start(bf16[64,128,256]{2,1,0:T(8,128)(2,1)S(1)} %get-tuple-element.10.spec_ref) | copy-start | bytes 12582916
  65.0 33.4 %all-to-all-start.1 = ((bf16[32,2,128,128]{3,2,1,0:T(8,128)(2,1)}), bf16[32,2,128,128]{3,2,1,0:T(8,128)(2,1)S(1)}, u32[]{:S(2)}, u32[]{:S(2)}) async-start(bf16[32,2,128,128]{3,2,1,0:T(8,128)(2,1)} %copy-done.3), calls=%async_computation.1 | async-start | bytes 4194304 | tf_op jit(solution)/shard_map/all_to_all | solution.py:335
  69.8 1.0 %copy-start.8 = (bf16[8,256,128]{2,1,0:T(8,128)(2,1)S(1)}, bf16[8,256,128]{2,1,0:T(8,128)(2,1)}, u32[]{:S(2)}) copy-start(bf16[8,256,128]{2,1,0:T(8,128)(2,1)} %constant.70.clone.member_ref) | copy-start | bytes 1572868
  70.8 0.9 copy-start.9
  71.8 0.9 copy-start.12
  72.7 0.9 copy-start.14
  73.6 0.9 copy-start.15
  74.5 0.9 copy-start.16
  75.4 2.2 %copy-start.19 = (bf16[64,128,256]{2,1,0:T(8,128)(2,1)S(1)}, bf16[64,128,256]{2,1,0:T(8,128)(2,1)}, u32[]{:S(2)}) copy-start(bf16[64,128,256]{2,1,0:T(8,128)(2,1)} %copy-done.18) | copy-start | bytes 12582916
  77.6 20.8 %copy-start.2 = (bf16[1,128,4096]{2,1,0:T(8,128)(2,1)S(1)}, bf16[1,128,4096]{2,1,0:T(8,128)(2,1)}, u32[]{:S(2)}) copy-start(bf16[1,128,4096]{2,1,0:T(8,128)(2,1)} %param.18) | copy-start | bytes 3145732
  80.9 3.9 %collective-permute-start.2 = (f32[64,128]{1,0:T(8,128)S(1)}, f32[64,128]{1,0:T(8,128)S(1)}, u32[]{:S(2)}, u32[]{:S(2)}) collective-permute-start(f32[64,128]{1,0:T(8,128)S(1)} %get-tuple-element.12), channel_id=1, source_target_pairs={{0,96},{32,0},{64,32},{96,64},{1,97},{33,1},{65,33},{97,65},{2,98}... | collective-permute-start | bytes 98312 | tf_op jit(solution)/shard_map/ppermute | solution.py:347
  83.2 7.9 %collective-permute-start.1 = (f32[64,128]{1,0:T(8,128)S(1)}, f32[64,128]{1,0:T(8,128)S(1)}, u32[]{:S(2)}, u32[]{:S(2)}) collective-permute-start(f32[64,128]{1,0:T(8,128)S(1)} %get-tuple-element.13), channel_id=1, source_target_pairs={{0,64},{32,96},{64,0},{96,32},{1,65},{33,97},{65,1},{97,33},{2,66}... | collective-permute-start | bytes 98312 | tf_op jit(solution)/shard_map/ppermute | solution.py:347
  83.9 8.9 %collective-permute-start = (f32[64,128]{1,0:T(8,128)S(1)}, f32[64,128]{1,0:T(8,128)S(1)}, u32[]{:S(2)}, u32[]{:S(2)}) collective-permute-start(f32[64,128]{1,0:T(8,128)S(1)} %get-tuple-element.11), channel_id=1, source_target_pairs={{0,32},{32,64},{64,96},{96,0},{1,33},{33,65},{65,97},{97,1},{2,34}... | collective-permute-start | bytes 98312 | tf_op jit(solution)/shard_map/ppermute | solution.py:347

commit v2 on v1

--- a/solution.py
+++ b/solution.py
@@ -51,8 +51,11 @@
     weight = np.ones((256, 1))
     weight[0] = 0.5
     weight[128] = 0.5
-    table_three = table_two.T
-    table_three_zero = (table_two_zero * weight).T
+    mixed_rows = np.arange(256).reshape(2, 16, 8).transpose(1, 0, 2).reshape(256)
+    table_three = table_two.T[:, mixed_rows]
+    table_three_zero = (table_two_zero * weight).T[:, mixed_rows]
+    table_two = table_two[mixed_rows]
+    table_two_zero = table_two_zero[mixed_rows]
 
     member = np.zeros((8, 256, LANES))
     for pair in range(8):
@@ -81,10 +84,7 @@
     return dict(
         one=low(table_one),
         last=low(table_last),
-        two=low(table_two),
-        two_zero=low(table_two_zero),
-        three=low(table_three),
-        three_zero=low(table_three_zero),
+        inner=low(np.stack([table_two, table_two_zero, table_three, table_three_zero])),
         member=low(member),
         turn_cos=wide(turn_cos),
         turn_sin=wide(turn_sin),
@@ -96,23 +96,25 @@
     return jnp.dot(left, right, preferred_element_type=F32)
 
 
-def outer_stage(load, one_ref, u_ref):
-    @pl.loop(0, 8)
-    def _(p):
-        row = pl.multiple_of(p * 16, 16)
-        given = load(row)
-        lanes = given.shape[2]
-        out = []
-        for h in range(2):
-            held = given[:, 8 * h : 8 * h + 8].reshape(256, lanes).astype(BF16)
-            out.append(dot(one_ref[2 * p + h], held).reshape(64, 8, lanes))
-        u_ref[:, pl.ds(row, 16), :] = jnp.concatenate(out, 1).astype(BF16)
-
-
-def slab_matrix(u_ref, start, count):
-    real = [u_ref[start + k] for k in range(count)]
-    imag = [u_ref[OUTER + start + k] for k in range(count)]
-    return jnp.concatenate([jnp.concatenate(real, 1), jnp.concatenate(imag, 1)], 0)
+def outer_block(given, one_ref, p, u_ref):
+    lanes = given.shape[2]
+    out = []
+    for h in range(2):
+        held = given[:, 8 * h : 8 * h + 8].reshape(256, lanes).astype(BF16)
+        out.append(dot(one_ref[2 * p + h], held).reshape(64, 8, lanes))
+    both = jnp.concatenate(out, 1).astype(BF16)
+    row = pl.multiple_of(p * 16, 16)
+    u_ref[:, pl.ds(row, 16), :] = both[:OUTER]
+    u_ref[:, pl.ds(INNER + row, 16), :] = both[OUTER:]
+
+
+def apart(values):
+    values = values.reshape(16, 2, 8, values.shape[1])
+    return values[:, 0], values[:, 1]
+
+
+def together(real, imag):
+    return jnp.stack([real, imag], 1).reshape(256, real.shape[2])
 
 
 def times(ar, ai, br, bi, conjugate, packed):
@@ -122,12 +124,17 @@
     else:
         real, imag = ar * br - cross, ar * bi + ai * br
     if packed:
-        edge = lax.broadcasted_iota(jnp.int32, ar.shape, 0) == 0
+        place = lax.broadcasted_iota(jnp.int32, ar.shape, 0) * 8
+        edge = place + lax.broadcasted_iota(jnp.int32, ar.shape, 1) == 0
         real = jnp.where(edge, ar * br, real)
         imag = jnp.where(edge, cross, imag)
     return real, imag
 
 
+def lane_cut(values, k, width):
+    return values[:, width * k : width * k + width]
+
+
 def slabs(body, count):
     body(0, 1, True)
     body(1, count - 1, False)
@@ -137,59 +144,112 @@
         body(count * m, count, False)
 
 
-def filter_kernel(v_ref, one_ref, two_ref, two_zero_ref, spec_ref, u_ref):
-    outer_stage(lambda row: v_ref[:, pl.ds(row, 16), :].astype(F32), one_ref, u_ref)
-
-    def body(start, count, packed):
-        spec = dot((two_zero_ref if packed else two_ref)[...], slab_matrix(u_ref, start, count))
-        for k in range(count):
-            spec_ref[start + k] = spec[:INNER, LANES * k : LANES * k + LANES]
-            spec_ref[OUTER + start + k] = spec[INNER:, LANES * k : LANES * k + LANES]
-
-    slabs(body, 4)
-
-
-def main_kernel(
-    v_ref, h_ref, gain_ref, one_ref, two_ref, two_zero_ref, three_ref, three_zero_ref, last_ref,
-    out_ref, u_ref, back_ref,
-):
-    def load(row):
-        both = v_ref[:, :, pl.ds(row, 16), :].astype(F32)
-        return jnp.concatenate([both[:, 0], both[:, 1]], 2)
-
-    outer_stage(load, one_ref, u_ref)
-
-    def body(start, count, packed):
-        spec = dot((two_zero_ref if packed else two_ref)[...], slab_matrix(u_ref, start, count))
-        top, bottom = [], []
-        for k in range(count):
-            real = spec[:INNER, PAIR * k : PAIR * k + PAIR]
-            imag = spec[INNER:, PAIR * k : PAIR * k + PAIR]
-            hr, hi = h_ref[start + k], h_ref[OUTER + start + k]
-            pr, pi = times(hr, hi, real[:, :LANES], imag[:, :LANES], False, packed)
-            ar, ai = times(hr, hi, real[:, LANES:], imag[:, LANES:], True, packed)
-            top += [pr, ar]
-            bottom += [pi, ai]
-        product = jnp.concatenate(
-            [jnp.concatenate(top, 1), jnp.concatenate(bottom, 1)], 0
-        ).astype(BF16)
-        back = dot((three_zero_ref if packed else three_ref)[...], product)
-        for k in range(count):
-            u_ref[start + k] = spec[:INNER, PAIR * k : PAIR * k + PAIR].astype(BF16)
-            u_ref[OUTER + start + k] = spec[INNER:, PAIR * k : PAIR * k + PAIR].astype(BF16)
-            back_ref[start + k] = back[:INNER, PAIR * k : PAIR * k + PAIR]
-            back_ref[OUTER + start + k] = back[INNER:, PAIR * k : PAIR * k + PAIR]
-
-    slabs(body, 4)
-
+def filter_kernel(v_ref, one_ref, inner_ref, spec_ref, u_ref):
     @pl.loop(0, 8)
     def _(p):
+        row = pl.multiple_of(p * 16, 16)
+        outer_block(v_ref[:, pl.ds(row, 16), :].astype(F32), one_ref, p, u_ref)
+
+    def body(start, count, packed):
+        held = jnp.concatenate([u_ref[start + k] for k in range(count)], 1)
+        spec = dot(inner_ref[int(packed)], held)
+        for k in range(count):
+            spec_ref[start + k] = lane_cut(spec, k, LANES)
+
+    slabs(body, 4)
+
+
+def main_kernel(
+    v_hbm, h_hbm, gain_hbm, one_hbm, inner_hbm, last_hbm, out_hbm, spec_hbm,
+    v_ref, h_ref, gain_ref, one_ref, inner_ref, last_ref, out_ref, u_ref, back_ref,
+    v_sem, h_sem, gain_sem, one_sem, inner_sem, last_sem, out_sem, spec_sem,
+):
+    def v_copy(p):
+        cut = pl.ds(pl.multiple_of(p * 16, 16), 16)
+        return pltpu.make_async_copy(v_hbm.at[:, :, cut], v_ref.at[:, :, cut], v_sem.at[p])
+
+    def out_copy(p):
+        cut = pl.ds(pl.multiple_of(p * 16, 16), 16)
+        return pltpu.make_async_copy(out_ref.at[:, :, cut], out_hbm.at[:, :, cut], out_sem.at[p])
+
+    def table_copy(hbm, ref, sem, p):
+        cut = pl.ds(2 * p, 2)
+        return pltpu.make_async_copy(hbm.at[cut], ref.at[cut], sem.at[p])
+
+    def slab_copy(source, target, sem, m):
+        cut = pl.ds(4 * m, 4)
+        return pltpu.make_async_copy(source.at[cut], target.at[cut], sem.at[m])
+
+    inner_copy = pltpu.make_async_copy(inner_hbm, inner_ref, inner_sem)
+    gain_copy = pltpu.make_async_copy(gain_hbm, gain_ref, gain_sem)
+
+    @pl.loop(0, 8)
+    def _(p):
+        v_copy(p).start()
+        table_copy(one_hbm, one_ref, one_sem, p).start()
+
+    inner_copy.start()
+    gain_copy.start()
+
+    @pl.loop(0, 8)
+    def _(p):
+        slab_copy(h_hbm, h_ref, h_sem, p).start()
+        table_copy(last_hbm, last_ref, last_sem, p).start()
+        v_copy(p).wait()
+        table_copy(one_hbm, one_ref, one_sem, p).wait()
+        row = pl.multiple_of(p * 16, 16)
+        both = v_ref[:, :, pl.ds(row, 16), :].astype(F32)
+        outer_block(jnp.concatenate([both[:, 0], both[:, 1]], 2), one_ref, p, u_ref)
+
+    inner_copy.wait()
+
+    def body(start, count, packed):
+        held = jnp.concatenate([u_ref[start + k] for k in range(count)], 1)
+        spec = dot(inner_ref[int(packed)], held)
+        real, imag = apart(spec)
+        out_real, out_imag = [], []
+        for k in range(count):
+            hr, hi = apart(h_ref[start + k])
+            low = slice(PAIR * k, PAIR * k + LANES)
+            high = slice(PAIR * k + LANES, PAIR * k + PAIR)
+            pr, pi = times(hr, hi, real[..., low], imag[..., low], False, packed)
+            ar, ai = times(hr, hi, real[..., high], imag[..., high], True, packed)
+            out_real += [pr, ar]
+            out_imag += [pi, ai]
+        product = together(jnp.concatenate(out_real, 2), jnp.concatenate(out_imag, 2))
+        back = dot(inner_ref[2 + int(packed)], product.astype(BF16))
+        for k in range(count):
+            u_ref[start + k] = lane_cut(spec, k, PAIR).astype(BF16)
+            back_ref[start + k] = lane_cut(back, k, PAIR)
+
+    slab_copy(h_hbm, h_ref, h_sem, 0).wait()
+    body(0, 1, True)
+    body(1, 3, False)
+    slab_copy(u_ref, spec_hbm, spec_sem, 0).start()
+
+    @pl.loop(1, 8)
+    def _(m):
+        slab_copy(h_hbm, h_ref, h_sem, m).wait()
+        body(4 * m, 4, False)
+        slab_copy(u_ref, spec_hbm, spec_sem, m).start()
+
+    gain_copy.wait()
+
+    @pl.loop(0, 8)
+    def _(p):
+        table_copy(last_hbm, last_ref, last_sem, p).wait()
         row = pl.multiple_of(p * 16, 16)
         gain = gain_ref[...]
         given = v_ref[:, :, pl.ds(row, 16), :].astype(F32)
         out = [[], []]
         for h in range(2):
-            held = back_ref[:, pl.ds(row + 8 * h, 8), :].reshape(512, PAIR).astype(BF16)
+            held = jnp.concatenate(
+                [
+                    back_ref[:, pl.ds(INNER * part + row + 8 * h, 8), :].reshape(256, PAIR)
+                    for part in range(2)
+                ],
+                0,
+            ).astype(BF16)
             lines = dot(last_ref[2 * p + h], held).reshape(OUTER, 8, PAIR)
             for a in range(2):
                 out[a].append(
@@ -198,22 +258,28 @@
                 )
         for a in range(2):
             out_ref[:, a, pl.ds(row, 16), :] = jnp.concatenate(out[a], 1).astype(BF16)
+        out_copy(p).start()
+
+    @pl.loop(0, 8)
+    def _(p):
+        slab_copy(u_ref, spec_hbm, spec_sem, p).wait()
+        out_copy(p).wait()
 
 
 def filter_grad_kernel(
-    spec_ref, two_ref, member_ref, three_ref, three_zero_ref, turn_cos_ref, turn_sin_ref, grad_ref,
-    filter_ref, sum_ref,
+    spec_ref, inner_ref, member_ref, turn_cos_ref, turn_sin_ref, grad_ref, filter_ref, sum_ref
 ):
     sum_ref[...] = jnp.zeros_like(sum_ref)
 
     def body(start, count, packed):
         for k in range(count):
-            real = spec_ref[start + k].astype(F32)
-            imag = spec_ref[OUTER + start + k].astype(F32)
-            fr, fi = times(
-                real[:, :LANES], imag[:, :LANES], real[:, LANES:], imag[:, LANES:], True, packed
+            real, imag = apart(spec_ref[start + k].astype(F32))
+            both = together(
+                *times(
+                    real[..., :LANES], imag[..., :LANES], real[..., LANES:], imag[..., LANES:],
+                    True, packed,
+                )
             )
-            both = jnp.concatenate([fr, fi], 0)
             high = both.astype(BF16)
             rest = (both - high.astype(F32)).astype(BF16)
             slab = start + k
@@ -222,8 +288,8 @@
 
     slabs(body, 4)
     total = jnp.concatenate([sum_ref[0], sum_ref[1]], 1).astype(BF16)
-    back = dot(three_ref[...], total)
-    back_zero = dot(three_zero_ref[...], total)
+    back = dot(inner_ref[2], total)
+    back_zero = dot(inner_ref[3], total)
     packed = lax.broadcasted_iota(jnp.int32, back.shape, 1) < 8
     back = jnp.where(packed, back_zero, back)
     br, bi = back[:INNER], back[INNER:]
@@ -248,12 +314,12 @@
         input_grad_ref[:, cut] = back_ref[k, 1]
 
 
-STEPS = 8
+STEPS = 4
 ROWS_BLOCK = pl.BlockSpec((INNER, OUTER // STEPS * LANES), lambda i: (0, i))
 MOVED_BLOCK = pl.BlockSpec((OUTER // STEPS, 2, INNER, LANES), lambda i: (i, 0, 0, 0))
 MOVED = jax.ShapeDtypeStruct((OUTER, 2, INNER, LANES), BF16)
 ROWS = jax.ShapeDtypeStruct((INNER, OUTER * LANES), BF16)
-HELD = jax.ShapeDtypeStruct((2 * OUTER, INNER, PAIR), BF16)
+HELD = jax.ShapeDtypeStruct((OUTER, PAIR, PAIR), BF16)
 
 
 def gather(gate, given, cotan):
@@ -263,7 +329,7 @@
         out_shape=MOVED,
         in_specs=[ROWS_BLOCK] * 3,
         out_specs=MOVED_BLOCK,
-        compiler_params=pltpu.CompilerParams(vmem_limit_bytes=8 << 20),
+        compiler_params=pltpu.CompilerParams(vmem_limit_bytes=60 << 20),
     )(gate, given, cotan)
 
 
@@ -274,7 +340,7 @@
         out_shape=(ROWS, ROWS),
         in_specs=[MOVED_BLOCK, ROWS_BLOCK],
         out_specs=(ROWS_BLOCK, ROWS_BLOCK),
-        compiler_params=pltpu.CompilerParams(vmem_limit_bytes=8 << 20),
+        compiler_params=pltpu.CompilerParams(vmem_limit_bytes=60 << 20),
     )(back, cotan)
 
 
@@ -294,29 +360,40 @@
 def filter_spectrum(t, laid):
     return call(
         filter_kernel,
-        (laid, t["one"], t["two"], t["two_zero"]),
-        jax.ShapeDtypeStruct((2 * OUTER, INNER, LANES), F32),
-        [pltpu.VMEM((2 * OUTER, INNER, LANES), BF16)],
+        (laid, t["one"], t["inner"]),
+        jax.ShapeDtypeStruct((OUTER, PAIR, LANES), F32),
+        [pltpu.VMEM((OUTER, PAIR, LANES), BF16)],
         4 << 30, 24 << 20,
     )
 
 
 def main_path(t, moved, kernel_spec, gains):
-    return call(
+    operands = (moved, kernel_spec, gains, t["one"], t["inner"], t["last"])
+    space = pl.BlockSpec(memory_space=pltpu.HBM)
+    sems = pltpu.SemaphoreType.DMA
+    return pl.pallas_call(
         main_kernel,
-        (moved, kernel_spec, gains, t["one"], t["two"], t["two_zero"], t["three"],
-         t["three_zero"], t["last"]),
-        (MOVED, HELD),
-        [pltpu.VMEM((2 * OUTER, INNER, PAIR), F32)],
-        6 << 30, 40 << 20,
-    )
+        out_shape=(MOVED, HELD),
+        in_specs=[space] * len(operands),
+        out_specs=(space, space),
+        scratch_shapes=[pltpu.VMEM(o.shape, o.dtype) for o in operands]
+        + [
+            pltpu.VMEM(MOVED.shape, BF16),
+            pltpu.VMEM(HELD.shape, BF16),
+            pltpu.VMEM(HELD.shape, F32),
+            sems((8,)), sems((8,)), sems, sems((8,)), sems, sems((8,)), sems((8,)), sems((8,)),
+        ],
+        compiler_params=pltpu.CompilerParams(vmem_limit_bytes=48 << 20),
+        cost_estimate=pl.CostEstimate(
+            flops=6 << 30, bytes_accessed=20 << 20, transcendentals=0
+        ),
+    )(*operands)
 
 
 def filter_gradient(t, spec):
     return call(
         filter_grad_kernel,
-        (spec, t["two"], t["member"], t["three"], t["three_zero"], t["turn_cos"], t["turn_sin"],
-         t["grad"]),
+        (spec, t["inner"], t["member"], t["turn_cos"], t["turn_sin"], t["grad"]),
         jax.ShapeDtypeStruct((PAIR, LANES), F32),
         [pltpu.VMEM((2, PAIR, LANES), F32)],
         2 << 30, 16 << 20,

time: 103 us -> 94.3 us (0.916)
  local copies, waits for them, and re-layouts: 22.5 us -> 10.7 us
  waiting for transfers between devices: 32.4 us -> 35.4 us
    pallas_call x3 -> x2, Pallas kernels: 21.3 us -> 7.21 us  [call(): pl.pallas_call(kernel, out_shape=outs, in_specs=[space] * len(operands),...]
    unnamed x46 -> x24, local copies, waits for them, and re-layouts: 21.2 us -> 8.43 us
    pallas_call x0 -> x1, Pallas kernels: none -> 11.6 us  [main_path(): pl.pallas_call(main_kernel, out_shape=(MOVED, HELD), in_specs=[space] * l...]
    ppermute x3, waiting for transfers between devices: 8.7 us -> 12.7 us  [sum_over_sequences(): lax.ppermute(share((place + hop) % count), 'dp', [(i, (i + hop) % count)...]
  transfers between devices with their start and end apart: 5 -> 5, of which waited for: 5 -> 4; matrix products, arithmetic and copies ran while one was open for 2% -> 4% of each run, Pallas kernels for 7% -> 8%
where the time goes in v2:
time: 94.3 us; the launch traced here: 93 us
  waiting for transfers between devices  35.4 us (38%)
  Pallas kernels  27 us (29%)
  starting transfers between devices  17.6 us (19%)
  local copies, waits for them, and re-layouts  10.7 us (11%)
  matrix products  1.44 us (2%)
    all_to_all x2, waiting for transfers between devices, exchange(): lax.all_to_all(blocks, 'ctx', split_axis=0, concat_axis=0, tiled=True)  22.7 us
    all_to_all x2, starting transfers between devices, exchange(): lax.all_to_all(blocks, 'ctx', split_axis=0, concat_axis=0, tiled=True)  14.4 us
    ppermute x3, waiting for transfers between devices, sum_over_sequences(): lax.ppermute(share((place + hop) % count), 'dp', [(i, (i + hop) % count)...  12.7 us
    pallas_call x1, Pallas kernels, main_path(): pl.pallas_call(main_kernel, out_shape=(MOVED, HELD), in_specs=[space] * l...  11.6 us
    unnamed x24, local copies, waits for them, and re-layouts  8.43 us
    pallas_call x2, Pallas kernels, call(): pl.pallas_call(kernel, out_shape=outs, in_specs=[space] * len(operands),...  7.21 us
    pallas_call x1, Pallas kernels, gather(): pl.pallas_call(gather_kernel, grid=(STEPS,), out_shape=MOVED, in_specs=[R...  4.13 us
    pallas_call x1, Pallas kernels, spread(): pl.pallas_call(spread_kernel, grid=(STEPS,), out_shape=(ROWS, ROWS), in_s...  4.04 us
  transfers between devices with their start and end apart: 5, of which 4 were waited for; matrix products, arithmetic and copies ran while one was open for 4% of the time, Pallas kernels for 8%

profile of v2, /device:TPU:0, one launch (start us, length us, event | category | flops | bytes accessed | tf_op | source)
XLA Modules:
  0.0 93.0 jit_solution(2797701936226915495)
XLA Ops:
  0.6 0.0 copy-start
  0.6 4.1 %shard_map.148 = bf16[32,2,128,128]{3,2,1,0:T(8,128)(2,1)} custom-call(bf16[128,4096]{1,0:T(8,128)(2,1)} %bitcast.30, bf16[128,4096]{1,0:T(8,128)(2,1)} %bitcast.31, bf16[128,4096]{1,0:T(8,128)(2,1)} %bitcast.28), custom_call_target="tpu_custom_call" | custom-call | tf_op jit(solution)/shard_map/pallas_call | solution.py:326
  4.8 0.0 copy-start.11
  4.8 9.4 %all-to-all-start = ((bf16[32,2,128,128]{3,2,1,0:T(8,128)(2,1)}), bf16[32,2,128,128]{3,2,1,0:T(8,128)(2,1)S(1)}, u32[]{:S(2)}, u32[]{:S(2)}) async-start(bf16[32,2,128,128]{3,2,1,0:T(8,128)(2,1)} %shard_map.148), calls=%async_computation | async-start | bytes 4194304 | tf_op jit(solution)/shard_map/all_to_all | solution.py:412
  14.2 0.0 copy-done
  14.2 0.0 copy-done.11
  14.2 1.4 %fusion = bf16[4096,128]{0,1:T(8,128)(2,1)} fusion(bf16[8,128]{1,0:T(8,128)(2,1)S(1)} %copy-done.11, bf16[8,4096]{1,0:T(8,128)(2,1)S(1)} %copy-done), kind=kOutput, calls=%fused_computation.1 | convolution fusion | flops 8912896 | bytes 1116160 | tf_op jit(solution)/shard_map/gt,gc->tc/dot_general | solution.py:406
  15.6 1.6 %copy.16 = bf16[4096,128]{1,0:T(8,128)(2,1)S(1)} copy(bf16[4096,128]{0,1:T(8,128)(2,1)} %fusion) | data formatting | bytes 2097152 | tf_op jit(solution)/shard_map/convert_element_type | solution.py:408
  17.3 0.0 copy-start.2
  17.3 2.2 %copy-done.2 = bf16[16,512,256]{2,1,0:T(8,128)(2,1)S(1)} copy-done((bf16[16,512,256]{2,1,0:T(8,128)(2,1)S(1)}, bf16[16,512,256]{2,1,0:T(8,128)(2,1)}, u32[]{:S(2)}) %copy-start.2) | copy-done | bytes 4194328
  19.5 0.0 copy-start.3
  19.5 1.0 %copy-done.3 = bf16[4,256,256]{2,1,0:T(8,128)(2,1)S(1)} copy-done((bf16[4,256,256]{2,1,0:T(8,128)(2,1)S(1)}, bf16[4,256,256]{2,1,0:T(8,128)(2,1)}, u32[]{:S(2)}) %copy-start.3) | copy-done | bytes 524312
  20.5 0.0 copy-start.1
  20.5 4.3 %shard_map.149.h_hbm = f32[32,256,128]{2,1,0:T(8,128)S(1)} custom-call(bf16[32,128,128]{2,1,0:T(8,128)(2,1)S(1)} %bitcast.24, bf16[16,512,256]{2,1,0:T(8,128)(2,1)S(1)} %copy-done.2, bf16[4,256,256]{2,1,0:T(8,128)(2,1)S(1)} %copy-done.3), custom_call_target="tpu_custom_call" | custom-call | flops 4294967296 | bytes 16777216 | tf_op jit(solution)/shard_map/pallas_call | solution.py:349
  24.8 0.0 copy-start.10
  24.8 1.9 %copy-done.10 = f32[32,256,128]{2,1,0:T(8,128)} copy-done((f32[32,256,128]{2,1,0:T(8,128)}, f32[32,256,128]{2,1,0:T(8,128)S(1)}, u32[]{:S(2)}) %copy-start.10) | copy-done | bytes 4194328
  26.7 15.9 %all-to-all-done.v_hbm = bf16[32,2,128,128]{3,2,1,0:T(8,128)(2,1)S(1)} async-done(((bf16[32,2,128,128]{3,2,1,0:T(8,128)(2,1)}), bf16[32,2,128,128]{3,2,1,0:T(8,128)(2,1)S(1)}, u32[]{:S(2)}, u32[]{:S(2)}) %all-to-all-start) | async-done | bytes 2097184 | tf_op jit(solution)/shard_map/all_to_all | solution.py:412
  42.6 0.0 copy-done.1
  42.6 0.0 copy-start.4
  42.6 1.0 %copy-done.4 = bf16[4,256,256]{2,1,0:T(8,128)(2,1)S(1)} copy-done((bf16[4,256,256]{2,1,0:T(8,128)(2,1)S(1)}, bf16[4,256,256]{2,1,0:T(8,128)(2,1)}, u32[]{:S(2)}) %copy-start.4) | copy-done | bytes 524312
  43.6 11.6 %shard_map.150 = (bf16[32,2,128,128]{3,2,1,0:T(8,128)(2,1)}, bf16[32,256,256]{2,1,0:T(8,128)(2,1)}) custom-call(bf16[32,2,128,128]{3,2,1,0:T(8,128)(2,1)S(1)} %all-to-all-done.v_hbm, f32[32,256,128]{2,1,0:T(8,128)} %copy-done.10, f32[1,128]{1,0:T(1,128)S(1)} %bitcast.27, bf16[16,512,256]{2,1,0:T(8,128)(2,1)} %constant.58.clone.one_ref.one_hbm, ...), custom_call_target="tpu_custom_call" | custom-call | flops 6442450944 | bytes 20971520 | tf_op jit(solution)/shard_map/pallas_call | solution.py:374
  55.3 0.0 copy-start.5
  55.3 0.0 copy-start.6
  55.3 0.0 copy-start.7
  55.3 0.0 copy-start.8
  55.3 5.0 %all-to-all-start.1 = ((bf16[32,2,128,128]{3,2,1,0:T(8,128)(2,1)}), bf16[32,2,128,128]{3,2,1,0:T(8,128)(2,1)}, u32[]{:S(2)}, u32[]{:S(2)}) async-start(bf16[32,2,128,128]{3,2,1,0:T(8,128)(2,1)} %get-tuple-element.7), calls=%async_computation.1 | async-start | bytes 4194304 | tf_op jit(solution)/shard_map/all_to_all | solution.py:412
  60.4 0.0 copy-done.5
  60.4 0.0 copy-done.6
  60.4 0.0 copy-done.7
  60.4 0.0 copy-done.8
  60.5 0.0 copy-start.9
  60.5 2.2 %copy-done.9 = bf16[32,256,256]{2,1,0:T(8,128)(2,1)S(1)} copy-done((bf16[32,256,256]{2,1,0:T(8,128)(2,1)S(1)}, bf16[32,256,256]{2,1,0:T(8,128)(2,1)}, u32[]{:S(2)}) %copy-start.9) | copy-done | bytes 4194328
  62.6 2.9 %shard_map.152 = f32[256,128]{1,0:T(8,128)S(1)} custom-call(bf16[32,256,256]{2,1,0:T(8,128)(2,1)S(1)} %copy-done.9, bf16[4,256,256]{2,1,0:T(8,128)(2,1)S(1)} %copy-done.4, bf16[8,256,128]{2,1,0:T(8,128)(2,1)S(1)} %copy-done.5, f32[128,256]{1,0:T(8,128)S(1)} %copy-done.7, f32[128,256]{1,0:T(8,128)S(1)} %copy-done.8, bf16[512,256]{1,0:T(8,128)(2,1)S(1)} %copy-done.6), custom_call_target="tpu_custom_call" | custom-call | flops 2147483648 | bytes 16777216 | tf_op jit(solution)/shard_map/pallas_call | solution.py:349
  65.6 2.3 %collective-permute-start.2 = (f32[64,128]{1,0:T(8,128)S(1)}, f32[64,128]{1,0:T(8,128)S(1)}, u32[]{:S(2)}, u32[]{:S(2)}) collective-permute-start(f32[64,128]{1,0:T(8,128)S(1)} %get-tuple-element.12), channel_id=1, source_target_pairs={{0,96},{32,0},{64,32},{96,64},{1,97},{33,1},{65,33},{97,65},{2,98}... | collective-permute-start | bytes 98312 | tf_op jit(solution)/shard_map/ppermute | solution.py:424
  67.9 0.8 collective-permute-start.1
  68.7 0.2 collective-permute-start
  68.8 6.7 %collective-permute-done.2 = f32[64,128]{1,0:T(8,128)S(1)} collective-permute-done((f32[64,128]{1,0:T(8,128)S(1)}, f32[64,128]{1,0:T(8,128)S(1)}, u32[]{:S(2)}, u32[]{:S(2)}) %collective-permute-start.2) | collective-permute-done | bytes 32800 | tf_op jit(solution)/shard_map/ppermute | solution.py:424
  75.5 6.0 %collective-permute-done.1 = f32[64,128]{1,0:T(8,128)S(1)} collective-permute-done((f32[64,128]{1,0:T(8,128)S(1)}, f32[64,128]{1,0:T(8,128)S(1)}, u32[]{:S(2)}, u32[]{:S(2)}) %collective-permute-start.1) | collective-permute-done | bytes 32800 | tf_op jit(solution)/shard_map/ppermute | solution.py:424
  81.5 0.0 collective-permute-done
  81.5 0.6 reshape.17
  82.2 6.8 %all-to-all-done.1.back_ref = bf16[32,2,128,128]{3,2,1,0:T(8,128)(2,1)} async-done(((bf16[32,2,128,128]{3,2,1,0:T(8,128)(2,1)}), bf16[32,2,128,128]{3,2,1,0:T(8,128)(2,1)}, u32[]{:S(2)}, u32[]{:S(2)}) %all-to-all-start.1) | async-done | bytes 2097184 | tf_op jit(solution)/shard_map/all_to_all | solution.py:412
  89.0 4.0 %shard_map.151 = (bf16[128,4096]{1,0:T(8,128)(2,1)}, bf16[128,4096]{1,0:T(8,128)(2,1)}) custom-call(bf16[32,2,128,128]{3,2,1,0:T(8,128)(2,1)} %all-to-all-done.1.back_ref, bf16[128,4096]{1,0:T(8,128)(2,1)} %bitcast.29), custom_call_target="tpu_custom_call" | custom-call | tf_op jit(solution)/shard_map/pallas_call | solution.py:337
  (2 shorter events, 0.0 us)
Async XLA Ops:
  0.6 13.6 %copy-start = (bf16[8,4096]{1,0:T(8,128)(2,1)S(1)}, bf16[8,4096]{1,0:T(8,128)(2,1)}, u32[]{:S(2)}) copy-start(bf16[8,4096]{1,0:T(8,128)(2,1)} %param.16) | copy-start | bytes 196612
  4.8 9.4 %copy-start.11 = (bf16[8,128]{1,0:T(8,128)(2,1)S(1)}, bf16[8,128]{1,0:T(8,128)(2,1)}, u32[]{:S(2)}) copy-start(bf16[8,128]{1,0:T(8,128)(2,1)} %constant.65.clone) | copy-start | bytes 6148
  4.8 37.8 %all-to-all-start = ((bf16[32,2,128,128]{3,2,1,0:T(8,128)(2,1)}), bf16[32,2,128,128]{3,2,1,0:T(8,128)(2,1)S(1)}, u32[]{:S(2)}, u32[]{:S(2)}) async-start(bf16[32,2,128,128]{3,2,1,0:T(8,128)(2,1)} %shard_map.148), calls=%async_computation | async-start | bytes 4194304 | tf_op jit(solution)/shard_map/all_to_all | solution.py:412
  17.3 2.2 %copy-start.2 = (bf16[16,512,256]{2,1,0:T(8,128)(2,1)S(1)}, bf16[16,512,256]{2,1,0:T(8,128)(2,1)}, u32[]{:S(2)}) copy-start(bf16[16,512,256]{2,1,0:T(8,128)(2,1)} %constant.58.clone.one_ref.one_hbm) | copy-start | bytes 12582916
  19.5 1.0 %copy-start.3 = (bf16[4,256,256]{2,1,0:T(8,128)(2,1)S(1)}, bf16[4,256,256]{2,1,0:T(8,128)(2,1)}, u32[]{:S(2)}) copy-start(bf16[4,256,256]{2,1,0:T(8,128)(2,1)} %constant.60.clone.inner_ref.inner_hbm) | copy-start | bytes 1572868
  20.5 22.1 %copy-start.1 = (f32[128]{0:T(128)S(1)}, f32[128]{0:T(128)}, u32[]{:S(2)}) copy-start(f32[128]{0:T(128)} %param.17) | copy-start | bytes 1540
  24.8 1.9 %copy-start.10 = (f32[32,256,128]{2,1,0:T(8,128)}, f32[32,256,128]{2,1,0:T(8,128)S(1)}, u32[]{:S(2)}) copy-start(f32[32,256,128]{2,1,0:T(8,128)S(1)} %shard_map.149.h_hbm) | copy-start | bytes 12582916
  42.6 1.0 %copy-start.4 = (bf16[4,256,256]{2,1,0:T(8,128)(2,1)S(1)}, bf16[4,256,256]{2,1,0:T(8,128)(2,1)}, u32[]{:S(2)}) copy-start(bf16[4,256,256]{2,1,0:T(8,128)(2,1)} %constant.60.clone.inner_ref.inner_hbm) | copy-start | bytes 1572868
  55.3 5.1 %copy-start.5 = (bf16[8,256,128]{2,1,0:T(8,128)(2,1)S(1)}, bf16[8,256,128]{2,1,0:T(8,128)(2,1)}, u32[]{:S(2)}) copy-start(bf16[8,256,128]{2,1,0:T(8,128)(2,1)} %constant.61.clone.member_ref) | copy-start | bytes 1572868
  55.3 5.1 %copy-start.6 = (bf16[512,256]{1,0:T(8,128)(2,1)S(1)}, bf16[512,256]{1,0:T(8,128)(2,1)}, u32[]{:S(2)}) copy-start(bf16[512,256]{1,0:T(8,128)(2,1)} %constant.64.clone.grad_ref) | copy-start | bytes 786436
  55.3 5.1 %copy-start.7 = (f32[128,256]{1,0:T(8,128)S(1)}, f32[128,256]{1,0:T(8,128)}, u32[]{:S(2)}) copy-start(f32[128,256]{1,0:T(8,128)} %constant.62.clone.turn_cos_ref) | copy-start | bytes 393220
  55.3 5.1 %copy-start.8 = (f32[128,256]{1,0:T(8,128)S(1)}, f32[128,256]{1,0:T(8,128)}, u32[]{:S(2)}) copy-start(f32[128,256]{1,0:T(8,128)} %constant.63.clone.turn_sin_ref) | copy-start | bytes 393220
  55.3 33.7 %all-to-all-start.1 = ((bf16[32,2,128,128]{3,2,1,0:T(8,128)(2,1)}), bf16[32,2,128,128]{3,2,1,0:T(8,128)(2,1)}, u32[]{:S(2)}, u32[]{:S(2)}) async-start(bf16[32,2,128,128]{3,2,1,0:T(8,128)(2,1)} %get-tuple-element.7), calls=%async_computation.1 | async-start | bytes 4194304 | tf_op jit(solution)/shard_map/all_to_all | solution.py:412
  60.5 2.2 %copy-start.9 = (bf16[32,256,256]{2,1,0:T(8,128)(2,1)S(1)}, bf16[32,256,256]{2,1,0:T(8,128)(2,1)}, u32[]{:S(2)}) copy-start(bf16[32,256,256]{2,1,0:T(8,128)(2,1)} %get-tuple-element.10.spec_ref) | copy-start | bytes 12582916
  65.6 9.9 %collective-permute-start.2 = (f32[64,128]{1,0:T(8,128)S(1)}, f32[64,128]{1,0:T(8,128)S(1)}, u32[]{:S(2)}, u32[]{:S(2)}) collective-permute-start(f32[64,128]{1,0:T(8,128)S(1)} %get-tuple-element.12), channel_id=1, source_target_pairs={{0,96},{32,0},{64,32},{96,64},{1,97},{33,1},{65,33},{97,65},{2,98}... | collective-permute-start | bytes 98312 | tf_op jit(solution)/shard_map/ppermute | solution.py:424
  67.9 13.6 %collective-permute-start.1 = (f32[64,128]{1,0:T(8,128)S(1)}, f32[64,128]{1,0:T(8,128)S(1)}, u32[]{:S(2)}, u32[]{:S(2)}) collective-permute-start(f32[64,128]{1,0:T(8,128)S(1)} %get-tuple-element.13), channel_id=1, source_target_pairs={{0,64},{32,96},{64,0},{96,32},{1,65},{33,97},{65,1},{97,33},{2,66}... | collective-permute-start | bytes 98312 | tf_op jit(solution)/shard_map/ppermute | solution.py:424
  68.7 12.9 %collective-permute-start = (f32[64,128]{1,0:T(8,128)S(1)}, f32[64,128]{1,0:T(8,128)S(1)}, u32[]{:S(2)}, u32[]{:S(2)}) collective-permute-start(f32[64,128]{1,0:T(8,128)S(1)} %get-tuple-element.11), channel_id=1, source_target_pairs={{0,32},{32,64},{64,96},{96,0},{1,33},{33,65},{65,97},{97,1},{2,34}... | collective-permute-start | bytes 98312 | tf_op jit(solution)/shard_map/ppermute | solution.py:424

commit v3 on v2

--- a/solution.py
+++ b/solution.py
@@ -103,7 +103,7 @@
         held = given[:, 8 * h : 8 * h + 8].reshape(256, lanes).astype(BF16)
         out.append(dot(one_ref[2 * p + h], held).reshape(64, 8, lanes))
     both = jnp.concatenate(out, 1).astype(BF16)
-    row = pl.multiple_of(p * 16, 16)
+    row = p * 16 if isinstance(p, int) else pl.multiple_of(p * 16, 16)
     u_ref[:, pl.ds(row, 16), :] = both[:OUTER]
     u_ref[:, pl.ds(INNER + row, 16), :] = both[OUTER:]
 
@@ -144,6 +144,19 @@
         body(count * m, count, False)
 
 
+OUTER_AT_ONCE = 2
+SLABS_AT_ONCE = 2
+LAST_AT_ONCE = 2
+
+
+def several(count, body, first=0):
+    if count - first <= 1:
+        for g in range(first, count):
+            body(g)
+    else:
+        pl.loop(first, count)(body)
+
+
 def filter_kernel(v_ref, one_ref, inner_ref, spec_ref, u_ref):
     @pl.loop(0, 8)
     def _(p):
@@ -160,18 +173,10 @@
 
 
 def main_kernel(
-    v_hbm, h_hbm, gain_hbm, one_hbm, inner_hbm, last_hbm, out_hbm, spec_hbm,
-    v_ref, h_ref, gain_ref, one_ref, inner_ref, last_ref, out_ref, u_ref, back_ref,
-    v_sem, h_sem, gain_sem, one_sem, inner_sem, last_sem, out_sem, spec_sem,
+    v_ref, h_hbm, gain_hbm, one_hbm, inner_hbm, last_hbm, out_hbm, spec_hbm,
+    h_ref, gain_ref, one_ref, inner_ref, last_ref, out_ref, u_ref, back_ref,
+    h_sem, gain_sem, one_sem, inner_sem, last_sem, out_sem, spec_sem,
 ):
-    def v_copy(p):
-        cut = pl.ds(pl.multiple_of(p * 16, 16), 16)
-        return pltpu.make_async_copy(v_hbm.at[:, :, cut], v_ref.at[:, :, cut], v_sem.at[p])
-
-    def out_copy(p):
-        cut = pl.ds(pl.multiple_of(p * 16, 16), 16)
-        return pltpu.make_async_copy(out_ref.at[:, :, cut], out_hbm.at[:, :, cut], out_sem.at[p])
-
     def table_copy(hbm, ref, sem, p):
         cut = pl.ds(2 * p, 2)
         return pltpu.make_async_copy(hbm.at[cut], ref.at[cut], sem.at[p])
@@ -185,7 +190,6 @@
 
     @pl.loop(0, 8)
     def _(p):
-        v_copy(p).start()
         table_copy(one_hbm, one_ref, one_sem, p).start()
 
     inner_copy.start()
@@ -194,13 +198,21 @@
     @pl.loop(0, 8)
     def _(p):
         slab_copy(h_hbm, h_ref, h_sem, p).start()
+
+    @pl.loop(0, 8)
+    def _(p):
         table_copy(last_hbm, last_ref, last_sem, p).start()
-        v_copy(p).wait()
-        table_copy(one_hbm, one_ref, one_sem, p).wait()
-        row = pl.multiple_of(p * 16, 16)
-        both = v_ref[:, :, pl.ds(row, 16), :].astype(F32)
-        outer_block(jnp.concatenate([both[:, 0], both[:, 1]], 2), one_ref, p, u_ref)
-
+
+    def outer_group(g):
+        for k in range(OUTER_AT_ONCE):
+            table_copy(one_hbm, one_ref, one_sem, g * OUTER_AT_ONCE + k).wait()
+        for k in range(OUTER_AT_ONCE):
+            p = g * OUTER_AT_ONCE + k
+            row = p * 16 if isinstance(p, int) else pl.multiple_of(p * 16, 16)
+            both = v_ref[:, :, pl.ds(row, 16), :].astype(F32)
+            outer_block(jnp.concatenate([both[:, 0], both[:, 1]], 2), one_ref, p, u_ref)
+
+    several(8 // OUTER_AT_ONCE, outer_group)
     inner_copy.wait()
 
     def body(start, count, packed):
@@ -222,23 +234,33 @@
             u_ref[start + k] = lane_cut(spec, k, PAIR).astype(BF16)
             back_ref[start + k] = lane_cut(back, k, PAIR)
 
-    slab_copy(h_hbm, h_ref, h_sem, 0).wait()
-    body(0, 1, True)
-    body(1, 3, False)
-    slab_copy(u_ref, spec_hbm, spec_sem, 0).start()
-
-    @pl.loop(1, 8)
-    def _(m):
-        slab_copy(h_hbm, h_ref, h_sem, m).wait()
-        body(4 * m, 4, False)
-        slab_copy(u_ref, spec_hbm, spec_sem, m).start()
-
+    def slab_group(g):
+        for k in range(SLABS_AT_ONCE):
+            slab_copy(h_hbm, h_ref, h_sem, g * SLABS_AT_ONCE + k).wait()
+        for k in range(SLABS_AT_ONCE):
+            m = g * SLABS_AT_ONCE + k
+            if isinstance(m, int) and m == 0:
+                body(0, 1, True)
+                body(1, 3, False)
+            else:
+                body(4 * m, 4, False)
+        for k in range(SLABS_AT_ONCE):
+            slab_copy(u_ref, spec_hbm, spec_sem, g * SLABS_AT_ONCE + k).start()
+
+    slab_group(0)
+    several(8 // SLABS_AT_ONCE, slab_group, 1)
     gain_copy.wait()
 
-    @pl.loop(0, 8)
-    def _(p):
-        table_copy(last_hbm, last_ref, last_sem, p).wait()
-        row = pl.multiple_of(p * 16, 16)
+    def last_group(g):
+        for k in range(LAST_AT_ONCE):
+            table_copy(last_hbm, last_ref, last_sem, g * LAST_AT_ONCE + k).wait()
+        for k in range(LAST_AT_ONCE):
+            last_block(g * LAST_AT_ONCE + k)
+        for k in range(LAST_AT_ONCE):
+            block_copy(out_ref, out_hbm, out_sem, g * LAST_AT_ONCE + k, 16).start()
+
+    def last_block(p):
+        row = p * 16 if isinstance(p, int) else pl.multiple_of(p * 16, 16)
         gain = gain_ref[...]
         given = v_ref[:, :, pl.ds(row, 16), :].astype(F32)
         out = [[], []]
@@ -258,12 +280,13 @@
                 )
         for a in range(2):
             out_ref[:, a, pl.ds(row, 16), :] = jnp.concatenate(out[a], 1).astype(BF16)
-        out_copy(p).start()
+
+    several(8 // LAST_AT_ONCE, last_group)
 
     @pl.loop(0, 8)
     def _(p):
         slab_copy(u_ref, spec_hbm, spec_sem, p).wait()
-        out_copy(p).wait()
+        block_copy(out_ref, out_hbm, out_sem, p, 16).wait()
 
 
 def filter_grad_kernel(
@@ -298,37 +321,80 @@
     filter_ref[...] = dot(turned, grad_ref[...]).T
 
 
-def gather_kernel(gate_ref, input_ref, cotan_ref, out_ref):
-    for k in range(out_ref.shape[0]):
-        cut = slice(LANES * k, LANES * k + LANES)
-        out_ref[k, 0] = input_ref[:, cut]
-        product = cotan_ref[:, cut].astype(F32) * gate_ref[:, cut].astype(F32)
-        out_ref[k, 1] = product.astype(BF16)
-
-
-def spread_kernel(back_ref, cotan_ref, gate_grad_ref, input_grad_ref):
-    for k in range(back_ref.shape[0]):
-        cut = slice(LANES * k, LANES * k + LANES)
-        product = cotan_ref[:, cut].astype(F32) * back_ref[k, 0].astype(F32)
-        gate_grad_ref[:, cut] = product.astype(BF16)
-        input_grad_ref[:, cut] = back_ref[k, 1]
-
-
-STEPS = 4
-ROWS_BLOCK = pl.BlockSpec((INNER, OUTER // STEPS * LANES), lambda i: (0, i))
-MOVED_BLOCK = pl.BlockSpec((OUTER // STEPS, 2, INNER, LANES), lambda i: (i, 0, 0, 0))
+def row_copy(source, target, sem, i, rows):
+    cut = pl.ds(i * rows, rows)
+    return pltpu.make_async_copy(source.at[cut], target.at[cut], sem.at[i])
+
+
+def block_copy(source, target, sem, i, rows):
+    cut = pl.ds(i * rows, rows)
+    return pltpu.make_async_copy(source.at[:, :, cut], target.at[:, :, cut], sem.at[i])
+
+
+def product(left, right):
+    return (left.astype(F32) * right.astype(F32)).astype(BF16)
+
+
+def gather_kernel(
+    gate_hbm, input_hbm, cotan_hbm, out_hbm, gate_ref, input_ref, cotan_ref, out_ref,
+    gate_sem, input_sem, cotan_sem, out_sem,
+):
+    operands = (
+        (gate_hbm, gate_ref, gate_sem),
+        (cotan_hbm, cotan_ref, cotan_sem),
+        (input_hbm, input_ref, input_sem),
+    )
+    for i in range(CUTS):
+        for operand in operands:
+            row_copy(*operand, i, CUT).start()
+    for i in range(CUTS):
+        for operand in operands:
+            row_copy(*operand, i, CUT).wait()
+        rows = pl.ds(i * CUT, CUT)
+        for k in range(OUTER):
+            lanes = slice(LANES * k, LANES * k + LANES)
+            out_ref[k, 0, rows] = input_ref[rows, lanes]
+            out_ref[k, 1, rows] = product(cotan_ref[rows, lanes], gate_ref[rows, lanes])
+        block_copy(out_ref, out_hbm, out_sem, i, CUT).start()
+    for i in range(CUTS):
+        block_copy(out_ref, out_hbm, out_sem, i, CUT).wait()
+
+
+def spread_kernel(
+    back_ref, cotan_ref, gate_hbm, input_hbm, gate_ref, input_ref, gate_sem, input_sem
+):
+    for i in range(CUTS):
+        rows = pl.ds(i * CUT, CUT)
+        for k in range(OUTER):
+            lanes = slice(LANES * k, LANES * k + LANES)
+            gate_ref[rows, lanes] = product(cotan_ref[rows, lanes], back_ref[k, 0, rows])
+            input_ref[rows, lanes] = back_ref[k, 1, rows]
+        row_copy(gate_ref, gate_hbm, gate_sem, i, CUT).start()
+        row_copy(input_ref, input_hbm, input_sem, i, CUT).start()
+    for i in range(CUTS):
+        row_copy(gate_ref, gate_hbm, gate_sem, i, CUT).wait()
+        row_copy(input_ref, input_hbm, input_sem, i, CUT).wait()
+
+
+CUT = 32
+CUTS = INNER // CUT
 MOVED = jax.ShapeDtypeStruct((OUTER, 2, INNER, LANES), BF16)
 ROWS = jax.ShapeDtypeStruct((INNER, OUTER * LANES), BF16)
 HELD = jax.ShapeDtypeStruct((OUTER, PAIR, PAIR), BF16)
+IN_HBM = pl.BlockSpec(memory_space=pltpu.HBM)
+IN_VMEM = pl.BlockSpec(memory_space=pltpu.VMEM)
+DMA = pltpu.SemaphoreType.DMA
 
 
 def gather(gate, given, cotan):
     return pl.pallas_call(
         gather_kernel,
-        grid=(STEPS,),
         out_shape=MOVED,
-        in_specs=[ROWS_BLOCK] * 3,
-        out_specs=MOVED_BLOCK,
+        in_specs=[IN_HBM] * 3,
+        out_specs=IN_HBM,
+        scratch_shapes=[pltpu.VMEM(ROWS.shape, BF16)] * 3
+        + [pltpu.VMEM(MOVED.shape, BF16)]
+        + [DMA((CUTS,))] * 4,
         compiler_params=pltpu.CompilerParams(vmem_limit_bytes=60 << 20),
     )(gate, given, cotan)
 
@@ -336,11 +402,11 @@
 def spread(back, cotan):
     return pl.pallas_call(
         spread_kernel,
-        grid=(STEPS,),
         out_shape=(ROWS, ROWS),
-        in_specs=[MOVED_BLOCK, ROWS_BLOCK],
-        out_specs=(ROWS_BLOCK, ROWS_BLOCK),
-        compiler_params=pltpu.CompilerParams(vmem_limit_bytes=60 << 20),
+        in_specs=[IN_VMEM] * 2,
+        out_specs=(IN_HBM, IN_HBM),
+        scratch_shapes=[pltpu.VMEM(ROWS.shape, BF16)] * 2 + [DMA((CUTS,))] * 2,
+        compiler_params=pltpu.CompilerParams(vmem_limit_bytes=8 << 20),
     )(back, cotan)
 
 
@@ -368,26 +434,24 @@
 
 
 def main_path(t, moved, kernel_spec, gains):
-    operands = (moved, kernel_spec, gains, t["one"], t["inner"], t["last"])
-    space = pl.BlockSpec(memory_space=pltpu.HBM)
-    sems = pltpu.SemaphoreType.DMA
+    operands = (kernel_spec, gains, t["one"], t["inner"], t["last"])
     return pl.pallas_call(
         main_kernel,
         out_shape=(MOVED, HELD),
-        in_specs=[space] * len(operands),
-        out_specs=(space, space),
+        in_specs=[IN_VMEM] + [IN_HBM] * len(operands),
+        out_specs=(IN_HBM, IN_HBM),
         scratch_shapes=[pltpu.VMEM(o.shape, o.dtype) for o in operands]
         + [
             pltpu.VMEM(MOVED.shape, BF16),
             pltpu.VMEM(HELD.shape, BF16),
             pltpu.VMEM(HELD.shape, F32),
-            sems((8,)), sems((8,)), sems, sems((8,)), sems, sems((8,)), sems((8,)), sems((8,)),
+            DMA((8,)), DMA, DMA((8,)), DMA, DMA((8,)), DMA((8,)), DMA((8,)),
         ],
-        compiler_params=pltpu.CompilerParams(vmem_limit_bytes=48 << 20),
+        compiler_params=pltpu.CompilerParams(vmem_limit_bytes=59 << 20),
         cost_estimate=pl.CostEstimate(
             flops=6 << 30, bytes_accessed=20 << 20, transcendentals=0
         ),
-    )(*operands)
+    )(moved, *operands)
 
 
 def filter_gradient(t, spec):

time: 94.3 us -> 89 us (0.944)
  Pallas kernels: 27 us -> 22.8 us
  waiting for transfers between devices: 35.4 us -> 34.4 us
  matrix products: 1.44 us -> 0.47 us
    pallas_call x3, Pallas kernels: 19.8 us -> 15.6 us  [the longest x1 11.3 us: main_path(): pl.pallas_call(main_kernel, out_shape=(MOVED, HELD), in_specs=[IN_VMEM] +...]
    ppermute x3, waiting for transfers between devices: 12.7 us -> 8.88 us  [sum_over_sequences(): lax.ppermute(share((place + hop) % count), 'dp', [(i, (i + hop) % count)...]
    all_to_all x2, waiting for transfers between devices: 22.7 us -> 25.5 us  [exchange(): lax.all_to_all(blocks, 'ctx', split_axis=0, concat_axis=0, tiled=True)]
    unnamed x24, local copies, waits for them, and re-layouts: 8.43 us -> 10.3 us
    dot_general x1, matrix products: 1.44 us -> 0.47 us  [lay_filters(): jnp.einsum('gt,gc->tc', filters, jnp.asarray(member, BF16), preferred_ele...]
    convert_element_type x1, local copies, waits for them, and re-layouts: 1.61 us -> 0.66 us  [lay_filters(): return jnp.einsum('gt,gc->tc', filters, jnp.asarray(member, BF16), prefer...]
  transfers between devices with their start and end apart: 5 -> 5, of which waited for: 4 -> 4; matrix products, arithmetic and copies ran while one was open for 4% -> 2% of each run, Pallas kernels for 8% -> 8%
where the time goes in v3:
time: 89 us; the launch traced here: 87.7 us
  waiting for transfers between devices  34.4 us (39%)
  Pallas kernels  22.8 us (26%)
  starting transfers between devices  17.5 us (20%)
  local copies, waits for them, and re-layouts  11.6 us (13%)
    all_to_all x2, waiting for transfers between devices, exchange(): lax.all_to_all(blocks, 'ctx', split_axis=0, concat_axis=0, tiled=True)  25.5 us
    all_to_all x2, starting transfers between devices, exchange(): lax.all_to_all(blocks, 'ctx', split_axis=0, concat_axis=0, tiled=True)  14.3 us
    pallas_call x1, Pallas kernels, main_path(): pl.pallas_call(main_kernel, out_shape=(MOVED, HELD), in_specs=[IN_VMEM] +...  11.3 us
    unnamed x24, local copies, waits for them, and re-layouts  10.3 us
    ppermute x3, waiting for transfers between devices, sum_over_sequences(): lax.ppermute(share((place + hop) % count), 'dp', [(i, (i + hop) % count)...  8.88 us
    pallas_call x2, Pallas kernels, call(): pl.pallas_call(kernel, out_shape=outs, in_specs=[space] * len(operands),...  7.19 us
    ppermute x3, starting transfers between devices, sum_over_sequences(): lax.ppermute(share((place + hop) % count), 'dp', [(i, (i + hop) % count)...  3.19 us
    pallas_call x1, Pallas kernels, gather(): pl.pallas_call(gather_kernel, out_shape=MOVED, in_specs=[IN_HBM] * 3, out...  2.9 us
  transfers between devices with their start and end apart: 5, of which 4 were waited for; matrix products, arithmetic and copies ran while one was open for 2% of the time, Pallas kernels for 8%

profile of v3, /device:TPU:0, one launch (start us, length us, event | category | flops | bytes accessed | tf_op | source)
XLA Modules:
  0.0 87.7 jit_solution(7028756488392955037)
XLA Ops:
  0.6 0.0 copy-start
  0.6 2.9 %shard_map.148 = bf16[32,2,128,128]{3,2,1,0:T(8,128)(2,1)} custom-call(bf16[128,4096]{1,0:T(8,128)(2,1)} %bitcast.29, bf16[128,4096]{1,0:T(8,128)(2,1)} %bitcast.30, bf16[128,4096]{1,0:T(8,128)(2,1)} %bitcast.24), custom_call_target="tpu_custom_call" | custom-call | tf_op jit(solution)/shard_map/pallas_call | solution.py:390
  3.5 0.0 copy-start.11
  3.6 9.4 %all-to-all-start = ((bf16[32,2,128,128]{3,2,1,0:T(8,128)(2,1)}), bf16[32,2,128,128]{3,2,1,0:T(8,128)(2,1)}, u32[]{:S(2)}, u32[]{:S(2)}) async-start(bf16[32,2,128,128]{3,2,1,0:T(8,128)(2,1)} %shard_map.148), calls=%async_computation | async-start | bytes 4194304 | tf_op jit(solution)/shard_map/all_to_all | solution.py:476
  13.0 0.0 copy-done
  13.0 0.0 copy-done.11
  13.0 0.0 copy-start.3
  13.0 0.5 fusion
  13.5 0.7 copy.16
  14.2 0.0 copy-done.3
  14.2 0.0 copy-start.2
  14.2 2.2 %copy-done.2 = bf16[16,512,256]{2,1,0:T(8,128)(2,1)S(1)} copy-done((bf16[16,512,256]{2,1,0:T(8,128)(2,1)S(1)}, bf16[16,512,256]{2,1,0:T(8,128)(2,1)}, u32[]{:S(2)}) %copy-start.2) | copy-done | bytes 4194328
  16.4 4.3 %shard_map.149.h_hbm = f32[32,256,128]{2,1,0:T(8,128)S(1)} custom-call(bf16[32,128,128]{2,1,0:T(8,128)(2,1)S(1)} %bitcast.26, bf16[16,512,256]{2,1,0:T(8,128)(2,1)S(1)} %copy-done.2, bf16[4,256,256]{2,1,0:T(8,128)(2,1)S(1)} %copy-done.3), custom_call_target="tpu_custom_call" | custom-call | flops 4294967296 | bytes 16777216 | tf_op jit(solution)/shard_map/pallas_call | solution.py:415
  20.6 0.0 copy-start.10
  20.6 1.9 %copy-done.10 = f32[32,256,128]{2,1,0:T(8,128)} copy-done((f32[32,256,128]{2,1,0:T(8,128)}, f32[32,256,128]{2,1,0:T(8,128)S(1)}, u32[]{:S(2)}) %copy-start.10) | copy-done | bytes 4194328
  22.6 18.8 %all-to-all-done.v_ref = bf16[32,2,128,128]{3,2,1,0:T(8,128)(2,1)} async-done(((bf16[32,2,128,128]{3,2,1,0:T(8,128)(2,1)}), bf16[32,2,128,128]{3,2,1,0:T(8,128)(2,1)}, u32[]{:S(2)}, u32[]{:S(2)}) %all-to-all-start) | async-done | bytes 2097184 | tf_op jit(solution)/shard_map/all_to_all | solution.py:476
  41.4 11.3 %shard_map.150 = (bf16[32,2,128,128]{3,2,1,0:T(8,128)(2,1)}, bf16[32,256,256]{2,1,0:T(8,128)(2,1)}) custom-call(bf16[32,2,128,128]{3,2,1,0:T(8,128)(2,1)} %all-to-all-done.v_ref, f32[32,256,128]{2,1,0:T(8,128)} %copy-done.10, f32[1,128]{1,0:T(1,128)} %bitcast.33, bf16[16,512,256]{2,1,0:T(8,128)(2,1)} %constant.58.clone.one_ref.one_hbm, ...), custom_call_target="tpu_custom_call" | custom-call | flops 6442450944 | bytes 20971520 | tf_op jit(solution)/shard_map/pallas_call | solution.py:438
  52.7 0.0 copy-start.7
  52.7 4.9 %all-to-all-start.1 = ((bf16[32,2,128,128]{3,2,1,0:T(8,128)(2,1)}), bf16[32,2,128,128]{3,2,1,0:T(8,128)(2,1)S(1)}, u32[]{:S(2)}, u32[]{:S(2)}) async-start(bf16[32,2,128,128]{3,2,1,0:T(8,128)(2,1)} %get-tuple-element.7), calls=%async_computation.1 | async-start | bytes 4194304 | tf_op jit(solution)/shard_map/all_to_all | solution.py:476
  57.6 0.0 copy-done.7
  57.7 0.0 copy-start.4
  57.7 1.0 %copy-done.4 = bf16[4,256,256]{2,1,0:T(8,128)(2,1)S(1)} copy-done((bf16[4,256,256]{2,1,0:T(8,128)(2,1)S(1)}, bf16[4,256,256]{2,1,0:T(8,128)(2,1)}, u32[]{:S(2)}) %copy-start.4) | copy-done | bytes 524312
  58.7 0.0 copy-start.5
  58.7 1.0 %copy-done.5 = bf16[8,256,128]{2,1,0:T(8,128)(2,1)S(1)} copy-done((bf16[8,256,128]{2,1,0:T(8,128)(2,1)S(1)}, bf16[8,256,128]{2,1,0:T(8,128)(2,1)}, u32[]{:S(2)}) %copy-start.5) | copy-done | bytes 524312
  59.7 0.0 copy-start.6
  59.7 0.9 %copy-done.6 = bf16[512,256]{1,0:T(8,128)(2,1)S(1)} copy-done((bf16[512,256]{1,0:T(8,128)(2,1)S(1)}, bf16[512,256]{1,0:T(8,128)(2,1)}, u32[]{:S(2)}) %copy-start.6) | copy-done | bytes 262168
  60.7 0.0 copy-start.8
  60.7 0.9 %copy-done.8 = f32[128,256]{1,0:T(8,128)S(1)} copy-done((f32[128,256]{1,0:T(8,128)S(1)}, f32[128,256]{1,0:T(8,128)}, u32[]{:S(2)}) %copy-start.8) | copy-done | bytes 131096
  61.6 0.0 copy-start.9
  61.6 2.2 %copy-done.9 = bf16[32,256,256]{2,1,0:T(8,128)(2,1)S(1)} copy-done((bf16[32,256,256]{2,1,0:T(8,128)(2,1)S(1)}, bf16[32,256,256]{2,1,0:T(8,128)(2,1)}, u32[]{:S(2)}) %copy-start.9) | copy-done | bytes 4194328
  63.8 0.0 copy-start.1
  63.8 2.9 %shard_map.152 = f32[256,128]{1,0:T(8,128)S(1)} custom-call(bf16[32,256,256]{2,1,0:T(8,128)(2,1)S(1)} %copy-done.9, bf16[4,256,256]{2,1,0:T(8,128)(2,1)S(1)} %copy-done.4, bf16[8,256,128]{2,1,0:T(8,128)(2,1)S(1)} %copy-done.5, f32[128,256]{1,0:T(8,128)S(1)} %copy-done.7, f32[128,256]{1,0:T(8,128)S(1)} %copy-done.8, bf16[512,256]{1,0:T(8,128)(2,1)S(1)} %copy-done.6), custom_call_target="tpu_custom_call" | custom-call | flops 2147483648 | bytes 16777216 | tf_op jit(solution)/shard_map/pallas_call | solution.py:415
  66.8 2.3 %collective-permute-start.2 = (f32[64,128]{1,0:T(8,128)S(1)}, f32[64,128]{1,0:T(8,128)S(1)}, u32[]{:S(2)}, u32[]{:S(2)}) collective-permute-start(f32[64,128]{1,0:T(8,128)S(1)} %get-tuple-element.12), channel_id=1, source_target_pairs={{0,96},{32,0},{64,32},{96,64},{1,97},{33,1},{65,33},{97,65},{2,98}... | collective-permute-start | bytes 98312 | tf_op jit(solution)/shard_map/ppermute | solution.py:488
  69.1 0.7 collective-permute-start.1
  69.8 0.2 collective-permute-start
  69.9 2.3 %collective-permute-done.2 = f32[64,128]{1,0:T(8,128)S(1)} collective-permute-done((f32[64,128]{1,0:T(8,128)S(1)}, f32[64,128]{1,0:T(8,128)S(1)}, u32[]{:S(2)}, u32[]{:S(2)}) %collective-permute-start.2) | collective-permute-done | bytes 32800 | tf_op jit(solution)/shard_map/ppermute | solution.py:488
  72.3 6.5 %collective-permute-done.1 = f32[64,128]{1,0:T(8,128)S(1)} collective-permute-done((f32[64,128]{1,0:T(8,128)S(1)}, f32[64,128]{1,0:T(8,128)S(1)}, u32[]{:S(2)}, u32[]{:S(2)}) %collective-permute-start.1) | collective-permute-done | bytes 32800 | tf_op jit(solution)/shard_map/ppermute | solution.py:488
  78.8 0.0 collective-permute-done
  78.8 0.6 reshape.17
  79.5 6.7 %all-to-all-done.1.back_ref = bf16[32,2,128,128]{3,2,1,0:T(8,128)(2,1)S(1)} async-done(((bf16[32,2,128,128]{3,2,1,0:T(8,128)(2,1)}), bf16[32,2,128,128]{3,2,1,0:T(8,128)(2,1)S(1)}, u32[]{:S(2)}, u32[]{:S(2)}) %all-to-all-start.1) | async-done | bytes 2097184 | tf_op jit(solution)/shard_map/all_to_all | solution.py:476
  86.2 0.0 copy-done.1
  86.2 1.4 %shard_map.151 = (bf16[128,4096]{1,0:T(8,128)(2,1)}, bf16[128,4096]{1,0:T(8,128)(2,1)}) custom-call(bf16[32,2,128,128]{3,2,1,0:T(8,128)(2,1)S(1)} %all-to-all-done.1.back_ref, bf16[128,4096]{1,0:T(8,128)(2,1)S(1)} %bitcast.25), custom_call_target="tpu_custom_call" | custom-call | tf_op jit(solution)/shard_map/pallas_call | solution.py:403
  (2 shorter events, 0.0 us)
Async XLA Ops:
  0.6 12.3 %copy-start = (bf16[8,4096]{1,0:T(8,128)(2,1)S(1)}, bf16[8,4096]{1,0:T(8,128)(2,1)}, u32[]{:S(2)}) copy-start(bf16[8,4096]{1,0:T(8,128)(2,1)} %param.16) | copy-start | bytes 196612
  3.5 9.4 %copy-start.11 = (bf16[8,128]{1,0:T(8,128)(2,1)S(1)}, bf16[8,128]{1,0:T(8,128)(2,1)}, u32[]{:S(2)}) copy-start(bf16[8,128]{1,0:T(8,128)(2,1)} %constant.65.clone) | copy-start | bytes 6148
  3.6 37.8 %all-to-all-start = ((bf16[32,2,128,128]{3,2,1,0:T(8,128)(2,1)}), bf16[32,2,128,128]{3,2,1,0:T(8,128)(2,1)}, u32[]{:S(2)}, u32[]{:S(2)}) async-start(bf16[32,2,128,128]{3,2,1,0:T(8,128)(2,1)} %shard_map.148), calls=%async_computation | async-start | bytes 4194304 | tf_op jit(solution)/shard_map/all_to_all | solution.py:476
  13.0 1.2 %copy-start.3 = (bf16[4,256,256]{2,1,0:T(8,128)(2,1)S(1)}, bf16[4,256,256]{2,1,0:T(8,128)(2,1)}, u32[]{:S(2)}) copy-start(bf16[4,256,256]{2,1,0:T(8,128)(2,1)} %constant.60.clone.inner_ref.inner_hbm) | copy-start | bytes 1572868
  14.2 2.2 %copy-start.2 = (bf16[16,512,256]{2,1,0:T(8,128)(2,1)S(1)}, bf16[16,512,256]{2,1,0:T(8,128)(2,1)}, u32[]{:S(2)}) copy-start(bf16[16,512,256]{2,1,0:T(8,128)(2,1)} %constant.58.clone.one_ref.one_hbm) | copy-start | bytes 12582916
  20.6 1.9 %copy-start.10 = (f32[32,256,128]{2,1,0:T(8,128)}, f32[32,256,128]{2,1,0:T(8,128)S(1)}, u32[]{:S(2)}) copy-start(f32[32,256,128]{2,1,0:T(8,128)S(1)} %shard_map.149.h_hbm) | copy-start | bytes 12582916
  52.7 5.0 %copy-start.7 = (f32[128,256]{1,0:T(8,128)S(1)}, f32[128,256]{1,0:T(8,128)}, u32[]{:S(2)}) copy-start(f32[128,256]{1,0:T(8,128)} %constant.62.clone.turn_cos_ref) | copy-start | bytes 393220
  52.7 33.5 %all-to-all-start.1 = ((bf16[32,2,128,128]{3,2,1,0:T(8,128)(2,1)}), bf16[32,2,128,128]{3,2,1,0:T(8,128)(2,1)S(1)}, u32[]{:S(2)}, u32[]{:S(2)}) async-start(bf16[32,2,128,128]{3,2,1,0:T(8,128)(2,1)} %get-tuple-element.7), calls=%async_computation.1 | async-start | bytes 4194304 | tf_op jit(solution)/shard_map/all_to_all | solution.py:476
  57.7 1.0 %copy-start.4 = (bf16[4,256,256]{2,1,0:T(8,128)(2,1)S(1)}, bf16[4,256,256]{2,1,0:T(8,128)(2,1)}, u32[]{:S(2)}) copy-start(bf16[4,256,256]{2,1,0:T(8,128)(2,1)} %constant.60.clone.inner_ref.inner_hbm) | copy-start | bytes 1572868
  58.7 1.0 %copy-start.5 = (bf16[8,256,128]{2,1,0:T(8,128)(2,1)S(1)}, bf16[8,256,128]{2,1,0:T(8,128)(2,1)}, u32[]{:S(2)}) copy-start(bf16[8,256,128]{2,1,0:T(8,128)(2,1)} %constant.61.clone.member_ref) | copy-start | bytes 1572868
  59.7 0.9 %copy-start.6 = (bf16[512,256]{1,0:T(8,128)(2,1)S(1)}, bf16[512,256]{1,0:T(8,128)(2,1)}, u32[]{:S(2)}) copy-start(bf16[512,256]{1,0:T(8,128)(2,1)} %constant.64.clone.grad_ref) | copy-start | bytes 786436
  60.7 0.9 %copy-start.8 = (f32[128,256]{1,0:T(8,128)S(1)}, f32[128,256]{1,0:T(8,128)}, u32[]{:S(2)}) copy-start(f32[128,256]{1,0:T(8,128)} %constant.63.clone.turn_sin_ref) | copy-start | bytes 393220
  61.6 2.2 %copy-start.9 = (bf16[32,256,256]{2,1,0:T(8,128)(2,1)S(1)}, bf16[32,256,256]{2,1,0:T(8,128)(2,1)}, u32[]{:S(2)}) copy-start(bf16[32,256,256]{2,1,0:T(8,128)(2,1)} %get-tuple-element.10.spec_ref) | copy-start | bytes 12582916
  63.8 22.4 %copy-start.1 = (bf16[1,128,4096]{2,1,0:T(8,128)(2,1)S(1)}, bf16[1,128,4096]{2,1,0:T(8,128)(2,1)}, u32[]{:S(2)}) copy-start(bf16[1,128,4096]{2,1,0:T(8,128)(2,1)} %param.15) | copy-start | bytes 3145732
  66.8 5.5 %collective-permute-start.2 = (f32[64,128]{1,0:T(8,128)S(1)}, f32[64,128]{1,0:T(8,128)S(1)}, u32[]{:S(2)}, u32[]{:S(2)}) collective-permute-start(f32[64,128]{1,0:T(8,128)S(1)} %get-tuple-element.12), channel_id=1, source_target_pairs={{0,96},{32,0},{64,32},{96,64},{1,97},{33,1},{65,33},{97,65},{2,98}... | collective-permute-start | bytes 98312 | tf_op jit(solution)/shard_map/ppermute | solution.py:488
  69.1 9.8 %collective-permute-start.1 = (f32[64,128]{1,0:T(8,128)S(1)}, f32[64,128]{1,0:T(8,128)S(1)}, u32[]{:S(2)}, u32[]{:S(2)}) collective-permute-start(f32[64,128]{1,0:T(8,128)S(1)} %get-tuple-element.13), channel_id=1, source_target_pairs={{0,64},{32,96},{64,0},{96,32},{1,65},{33,97},{65,1},{97,33},{2,66}... | collective-permute-start | bytes 98312 | tf_op jit(solution)/shard_map/ppermute | solution.py:488
  69.8 9.0 %collective-permute-start = (f32[64,128]{1,0:T(8,128)S(1)}, f32[64,128]{1,0:T(8,128)S(1)}, u32[]{:S(2)}, u32[]{:S(2)}) collective-permute-start(f32[64,128]{1,0:T(8,128)S(1)} %get-tuple-element.11), channel_id=1, source_target_pairs={{0,32},{32,64},{64,96},{96,0},{1,33},{33,65},{65,97},{97,1},{2,34}... | collective-permute-start | bytes 98312 | tf_op jit(solution)/shard_map/ppermute | solution.py:488

commit v4 on v3

--- a/solution.py
+++ b/solution.py
@@ -32,12 +32,16 @@
     first = np.concatenate([cos_part, -sin_part], 0)
     first[0] = 1.0
     first[OUTER] = (1.0 - 2.0 * (np.arange(OUTER) % 2))[:, None]
-    table_one = np.einsum("rnqs,st->qrtns", first.reshape(64, OUTER, 16, 8), eye)
-    table_one = table_one.reshape(16, 512, 256)
-    table_last = table_one.transpose(0, 2, 1) * (2.0 / POINTS)
+    table_last = np.einsum("rnqs,st->qntrs", first.reshape(64, OUTER, 16, 8), eye)
+    table_last = table_last.reshape(16, 256, 512) * (2.0 / POINTS)
+    table_one = np.einsum("rn,st->rtns", first[:, :, 0], eye).reshape(512, 256)
 
     index = np.arange(INNER)
     cos_two, sin_two = turns(index[:, None] * index[None, :], INNER)
+    table_three = np.block([[cos_two, -sin_two], [sin_two, cos_two]])
+    cos_two, sin_two = turns(
+        64 * index[:, None] * index[None, :] + index * np.arange(OUTER)[:, None, None], POINTS
+    )
     table_two = np.block([[cos_two, sin_two], [-sin_two, cos_two]])
     half = np.arange(64)
     cos_low, sin_low = turns(half[:, None] * index[None, :], INNER)
@@ -52,10 +56,10 @@
     weight[0] = 0.5
     weight[128] = 0.5
     mixed_rows = np.arange(256).reshape(2, 16, 8).transpose(1, 0, 2).reshape(256)
-    table_three = table_two.T[:, mixed_rows]
+    table_three = table_three[:, mixed_rows]
     table_three_zero = (table_two_zero * weight).T[:, mixed_rows]
-    table_two = table_two[mixed_rows]
-    table_two_zero = table_two_zero[mixed_rows]
+    table_two[0] = table_two_zero
+    table_two = table_two[:, mixed_rows]
 
     member = np.zeros((8, 256, LANES))
     for pair in range(8):
@@ -84,7 +88,8 @@
     return dict(
         one=low(table_one),
         last=low(table_last),
-        inner=low(np.stack([table_two, table_two_zero, table_three, table_three_zero])),
+        two=low(table_two),
+        three=low(np.stack([table_three, table_three_zero])),
         member=low(member),
         turn_cos=wide(turn_cos),
         turn_sin=wide(turn_sin),
@@ -101,7 +106,7 @@
     out = []
     for h in range(2):
         held = given[:, 8 * h : 8 * h + 8].reshape(256, lanes).astype(BF16)
-        out.append(dot(one_ref[2 * p + h], held).reshape(64, 8, lanes))
+        out.append(dot(one_ref[...], held).reshape(64, 8, lanes))
     both = jnp.concatenate(out, 1).astype(BF16)
     row = p * 16 if isinstance(p, int) else pl.multiple_of(p * 16, 16)
     u_ref[:, pl.ds(row, 16), :] = both[:OUTER]
@@ -144,123 +149,100 @@
         body(count * m, count, False)
 
 
-OUTER_AT_ONCE = 2
-SLABS_AT_ONCE = 2
-LAST_AT_ONCE = 2
-
-
-def several(count, body, first=0):
-    if count - first <= 1:
-        for g in range(first, count):
-            body(g)
-    else:
-        pl.loop(first, count)(body)
-
-
-def filter_kernel(v_ref, one_ref, inner_ref, spec_ref, u_ref):
+OUTER_ENDS = (8,)
+SLAB_ENDS = (4, 8)
+LAST_ENDS = (4, 7, 8)
+
+
+def groups(ends):
+    return [range(start, end) for start, end in zip((0,) + ends[:-1], ends)]
+
+
+def filter_kernel(v_ref, one_ref, two_ref, spec_ref, u_ref):
     @pl.loop(0, 8)
     def _(p):
         row = pl.multiple_of(p * 16, 16)
         outer_block(v_ref[:, pl.ds(row, 16), :].astype(F32), one_ref, p, u_ref)
 
-    def body(start, count, packed):
-        held = jnp.concatenate([u_ref[start + k] for k in range(count)], 1)
-        spec = dot(inner_ref[int(packed)], held)
-        for k in range(count):
-            spec_ref[start + k] = lane_cut(spec, k, LANES)
-
-    slabs(body, 4)
+    @pl.loop(0, OUTER // 4)
+    def _(m):
+        for k in range(4):
+            spec_ref[4 * m + k] = dot(two_ref[4 * m + k], u_ref[4 * m + k])
 
 
 def main_kernel(
-    v_ref, h_hbm, gain_hbm, one_hbm, inner_hbm, last_hbm, out_hbm, spec_hbm,
-    h_ref, gain_ref, one_ref, inner_ref, last_ref, out_ref, u_ref, back_ref,
-    h_sem, gain_sem, one_sem, inner_sem, last_sem, out_sem, spec_sem,
+    v_hbm, gain_hbm, one_hbm, three_hbm, h_hbm, two_hbm, last_hbm, out_hbm, spec_hbm,
+    v_ref, gain_ref, one_ref, three_ref, h_ref, two_ref, last_ref, out_ref, u_ref, back_ref,
+    v_sem, gain_sem, one_sem, three_sem, h_sem, two_sem, last_sem, out_sem, spec_sem,
 ):
-    def table_copy(hbm, ref, sem, p):
-        cut = pl.ds(2 * p, 2)
-        return pltpu.make_async_copy(hbm.at[cut], ref.at[cut], sem.at[p])
-
-    def slab_copy(source, target, sem, m):
-        cut = pl.ds(4 * m, 4)
+    def part_copy(source, target, sem, m, size):
+        cut = pl.ds(size * m, size)
         return pltpu.make_async_copy(source.at[cut], target.at[cut], sem.at[m])
 
-    inner_copy = pltpu.make_async_copy(inner_hbm, inner_ref, inner_sem)
+    def h_copy(m):
+        return part_copy(h_hbm, h_ref, h_sem, m, 4)
+
+    def two_copy(m):
+        return part_copy(two_hbm, two_ref, two_sem, m, 4)
+
+    def last_copy(p):
+        return part_copy(last_hbm, last_ref, last_sem, p, 2)
+
+    def spec_copy(m):
+        return part_copy(u_ref, spec_hbm, spec_sem, m, 4)
+
+    def v_copy(p):
+        return block_copy(v_hbm, v_ref, v_sem, p, 16)
+
+    one_copy = pltpu.make_async_copy(one_hbm, one_ref, one_sem)
+    three_copy = pltpu.make_async_copy(three_hbm, three_ref, three_sem)
     gain_copy = pltpu.make_async_copy(gain_hbm, gain_ref, gain_sem)
 
-    @pl.loop(0, 8)
-    def _(p):
-        table_copy(one_hbm, one_ref, one_sem, p).start()
-
-    inner_copy.start()
+    one_copy.start()
+    for p in range(8):
+        v_copy(p).start()
+    three_copy.start()
     gain_copy.start()
-
-    @pl.loop(0, 8)
-    def _(p):
-        slab_copy(h_hbm, h_ref, h_sem, p).start()
-
-    @pl.loop(0, 8)
-    def _(p):
-        table_copy(last_hbm, last_ref, last_sem, p).start()
-
-    def outer_group(g):
-        for k in range(OUTER_AT_ONCE):
-            table_copy(one_hbm, one_ref, one_sem, g * OUTER_AT_ONCE + k).wait()
-        for k in range(OUTER_AT_ONCE):
-            p = g * OUTER_AT_ONCE + k
-            row = p * 16 if isinstance(p, int) else pl.multiple_of(p * 16, 16)
-            both = v_ref[:, :, pl.ds(row, 16), :].astype(F32)
+    late = [copy(m) for m in range(8) for copy in (two_copy, h_copy)]
+    late += [last_copy(p) for p in range(8)]
+
+    one_copy.wait()
+    for group in groups(OUTER_ENDS):
+        for p in group:
+            v_copy(p).wait()
+        for p in group:
+            for copy in late[2 * p : 2 * p + 2]:
+                copy.start()
+        for p in group:
+            both = v_ref[:, :, pl.ds(16 * p, 16), :].astype(F32)
             outer_block(jnp.concatenate([both[:, 0], both[:, 1]], 2), one_ref, p, u_ref)
-
-    several(8 // OUTER_AT_ONCE, outer_group)
-    inner_copy.wait()
-
-    def body(start, count, packed):
-        held = jnp.concatenate([u_ref[start + k] for k in range(count)], 1)
-        spec = dot(inner_ref[int(packed)], held)
+    for copy in late[16:]:
+        copy.start()
+    three_copy.wait()
+
+    def slab(j):
+        spec = dot(two_ref[j], u_ref[j])
         real, imag = apart(spec)
-        out_real, out_imag = [], []
-        for k in range(count):
-            hr, hi = apart(h_ref[start + k])
-            low = slice(PAIR * k, PAIR * k + LANES)
-            high = slice(PAIR * k + LANES, PAIR * k + PAIR)
-            pr, pi = times(hr, hi, real[..., low], imag[..., low], False, packed)
-            ar, ai = times(hr, hi, real[..., high], imag[..., high], True, packed)
-            out_real += [pr, ar]
-            out_imag += [pi, ai]
-        product = together(jnp.concatenate(out_real, 2), jnp.concatenate(out_imag, 2))
-        back = dot(inner_ref[2 + int(packed)], product.astype(BF16))
-        for k in range(count):
-            u_ref[start + k] = lane_cut(spec, k, PAIR).astype(BF16)
-            back_ref[start + k] = lane_cut(back, k, PAIR)
-
-    def slab_group(g):
-        for k in range(SLABS_AT_ONCE):
-            slab_copy(h_hbm, h_ref, h_sem, g * SLABS_AT_ONCE + k).wait()
-        for k in range(SLABS_AT_ONCE):
-            m = g * SLABS_AT_ONCE + k
-            if isinstance(m, int) and m == 0:
-                body(0, 1, True)
-                body(1, 3, False)
-            else:
-                body(4 * m, 4, False)
-        for k in range(SLABS_AT_ONCE):
-            slab_copy(u_ref, spec_hbm, spec_sem, g * SLABS_AT_ONCE + k).start()
-
-    slab_group(0)
-    several(8 // SLABS_AT_ONCE, slab_group, 1)
+        hr, hi = apart(h_ref[j])
+        pr, pi = times(hr, hi, real[..., :LANES], imag[..., :LANES], False, j == 0)
+        ar, ai = times(hr, hi, real[..., LANES:], imag[..., LANES:], True, j == 0)
+        product = together(jnp.concatenate([pr, ar], 2), jnp.concatenate([pi, ai], 2))
+        back_ref[j] = dot(three_ref[int(j == 0)], product.astype(BF16))
+        u_ref[j] = spec.astype(BF16)
+
+    for group in groups(SLAB_ENDS):
+        for m in group:
+            two_copy(m).wait()
+            h_copy(m).wait()
+        for m in group:
+            for k in range(4):
+                slab(4 * m + k)
+        for m in group:
+            spec_copy(m).start()
     gain_copy.wait()
 
-    def last_group(g):
-        for k in range(LAST_AT_ONCE):
-            table_copy(last_hbm, last_ref, last_sem, g * LAST_AT_ONCE + k).wait()
-        for k in range(LAST_AT_ONCE):
-            last_block(g * LAST_AT_ONCE + k)
-        for k in range(LAST_AT_ONCE):
-            block_copy(out_ref, out_hbm, out_sem, g * LAST_AT_ONCE + k, 16).start()
-
     def last_block(p):
-        row = p * 16 if isinstance(p, int) else pl.multiple_of(p * 16, 16)
+        row = p * 16
         gain = gain_ref[...]
         given = v_ref[:, :, pl.ds(row, 16), :].astype(F32)
         out = [[], []]
@@ -281,16 +263,20 @@
         for a in range(2):
             out_ref[:, a, pl.ds(row, 16), :] = jnp.concatenate(out[a], 1).astype(BF16)
 
-    several(8 // LAST_AT_ONCE, last_group)
-
-    @pl.loop(0, 8)
-    def _(p):
-        slab_copy(u_ref, spec_hbm, spec_sem, p).wait()
+    for group in groups(LAST_ENDS):
+        for p in group:
+            last_copy(p).wait()
+        for p in group:
+            last_block(p)
+        for p in group:
+            block_copy(out_ref, out_hbm, out_sem, p, 16).start()
+    for p in range(8):
+        spec_copy(p).wait()
         block_copy(out_ref, out_hbm, out_sem, p, 16).wait()
 
 
 def filter_grad_kernel(
-    spec_ref, inner_ref, member_ref, turn_cos_ref, turn_sin_ref, grad_ref, filter_ref, sum_ref
+    spec_ref, three_ref, member_ref, turn_cos_ref, turn_sin_ref, grad_ref, filter_ref, sum_ref
 ):
     sum_ref[...] = jnp.zeros_like(sum_ref)
 
@@ -311,8 +297,8 @@
 
     slabs(body, 4)
     total = jnp.concatenate([sum_ref[0], sum_ref[1]], 1).astype(BF16)
-    back = dot(inner_ref[2], total)
-    back_zero = dot(inner_ref[3], total)
+    back = dot(three_ref[0], total)
+    back_zero = dot(three_ref[1], total)
     packed = lax.broadcasted_iota(jnp.int32, back.shape, 1) < 8
     back = jnp.where(packed, back_zero, back)
     br, bi = back[:INNER], back[INNER:]
@@ -426,7 +412,7 @@
 def filter_spectrum(t, laid):
     return call(
         filter_kernel,
-        (laid, t["one"], t["inner"]),
+        (laid, t["one"], t["two"]),
         jax.ShapeDtypeStruct((OUTER, PAIR, LANES), F32),
         [pltpu.VMEM((OUTER, PAIR, LANES), BF16)],
         4 << 30, 24 << 20,
@@ -434,33 +420,33 @@
 
 
 def main_path(t, moved, kernel_spec, gains):
-    operands = (kernel_spec, gains, t["one"], t["inner"], t["last"])
+    operands = (moved, gains, t["one"], t["three"], kernel_spec, t["two"], t["last"])
     return pl.pallas_call(
         main_kernel,
         out_shape=(MOVED, HELD),
-        in_specs=[IN_VMEM] + [IN_HBM] * len(operands),
+        in_specs=[IN_HBM] * len(operands),
         out_specs=(IN_HBM, IN_HBM),
         scratch_shapes=[pltpu.VMEM(o.shape, o.dtype) for o in operands]
         + [
             pltpu.VMEM(MOVED.shape, BF16),
             pltpu.VMEM(HELD.shape, BF16),
             pltpu.VMEM(HELD.shape, F32),
-            DMA((8,)), DMA, DMA((8,)), DMA, DMA((8,)), DMA((8,)), DMA((8,)),
+            DMA((8,)), DMA, DMA, DMA, DMA((8,)), DMA((8,)), DMA((8,)), DMA((8,)), DMA((8,)),
         ],
-        compiler_params=pltpu.CompilerParams(vmem_limit_bytes=59 << 20),
+        compiler_params=pltpu.CompilerParams(vmem_limit_bytes=60 << 20),
         cost_estimate=pl.CostEstimate(
             flops=6 << 30, bytes_accessed=20 << 20, transcendentals=0
         ),
-    )(moved, *operands)
+    )(*operands)
 
 
 def filter_gradient(t, spec):
     return call(
         filter_grad_kernel,
-        (spec, t["inner"], t["member"], t["turn_cos"], t["turn_sin"], t["grad"]),
+        (spec, t["three"], t["member"], t["turn_cos"], t["turn_sin"], t["grad"]),
         jax.ShapeDtypeStruct((PAIR, LANES), F32),
         [pltpu.VMEM((2, PAIR, LANES), F32)],
-        2 << 30, 16 << 20,
+        2 << 30, 60 << 20,
     )
 
 

time: 89 us -> 88.6 us (level)
  the two profiles are of different devices: /device:TPU:0 before, /device:TPU:38 now
where the time goes in v4:
time: 88.6 us; the launch traced here: 88.1 us
  waiting for transfers between devices  34.3 us (39%)
  Pallas kernels  25.6 us (29%)
  starting transfers between devices  19.9 us (22%)
  local copies, waits for them, and re-layouts  6.25 us (7%)
    ppermute x3, waiting for transfers between devices, sum_over_sequences(): lax.ppermute(share((place + hop) % count), 'dp', [(i, (i + hop) % count)...  18.8 us
    all_to_all x2, starting transfers between devices, exchange(): lax.all_to_all(blocks, 'ctx', split_axis=0, concat_axis=0, tiled=True)  16.7 us
    all_to_all x2, waiting for transfers between devices, exchange(): lax.all_to_all(blocks, 'ctx', split_axis=0, concat_axis=0, tiled=True)  15.6 us
    pallas_call x2, Pallas kernels, call(): pl.pallas_call(kernel, out_shape=outs, in_specs=[space] * len(operands),...  10.9 us
    pallas_call x1, Pallas kernels, main_path(): pl.pallas_call(main_kernel, out_shape=(MOVED, HELD), in_specs=[IN_HBM] *...  10.3 us
    unnamed x12, local copies, waits for them, and re-layouts  4.16 us
    ppermute x3, starting transfers between devices, sum_over_sequences(): lax.ppermute(share((place + hop) % count), 'dp', [(i, (i + hop) % count)...  3.2 us
    pallas_call x1, Pallas kernels, gather(): pl.pallas_call(gather_kernel, out_shape=MOVED, in_specs=[IN_HBM] * 3, out...  2.9 us
  transfers between devices with their start and end apart: 5, of which 3 were waited for; matrix products, arithmetic and copies ran while one was open for 4% of the time, Pallas kernels for 12%

profile of v4, /device:TPU:38, one launch (start us, length us, event | category | flops | bytes accessed | tf_op | source)
XLA Modules:
  0.0 88.1 jit_solution(17899756606338903390)
XLA Ops:
  0.6 0.0 copy-start
  0.6 2.9 %shard_map.157 = bf16[32,2,128,128]{3,2,1,0:T(8,128)(2,1)} custom-call(bf16[128,4096]{1,0:T(8,128)(2,1)} %bitcast.27, bf16[128,4096]{1,0:T(8,128)(2,1)} %bitcast.28, bf16[128,4096]{1,0:T(8,128)(2,1)} %bitcast.24), custom_call_target="tpu_custom_call" | custom-call | tf_op jit(solution)/shard_map/pallas_call | solution.py:376
  3.6 0.0 copy-start.5
  3.6 9.0 %all-to-all-start = ((bf16[32,2,128,128]{3,2,1,0:T(8,128)(2,1)}), bf16[32,2,128,128]{3,2,1,0:T(8,128)(2,1)}, u32[]{:S(2)}, u32[]{:S(2)}) async-start(bf16[32,2,128,128]{3,2,1,0:T(8,128)(2,1)} %shard_map.157), calls=%async_computation | async-start | bytes 4194304 | tf_op jit(solution)/shard_map/all_to_all | solution.py:462
  12.6 0.0 copy-done
  12.6 0.0 copy-done.5
  12.6 0.0 copy-start.3
  12.6 0.5 fusion
  13.1 0.7 copy.17
  13.8 0.0 copy-done.3
  13.8 0.0 copy-start.2
  13.8 2.2 %copy-done.2 = bf16[32,256,256]{2,1,0:T(8,128)(2,1)S(1)} copy-done((bf16[32,256,256]{2,1,0:T(8,128)(2,1)S(1)}, bf16[32,256,256]{2,1,0:T(8,128)(2,1)}, u32[]{:S(2)}) %copy-start.2) | copy-done | bytes 4194328
  16.0 4.7 %shard_map.158.h_hbm = f32[32,256,128]{2,1,0:T(8,128)S(1)} custom-call(bf16[32,128,128]{2,1,0:T(8,128)(2,1)S(1)} %bitcast.26, bf16[512,256]{1,0:T(8,128)(2,1)S(1)} %copy-done.3, bf16[32,256,256]{2,1,0:T(8,128)(2,1)S(1)} %copy-done.2), custom_call_target="tpu_custom_call" | custom-call | flops 4294967296 | bytes 16777216 | tf_op jit(solution)/shard_map/pallas_call | solution.py:401
  20.7 0.0 copy-start.4
  20.7 1.9 %copy-done.4 = f32[32,256,128]{2,1,0:T(8,128)} copy-done((f32[32,256,128]{2,1,0:T(8,128)}, f32[32,256,128]{2,1,0:T(8,128)S(1)}, u32[]{:S(2)}) %copy-start.4) | copy-done | bytes 4194328
  22.6 15.6 %all-to-all-done.v_hbm = bf16[32,2,128,128]{3,2,1,0:T(8,128)(2,1)} async-done(((bf16[32,2,128,128]{3,2,1,0:T(8,128)(2,1)}), bf16[32,2,128,128]{3,2,1,0:T(8,128)(2,1)}, u32[]{:S(2)}, u32[]{:S(2)}) %all-to-all-start) | async-done | bytes 2097184 | tf_op jit(solution)/shard_map/all_to_all | solution.py:462
  38.2 10.3 %shard_map.159 = (bf16[32,2,128,128]{3,2,1,0:T(8,128)(2,1)}, bf16[32,256,256]{2,1,0:T(8,128)(2,1)}) custom-call(bf16[32,2,128,128]{3,2,1,0:T(8,128)(2,1)} %all-to-all-done.v_hbm, f32[1,128]{1,0:T(1,128)} %bitcast.33, bf16[512,256]{1,0:T(8,128)(2,1)} %constant.60.clone.one_ref.one_hbm, bf16[2,256,256]{2,1,0:T(8,128)(2,1)} %constant.63.clone.three_hbm.three_ref, ...), custom_call_target="tpu_custom_call" | custom-call | flops 6442450944 | bytes 20971520 | tf_op jit(solution)/shard_map/pallas_call | solution.py:424
  48.5 7.7 %all-to-all-start.1 = ((bf16[32,2,128,128]{3,2,1,0:T(8,128)(2,1)}), bf16[32,2,128,128]{3,2,1,0:T(8,128)(2,1)S(1)}, u32[]{:S(2)}, u32[]{:S(2)}) async-start(bf16[32,2,128,128]{3,2,1,0:T(8,128)(2,1)} %get-tuple-element.7), calls=%async_computation.1 | async-start | bytes 4194304 | tf_op jit(solution)/shard_map/all_to_all | solution.py:462
  56.2 0.0 copy-start.1
  56.2 6.2 %shard_map.161 = f32[256,128]{1,0:T(8,128)} custom-call(bf16[32,256,256]{2,1,0:T(8,128)(2,1)} %get-tuple-element.10.spec_ref, bf16[2,256,256]{2,1,0:T(8,128)(2,1)} %constant.63.clone.three_hbm.three_ref, bf16[8,256,128]{2,1,0:T(8,128)(2,1)} %constant.64.clone.member_ref, f32[128,256]{1,0:T(8,128)} %constant.65.clone.turn_cos_ref, ...), custom_call_target="tpu_custom_call" | custom-call | flops 2147483648 | bytes 16777216 | tf_op jit(solution)/shard_map/pallas_call | solution.py:401
  62.4 0.8 dynamic-slice_bitcast_fusion.2
  63.2 2.0 %collective-permute-start.2 = (f32[64,128]{1,0:T(8,128)S(1)}, f32[64,128]{1,0:T(8,128)S(1)}, u32[]{:S(2)}, u32[]{:S(2)}) collective-permute-start(f32[64,128]{1,0:T(8,128)S(1)} %get-tuple-element.12), channel_id=1, source_target_pairs={{0,96},{32,0},{64,32},{96,64},{1,97},{33,1},{65,33},{97,65},{2,98}... | collective-permute-start | bytes 98312 | tf_op jit(solution)/shard_map/ppermute | solution.py:474
  65.3 1.0 %collective-permute-start.1 = (f32[64,128]{1,0:T(8,128)S(1)}, f32[64,128]{1,0:T(8,128)S(1)}, u32[]{:S(2)}, u32[]{:S(2)}) collective-permute-start(f32[64,128]{1,0:T(8,128)S(1)} %get-tuple-element.13), channel_id=1, source_target_pairs={{0,64},{32,96},{64,0},{96,32},{1,65},{33,97},{65,1},{97,33},{2,66}... | collective-permute-start | bytes 98312 | tf_op jit(solution)/shard_map/ppermute | solution.py:474
  66.3 0.2 collective-permute-start
  66.4 15.1 %collective-permute-done.2 = f32[64,128]{1,0:T(8,128)S(1)} collective-permute-done((f32[64,128]{1,0:T(8,128)S(1)}, f32[64,128]{1,0:T(8,128)S(1)}, u32[]{:S(2)}, u32[]{:S(2)}) %collective-permute-start.2) | collective-permute-done | bytes 32800 | tf_op jit(solution)/shard_map/ppermute | solution.py:474
  81.5 3.7 %collective-permute-done.1 = f32[64,128]{1,0:T(8,128)S(1)} collective-permute-done((f32[64,128]{1,0:T(8,128)S(1)}, f32[64,128]{1,0:T(8,128)S(1)}, u32[]{:S(2)}, u32[]{:S(2)}) %collective-permute-start.1) | collective-permute-done | bytes 32800 | tf_op jit(solution)/shard_map/ppermute | solution.py:474
  85.2 0.0 collective-permute-done
  85.2 0.8 fusion.2
  86.0 0.6 reshape.17
  86.6 0.0 all-to-all-done.1.back_ref
  86.6 0.0 copy-done.1
  86.6 1.4 %shard_map.160 = (bf16[128,4096]{1,0:T(8,128)(2,1)}, bf16[128,4096]{1,0:T(8,128)(2,1)}) custom-call(bf16[32,2,128,128]{3,2,1,0:T(8,128)(2,1)S(1)} %all-to-all-done.1.back_ref, bf16[128,4096]{1,0:T(8,128)(2,1)S(1)} %bitcast.25), custom_call_target="tpu_custom_call" | custom-call | tf_op jit(solution)/shard_map/pallas_call | solution.py:389
Async XLA Ops:
  0.6 12.0 %copy-start = (bf16[8,4096]{1,0:T(8,128)(2,1)S(1)}, bf16[8,4096]{1,0:T(8,128)(2,1)}, u32[]{:S(2)}) copy-start(bf16[8,4096]{1,0:T(8,128)(2,1)} %param.17) | copy-start | bytes 196612
  3.6 9.1 %copy-start.5 = (bf16[8,128]{1,0:T(8,128)(2,1)S(1)}, bf16[8,128]{1,0:T(8,128)(2,1)}, u32[]{:S(2)}) copy-start(bf16[8,128]{1,0:T(8,128)(2,1)} %constant.68.clone) | copy-start | bytes 6148
  3.6 34.6 %all-to-all-start = ((bf16[32,2,128,128]{3,2,1,0:T(8,128)(2,1)}), bf16[32,2,128,128]{3,2,1,0:T(8,128)(2,1)}, u32[]{:S(2)}, u32[]{:S(2)}) async-start(bf16[32,2,128,128]{3,2,1,0:T(8,128)(2,1)} %shard_map.157), calls=%async_computation | async-start | bytes 4194304 | tf_op jit(solution)/shard_map/all_to_all | solution.py:462
  12.6 1.2 %copy-start.3 = (bf16[512,256]{1,0:T(8,128)(2,1)S(1)}, bf16[512,256]{1,0:T(8,128)(2,1)}, u32[]{:S(2)}) copy-start(bf16[512,256]{1,0:T(8,128)(2,1)} %constant.60.clone.one_ref.one_hbm) | copy-start | bytes 786436
  13.8 2.2 %copy-start.2 = (bf16[32,256,256]{2,1,0:T(8,128)(2,1)S(1)}, bf16[32,256,256]{2,1,0:T(8,128)(2,1)}, u32[]{:S(2)}) copy-start(bf16[32,256,256]{2,1,0:T(8,128)(2,1)} %constant.62.clone.two_ref.two_hbm) | copy-start | bytes 12582916
  20.7 2.0 %copy-start.4 = (f32[32,256,128]{2,1,0:T(8,128)}, f32[32,256,128]{2,1,0:T(8,128)S(1)}, u32[]{:S(2)}) copy-start(f32[32,256,128]{2,1,0:T(8,128)S(1)} %shard_map.158.h_hbm) | copy-start | bytes 12582916
  48.5 38.1 %all-to-all-start.1 = ((bf16[32,2,128,128]{3,2,1,0:T(8,128)(2,1)}), bf16[32,2,128,128]{3,2,1,0:T(8,128)(2,1)S(1)}, u32[]{:S(2)}, u32[]{:S(2)}) async-start(bf16[32,2,128,128]{3,2,1,0:T(8,128)(2,1)} %get-tuple-element.7), calls=%async_computation.1 | async-start | bytes 4194304 | tf_op jit(solution)/shard_map/all_to_all | solution.py:462
  56.2 30.4 %copy-start.1 = (bf16[1,128,4096]{2,1,0:T(8,128)(2,1)S(1)}, bf16[1,128,4096]{2,1,0:T(8,128)(2,1)}, u32[]{:S(2)}) copy-start(bf16[1,128,4096]{2,1,0:T(8,128)(2,1)} %param.16) | copy-start | bytes 3145732
  63.2 18.3 %collective-permute-start.2 = (f32[64,128]{1,0:T(8,128)S(1)}, f32[64,128]{1,0:T(8,128)S(1)}, u32[]{:S(2)}, u32[]{:S(2)}) collective-permute-start(f32[64,128]{1,0:T(8,128)S(1)} %get-tuple-element.12), channel_id=1, source_target_pairs={{0,96},{32,0},{64,32},{96,64},{1,97},{33,1},{65,33},{97,65},{2,98}... | collective-permute-start | bytes 98312 | tf_op jit(solution)/shard_map/ppermute | solution.py:474
  65.3 20.0 %collective-permute-start.1 = (f32[64,128]{1,0:T(8,128)S(1)}, f32[64,128]{1,0:T(8,128)S(1)}, u32[]{:S(2)}, u32[]{:S(2)}) collective-permute-start(f32[64,128]{1,0:T(8,128)S(1)} %get-tuple-element.13), channel_id=1, source_target_pairs={{0,64},{32,96},{64,0},{96,32},{1,65},{33,97},{65,1},{97,33},{2,66}... | collective-permute-start | bytes 98312 | tf_op jit(solution)/shard_map/ppermute | solution.py:474
  66.3 18.9 %collective-permute-start = (f32[64,128]{1,0:T(8,128)S(1)}, f32[64,128]{1,0:T(8,128)S(1)}, u32[]{:S(2)}, u32[]{:S(2)}) collective-permute-start(f32[64,128]{1,0:T(8,128)S(1)} %get-tuple-element.11), channel_id=1, source_target_pairs={{0,32},{32,64},{64,96},{96,0},{1,33},{33,65},{65,97},{97,1},{2,34}... | collective-permute-start | bytes 98312 | tf_op jit(solution)/shard_map/ppermute | solution.py:474

commit v5 on v4

--- a/solution.py
+++ b/solution.py
@@ -76,7 +76,7 @@
     parts = np.stack([last_cos, last_sin])
     same = group_lane[:, None] == np.arange(8)[None, :]
     table_grad = np.einsum("pln,lg->plgn", parts, same)
-    table_grad = table_grad.reshape(2, 256, 8, 4, 8).transpose(0, 1, 3, 2, 4)
+    table_grad = table_grad.reshape(2, 256, 8, 4, 8).transpose(0, 1, 3, 4, 2)
     table_grad = table_grad.reshape(512, 256) * (2.0 * grad_scale)
 
     def low(values):
@@ -150,8 +150,8 @@
 
 
 OUTER_ENDS = (8,)
-SLAB_ENDS = (4, 8)
-LAST_ENDS = (4, 7, 8)
+SLAB_ENDS = (16,32)
+LAST_ENDS = (8,)
 
 
 def groups(ends):
@@ -175,49 +175,49 @@
     v_ref, gain_ref, one_ref, three_ref, h_ref, two_ref, last_ref, out_ref, u_ref, back_ref,
     v_sem, gain_sem, one_sem, three_sem, h_sem, two_sem, last_sem, out_sem, spec_sem,
 ):
-    def part_copy(source, target, sem, m, size):
-        cut = pl.ds(size * m, size)
-        return pltpu.make_async_copy(source.at[cut], target.at[cut], sem.at[m])
-
-    def h_copy(m):
-        return part_copy(h_hbm, h_ref, h_sem, m, 4)
-
-    def two_copy(m):
-        return part_copy(two_hbm, two_ref, two_sem, m, 4)
-
-    def last_copy(p):
-        return part_copy(last_hbm, last_ref, last_sem, p, 2)
-
-    def spec_copy(m):
-        return part_copy(u_ref, spec_hbm, spec_sem, m, 4)
-
-    def v_copy(p):
-        return block_copy(v_hbm, v_ref, v_sem, p, 16)
-
+    def copies(ends, size, *arrays):
+        made = []
+        for g, group in enumerate(groups(ends)):
+            cut = pl.ds(size * group[0], size * len(group))
+            made.append(
+                [pltpu.make_async_copy(a.at[cut], b.at[cut], sem.at[g]) for a, b, sem in arrays]
+            )
+        return made
+
+    def row_copies(ends, source, target, sem):
+        made = []
+        for g, group in enumerate(groups(ends)):
+            cut = pl.ds(16 * group[0], 16 * len(group))
+            made.append(
+                pltpu.make_async_copy(source.at[:, :, cut], target.at[:, :, cut], sem.at[g])
+            )
+        return made
+
+    v_copies = row_copies(OUTER_ENDS, v_hbm, v_ref, v_sem)
+    slab_copies = copies(SLAB_ENDS, 1, (two_hbm, two_ref, two_sem), (h_hbm, h_ref, h_sem))
+    spec_copies = copies(SLAB_ENDS, 1, (u_ref, spec_hbm, spec_sem))
+    last_copies = copies(LAST_ENDS, 2, (last_hbm, last_ref, last_sem))
+    out_copies = row_copies(LAST_ENDS, out_ref, out_hbm, out_sem)
     one_copy = pltpu.make_async_copy(one_hbm, one_ref, one_sem)
     three_copy = pltpu.make_async_copy(three_hbm, three_ref, three_sem)
     gain_copy = pltpu.make_async_copy(gain_hbm, gain_ref, gain_sem)
 
+    v_copies[0].start()
     one_copy.start()
-    for p in range(8):
-        v_copy(p).start()
+    for copy in v_copies[1:]:
+        copy.start()
     three_copy.start()
     gain_copy.start()
-    late = [copy(m) for m in range(8) for copy in (two_copy, h_copy)]
-    late += [last_copy(p) for p in range(8)]
 
     one_copy.wait()
-    for group in groups(OUTER_ENDS):
-        for p in group:
-            v_copy(p).wait()
-        for p in group:
-            for copy in late[2 * p : 2 * p + 2]:
+    for g, group in enumerate(groups(OUTER_ENDS)):
+        v_copies[g].wait()
+        if g == len(OUTER_ENDS) - 1:
+            for copy in sum(slab_copies + last_copies, []):
                 copy.start()
         for p in group:
             both = v_ref[:, :, pl.ds(16 * p, 16), :].astype(F32)
             outer_block(jnp.concatenate([both[:, 0], both[:, 1]], 2), one_ref, p, u_ref)
-    for copy in late[16:]:
-        copy.start()
     three_copy.wait()
 
     def slab(j):
@@ -230,15 +230,12 @@
         back_ref[j] = dot(three_ref[int(j == 0)], product.astype(BF16))
         u_ref[j] = spec.astype(BF16)
 
-    for group in groups(SLAB_ENDS):
-        for m in group:
-            two_copy(m).wait()
-            h_copy(m).wait()
-        for m in group:
-            for k in range(4):
-                slab(4 * m + k)
-        for m in group:
-            spec_copy(m).start()
+    for g, group in enumerate(groups(SLAB_ENDS)):
+        for copy in slab_copies[g]:
+            copy.wait()
+        for j in group:
+            slab(j)
+        spec_copies[g][0].start()
     gain_copy.wait()
 
     def last_block(p):
@@ -263,16 +260,14 @@
         for a in range(2):
             out_ref[:, a, pl.ds(row, 16), :] = jnp.concatenate(out[a], 1).astype(BF16)
 
-    for group in groups(LAST_ENDS):
-        for p in group:
-            last_copy(p).wait()
+    for copy in sum(last_copies, []):
+        copy.wait()
+    for g, group in enumerate(groups(LAST_ENDS)):
         for p in group:
             last_block(p)
-        for p in group:
-            block_copy(out_ref, out_hbm, out_sem, p, 16).start()
-    for p in range(8):
-        spec_copy(p).wait()
-        block_copy(out_ref, out_hbm, out_sem, p, 16).wait()
+        out_copies[g].start()
+    for copy in sum(spec_copies, []) + out_copies:
+        copy.wait()
 
 
 def filter_grad_kernel(
@@ -304,7 +299,10 @@
     br, bi = back[:INNER], back[INNER:]
     c, s = turn_cos_ref[...], turn_sin_ref[...]
     turned = jnp.concatenate([br * c - bi * s, br * s + bi * c], 1).astype(BF16)
-    filter_ref[...] = dot(turned, grad_ref[...]).T
+    rows = dot(turned, grad_ref[...]).T
+    for n in range(OUTER):
+        lanes = slice(n % 8 * INNER, n % 8 * INNER + INNER)
+        filter_ref[n // 8, :, lanes] = rows[8 * n : 8 * n + 8]
 
 
 def row_copy(source, target, sem, i, rows):
@@ -431,7 +429,9 @@
             pltpu.VMEM(MOVED.shape, BF16),
             pltpu.VMEM(HELD.shape, BF16),
             pltpu.VMEM(HELD.shape, F32),
-            DMA((8,)), DMA, DMA, DMA, DMA((8,)), DMA((8,)), DMA((8,)), DMA((8,)), DMA((8,)),
+            DMA((len(OUTER_ENDS),)), DMA, DMA, DMA, DMA((len(SLAB_ENDS),)),
+            DMA((len(SLAB_ENDS),)), DMA((len(LAST_ENDS),)), DMA((len(LAST_ENDS),)),
+            DMA((len(SLAB_ENDS),)),
         ],
         compiler_params=pltpu.CompilerParams(vmem_limit_bytes=60 << 20),
         cost_estimate=pl.CostEstimate(
@@ -444,7 +444,7 @@
     return call(
         filter_grad_kernel,
         (spec, t["three"], t["member"], t["turn_cos"], t["turn_sin"], t["grad"]),
-        jax.ShapeDtypeStruct((PAIR, LANES), F32),
+        jax.ShapeDtypeStruct((4, 8, 1024), F32),
         [pltpu.VMEM((2, PAIR, LANES), F32)],
         2 << 30, 60 << 20,
     )
@@ -462,19 +462,19 @@
     return lax.all_to_all(blocks, "ctx", split_axis=0, concat_axis=0, tiled=True)
 
 
-def sum_over_sequences(parts):
+def shares(parts):
     count = lax.axis_size("dp")
     place = lax.axis_index("dp")
 
     def share(owner):
         return lax.dynamic_index_in_dim(parts, owner, 0, keepdims=False)
 
-    total = share(place)
-    for hop in range(1, count):
-        total = total + lax.ppermute(
+    return [share(place)] + [
+        lax.ppermute(
             share((place + hop) % count), "dp", [(i, (i + hop) % count) for i in range(count)]
         )
-    return total
+        for hop in range(1, count)
+    ]
 
 
 def unit(moved_input, moved_grad, filters, gains):
@@ -493,9 +493,10 @@
     out, spec = main_path(t, moved, kernel_spec, direct_scale[None, :])
     back = exchange(out)
     filter_part = filter_gradient(t, spec)
-    filter_grad = sum_over_sequences(filter_part.reshape(replica_count, -1, LANES))
-    filter_grad = filter_grad.reshape(filters.shape[0], -1)
+    terms = shares(filter_part)
     gate_grad, input_grad = spread(back, cotangent[0])
+    gate_grad, input_grad, terms = lax.optimization_barrier((gate_grad, input_grad, terms))
+    filter_grad = sum(terms[1:], terms[0])
     return gate_grad[None], input_grad[None], filter_grad
 
 

time: 88.6 us -> 86.7 us (0.979)
  the two profiles are of different devices: /device:TPU:38 before, /device:TPU:0 now
where the time goes in v5:
time: 86.7 us; the launch traced here: 86.3 us
  waiting for transfers between devices  33.9 us (39%)
  Pallas kernels  24.7 us (28%)
  starting transfers between devices  20.1 us (23%)
  local copies, waits for them, and re-layouts  5.64 us (7%)
    all_to_all x2, waiting for transfers between devices, exchange(): lax.all_to_all(blocks, 'ctx', split_axis=0, concat_axis=0, tiled=True)  33.9 us
    all_to_all x2, starting transfers between devices, exchange(): lax.all_to_all(blocks, 'ctx', split_axis=0, concat_axis=0, tiled=True)  14.2 us
    pallas_call x2, Pallas kernels, call(): pl.pallas_call(kernel, out_shape=outs, in_specs=[space] * len(operands),...  11 us
    pallas_call x1, Pallas kernels, main_path(): pl.pallas_call(main_kernel, out_shape=(MOVED, HELD), in_specs=[IN_HBM] *...  9.42 us
    ppermute x3, starting transfers between devices, shares(): lax.ppermute(share((place + hop) % count), 'dp', [(i, (i + hop) % count)...  5.93 us
    unnamed x12, local copies, waits for them, and re-layouts  4.16 us
    pallas_call x1, Pallas kernels, gather(): pl.pallas_call(gather_kernel, out_shape=MOVED, in_specs=[IN_HBM] * 3, out...  2.9 us
  transfers between devices with their start and end apart: 5, of which 2 were waited for; matrix products, arithmetic and copies ran while one was open for 2% of the time, Pallas kernels for 14%

profile of v5, /device:TPU:0, one launch (start us, length us, event | category | flops | bytes accessed | tf_op | source)
XLA Modules:
  0.0 86.3 jit_solution(16446696444820981055)
XLA Ops:
  0.6 0.0 copy-start
  0.6 2.9 %shard_map.157 = bf16[32,2,128,128]{3,2,1,0:T(8,128)(2,1)} custom-call(bf16[128,4096]{1,0:T(8,128)(2,1)} %bitcast.22, bf16[128,4096]{1,0:T(8,128)(2,1)} %bitcast.23, bf16[128,4096]{1,0:T(8,128)(2,1)} %bitcast.19), custom_call_target="tpu_custom_call" | custom-call | tf_op jit(solution)/shard_map/pallas_call | solution.py:374
  3.6 0.0 copy-start.5
  3.6 9.4 %all-to-all-start = ((bf16[32,2,128,128]{3,2,1,0:T(8,128)(2,1)}), bf16[32,2,128,128]{3,2,1,0:T(8,128)(2,1)}, u32[]{:S(2)}, u32[]{:S(2)}) async-start(bf16[32,2,128,128]{3,2,1,0:T(8,128)(2,1)} %shard_map.157), calls=%async_computation | async-start | bytes 4194304 | tf_op jit(solution)/shard_map/all_to_all | solution.py:462
  13.0 0.0 copy-done
  13.0 0.0 copy-done.5
  13.0 0.0 copy-start.3
  13.0 0.5 fusion
  13.5 0.7 copy.17
  14.1 0.0 copy-done.3
  14.2 0.0 copy-start.2
  14.2 2.2 %copy-done.2 = bf16[32,256,256]{2,1,0:T(8,128)(2,1)S(1)} copy-done((bf16[32,256,256]{2,1,0:T(8,128)(2,1)S(1)}, bf16[32,256,256]{2,1,0:T(8,128)(2,1)}, u32[]{:S(2)}) %copy-start.2) | copy-done | bytes 4194328
  16.3 4.7 %shard_map.158.h_hbm = f32[32,256,128]{2,1,0:T(8,128)S(1)} custom-call(bf16[32,128,128]{2,1,0:T(8,128)(2,1)S(1)} %bitcast.21, bf16[512,256]{1,0:T(8,128)(2,1)S(1)} %copy-done.3, bf16[32,256,256]{2,1,0:T(8,128)(2,1)S(1)} %copy-done.2), custom_call_target="tpu_custom_call" | custom-call | flops 4294967296 | bytes 16777216 | tf_op jit(solution)/shard_map/pallas_call | solution.py:399
  21.1 0.0 copy-start.4
  21.1 1.9 %copy-done.4 = f32[32,256,128]{2,1,0:T(8,128)} copy-done((f32[32,256,128]{2,1,0:T(8,128)}, f32[32,256,128]{2,1,0:T(8,128)S(1)}, u32[]{:S(2)}) %copy-start.4) | copy-done | bytes 4194328
  23.0 18.3 %all-to-all-done.v_hbm = bf16[32,2,128,128]{3,2,1,0:T(8,128)(2,1)} async-done(((bf16[32,2,128,128]{3,2,1,0:T(8,128)(2,1)}), bf16[32,2,128,128]{3,2,1,0:T(8,128)(2,1)}, u32[]{:S(2)}, u32[]{:S(2)}) %all-to-all-start) | async-done | bytes 2097184 | tf_op jit(solution)/shard_map/all_to_all | solution.py:462
  41.4 9.4 %shard_map.159 = (bf16[32,2,128,128]{3,2,1,0:T(8,128)(2,1)}, bf16[32,256,256]{2,1,0:T(8,128)(2,1)}) custom-call(bf16[32,2,128,128]{3,2,1,0:T(8,128)(2,1)} %all-to-all-done.v_hbm, f32[1,128]{1,0:T(1,128)} %bitcast.26, bf16[512,256]{1,0:T(8,128)(2,1)} %constant.60.clone.one_ref.one_hbm, bf16[2,256,256]{2,1,0:T(8,128)(2,1)} %constant.63.clone.three_hbm.three_ref, ...), custom_call_target="tpu_custom_call" | custom-call | flops 6442450944 | bytes 20971520 | tf_op jit(solution)/shard_map/pallas_call | solution.py:422
  50.8 4.8 %all-to-all-start.1 = ((bf16[32,2,128,128]{3,2,1,0:T(8,128)(2,1)}), bf16[32,2,128,128]{3,2,1,0:T(8,128)(2,1)S(1)}, u32[]{:S(2)}, u32[]{:S(2)}) async-start(bf16[32,2,128,128]{3,2,1,0:T(8,128)(2,1)} %get-tuple-element.13), calls=%async_computation.1 | async-start | bytes 4194304 | tf_op jit(solution)/shard_map/all_to_all | solution.py:462
  55.6 0.0 copy-start.1
  55.6 6.2 %shard_map.161 = f32[4,8,1024]{2,1,0:T(8,128)} custom-call(bf16[32,256,256]{2,1,0:T(8,128)(2,1)} %get-tuple-element.16.spec_ref, bf16[2,256,256]{2,1,0:T(8,128)(2,1)} %constant.63.clone.three_hbm.three_ref, bf16[8,256,128]{2,1,0:T(8,128)(2,1)} %constant.64.clone.member_ref, f32[128,256]{1,0:T(8,128)} %constant.65.clone.turn_cos_ref, ...), custom_call_target="tpu_custom_call" | custom-call | flops 2147483648 | bytes 16777216 | tf_op jit(solution)/shard_map/pallas_call | solution.py:399
  61.9 0.8 dynamic-slice_bitcast_fusion
  62.7 0.1 collective-permute-start
  62.8 3.0 %collective-permute-start.1 = (f32[8,1024]{1,0:T(8,128)S(1)}, f32[8,1024]{1,0:T(8,128)S(1)}, u32[]{:S(2)}, u32[]{:S(2)}) collective-permute-start(f32[8,1024]{1,0:T(8,128)S(1)} %get-tuple-element.24), channel_id=1, source_target_pairs={{0,64},{32,96},{64,0},{96,32},{1,65},{33,97},{65,1},{97,33},{2,66}... | collective-permute-start | bytes 98312 | tf_op jit(solution)/shard_map/ppermute | solution.py:473
  65.8 2.9 %collective-permute-start.2 = (f32[8,1024]{1,0:T(8,128)S(1)}, f32[8,1024]{1,0:T(8,128)S(1)}, u32[]{:S(2)}, u32[]{:S(2)}) collective-permute-start(f32[8,1024]{1,0:T(8,128)S(1)} %get-tuple-element.23), channel_id=1, source_target_pairs={{0,96},{32,0},{64,32},{96,64},{1,97},{33,1},{65,33},{97,65},{2,98}... | collective-permute-start | bytes 98312 | tf_op jit(solution)/shard_map/ppermute | solution.py:473
  68.6 15.6 %all-to-all-done.1.back_ref = bf16[32,2,128,128]{3,2,1,0:T(8,128)(2,1)S(1)} async-done(((bf16[32,2,128,128]{3,2,1,0:T(8,128)(2,1)}), bf16[32,2,128,128]{3,2,1,0:T(8,128)(2,1)S(1)}, u32[]{:S(2)}, u32[]{:S(2)}) %all-to-all-start.1) | async-done | bytes 2097184 | tf_op jit(solution)/shard_map/all_to_all | solution.py:462
  84.2 0.0 copy-done.1
  84.2 1.4 %shard_map.160 = (bf16[128,4096]{1,0:T(8,128)(2,1)}, bf16[128,4096]{1,0:T(8,128)(2,1)}) custom-call(bf16[32,2,128,128]{3,2,1,0:T(8,128)(2,1)S(1)} %all-to-all-done.1.back_ref, bf16[128,4096]{1,0:T(8,128)(2,1)S(1)} %bitcast.20), custom_call_target="tpu_custom_call" | custom-call | tf_op jit(solution)/shard_map/pallas_call | solution.py:387
  85.6 0.0 collective-permute-done
  85.7 0.0 collective-permute-done.1
  85.7 0.0 collective-permute-done.2
  85.7 0.6 add_add_fusion
Async XLA Ops:
  0.6 12.3 %copy-start = (bf16[8,4096]{1,0:T(8,128)(2,1)S(1)}, bf16[8,4096]{1,0:T(8,128)(2,1)}, u32[]{:S(2)}) copy-start(bf16[8,4096]{1,0:T(8,128)(2,1)} %param.17) | copy-start | bytes 196612
  3.6 9.4 %copy-start.5 = (bf16[8,128]{1,0:T(8,128)(2,1)S(1)}, bf16[8,128]{1,0:T(8,128)(2,1)}, u32[]{:S(2)}) copy-start(bf16[8,128]{1,0:T(8,128)(2,1)} %constant.68.clone) | copy-start | bytes 6148
  3.6 37.8 %all-to-all-start = ((bf16[32,2,128,128]{3,2,1,0:T(8,128)(2,1)}), bf16[32,2,128,128]{3,2,1,0:T(8,128)(2,1)}, u32[]{:S(2)}, u32[]{:S(2)}) async-start(bf16[32,2,128,128]{3,2,1,0:T(8,128)(2,1)} %shard_map.157), calls=%async_computation | async-start | bytes 4194304 | tf_op jit(solution)/shard_map/all_to_all | solution.py:462
  13.0 1.2 %copy-start.3 = (bf16[512,256]{1,0:T(8,128)(2,1)S(1)}, bf16[512,256]{1,0:T(8,128)(2,1)}, u32[]{:S(2)}) copy-start(bf16[512,256]{1,0:T(8,128)(2,1)} %constant.60.clone.one_ref.one_hbm) | copy-start | bytes 786436
  14.2 2.2 %copy-start.2 = (bf16[32,256,256]{2,1,0:T(8,128)(2,1)S(1)}, bf16[32,256,256]{2,1,0:T(8,128)(2,1)}, u32[]{:S(2)}) copy-start(bf16[32,256,256]{2,1,0:T(8,128)(2,1)} %constant.62.clone.two_ref.two_hbm) | copy-start | bytes 12582916
  21.1 2.0 %copy-start.4 = (f32[32,256,128]{2,1,0:T(8,128)}, f32[32,256,128]{2,1,0:T(8,128)S(1)}, u32[]{:S(2)}) copy-start(f32[32,256,128]{2,1,0:T(8,128)S(1)} %shard_map.158.h_hbm) | copy-start | bytes 12582916
  50.8 33.4 %all-to-all-start.1 = ((bf16[32,2,128,128]{3,2,1,0:T(8,128)(2,1)}), bf16[32,2,128,128]{3,2,1,0:T(8,128)(2,1)S(1)}, u32[]{:S(2)}, u32[]{:S(2)}) async-start(bf16[32,2,128,128]{3,2,1,0:T(8,128)(2,1)} %get-tuple-element.13), calls=%async_computation.1 | async-start | bytes 4194304 | tf_op jit(solution)/shard_map/all_to_all | solution.py:462
  55.6 28.6 %copy-start.1 = (bf16[1,128,4096]{2,1,0:T(8,128)(2,1)S(1)}, bf16[1,128,4096]{2,1,0:T(8,128)(2,1)}, u32[]{:S(2)}) copy-start(bf16[1,128,4096]{2,1,0:T(8,128)(2,1)} %param.16) | copy-start | bytes 3145732
  62.7 23.0 %collective-permute-start = (f32[8,1024]{1,0:T(8,128)S(1)}, f32[8,1024]{1,0:T(8,128)S(1)}, u32[]{:S(2)}, u32[]{:S(2)}) collective-permute-start(f32[8,1024]{1,0:T(8,128)S(1)} %get-tuple-element.25), channel_id=1, source_target_pairs={{0,32},{32,64},{64,96},{96,0},{1,33},{33,65},{65,97},{97,1},{2,34}... | collective-permute-start | bytes 98312 | tf_op jit(solution)/shard_map/ppermute | solution.py:473
  62.8 22.9 %collective-permute-start.1 = (f32[8,1024]{1,0:T(8,128)S(1)}, f32[8,1024]{1,0:T(8,128)S(1)}, u32[]{:S(2)}, u32[]{:S(2)}) collective-permute-start(f32[8,1024]{1,0:T(8,128)S(1)} %get-tuple-element.24), channel_id=1, source_target_pairs={{0,64},{32,96},{64,0},{96,32},{1,65},{33,97},{65,1},{97,33},{2,66}... | collective-permute-start | bytes 98312 | tf_op jit(solution)/shard_map/ppermute | solution.py:473
  65.8 19.9 %collective-permute-start.2 = (f32[8,1024]{1,0:T(8,128)S(1)}, f32[8,1024]{1,0:T(8,128)S(1)}, u32[]{:S(2)}, u32[]{:S(2)}) collective-permute-start(f32[8,1024]{1,0:T(8,128)S(1)} %get-tuple-element.23), channel_id=1, source_target_pairs={{0,96},{32,0},{64,32},{96,64},{1,97},{33,1},{65,33},{97,65},{2,98}... | collective-permute-start | bytes 98312 | tf_op jit(solution)/shard_map/ppermute | solution.py:473

commit v6 on v5

--- a/solution.py
+++ b/solution.py
@@ -149,9 +149,7 @@
         body(count * m, count, False)
 
 
-OUTER_ENDS = (8,)
 SLAB_ENDS = (16,32)
-LAST_ENDS = (8,)
 
 
 def groups(ends):
@@ -167,13 +165,14 @@
     @pl.loop(0, OUTER // 4)
     def _(m):
         for k in range(4):
-            spec_ref[4 * m + k] = dot(two_ref[4 * m + k], u_ref[4 * m + k])
+            spec = dot(two_ref[4 * m + k], u_ref[4 * m + k])
+            spec_ref[4 * m + k] = spec.astype(BF16)
 
 
 def main_kernel(
-    v_hbm, gain_hbm, one_hbm, three_hbm, h_hbm, two_hbm, last_hbm, out_hbm, spec_hbm,
-    v_ref, gain_ref, one_ref, three_ref, h_ref, two_ref, last_ref, out_ref, u_ref, back_ref,
-    v_sem, gain_sem, one_sem, three_sem, h_sem, two_sem, last_sem, out_sem, spec_sem,
+    v_ref, gain_ref, one_ref, three_ref, h_hbm, two_hbm, last_hbm, out_hbm, spec_hbm,
+    h_ref, two_ref, last_ref, out_ref, u_ref, back_ref,
+    h_sem, two_sem, last_sem, out_sem, spec_sem,
 ):
     def copies(ends, size, *arrays):
         made = []
@@ -184,46 +183,20 @@
             )
         return made
 
-    def row_copies(ends, source, target, sem):
-        made = []
-        for g, group in enumerate(groups(ends)):
-            cut = pl.ds(16 * group[0], 16 * len(group))
-            made.append(
-                pltpu.make_async_copy(source.at[:, :, cut], target.at[:, :, cut], sem.at[g])
-            )
-        return made
-
-    v_copies = row_copies(OUTER_ENDS, v_hbm, v_ref, v_sem)
     slab_copies = copies(SLAB_ENDS, 1, (two_hbm, two_ref, two_sem), (h_hbm, h_ref, h_sem))
     spec_copies = copies(SLAB_ENDS, 1, (u_ref, spec_hbm, spec_sem))
-    last_copies = copies(LAST_ENDS, 2, (last_hbm, last_ref, last_sem))
-    out_copies = row_copies(LAST_ENDS, out_ref, out_hbm, out_sem)
-    one_copy = pltpu.make_async_copy(one_hbm, one_ref, one_sem)
-    three_copy = pltpu.make_async_copy(three_hbm, three_ref, three_sem)
-    gain_copy = pltpu.make_async_copy(gain_hbm, gain_ref, gain_sem)
-
-    v_copies[0].start()
-    one_copy.start()
-    for copy in v_copies[1:]:
+    last_copies = copies((16,), 1, (last_hbm, last_ref, last_sem))
+    out_copy = pltpu.make_async_copy(out_ref, out_hbm, out_sem)
+    for copy in sum(slab_copies + last_copies, []):
         copy.start()
-    three_copy.start()
-    gain_copy.start()
-
-    one_copy.wait()
-    for g, group in enumerate(groups(OUTER_ENDS)):
-        v_copies[g].wait()
-        if g == len(OUTER_ENDS) - 1:
-            for copy in sum(slab_copies + last_copies, []):
-                copy.start()
-        for p in group:
-            both = v_ref[:, :, pl.ds(16 * p, 16), :].astype(F32)
-            outer_block(jnp.concatenate([both[:, 0], both[:, 1]], 2), one_ref, p, u_ref)
-    three_copy.wait()
+    for p in range(8):
+        both = v_ref[:, :, pl.ds(16 * p, 16), :].astype(F32)
+        outer_block(jnp.concatenate([both[:, 0], both[:, 1]], 2), one_ref, p, u_ref)
 
     def slab(j):
         spec = dot(two_ref[j], u_ref[j])
         real, imag = apart(spec)
-        hr, hi = apart(h_ref[j])
+        hr, hi = apart(h_ref[j].astype(F32))
         pr, pi = times(hr, hi, real[..., :LANES], imag[..., :LANES], False, j == 0)
         ar, ai = times(hr, hi, real[..., LANES:], imag[..., LANES:], True, j == 0)
         product = together(jnp.concatenate([pr, ar], 2), jnp.concatenate([pi, ai], 2))
@@ -236,7 +209,6 @@
         for j in group:
             slab(j)
         spec_copies[g][0].start()
-    gain_copy.wait()
 
     def last_block(p):
         row = p * 16
@@ -262,12 +234,12 @@
 
     for copy in sum(last_copies, []):
         copy.wait()
-    for g, group in enumerate(groups(LAST_ENDS)):
-        for p in group:
-            last_block(p)
-        out_copies[g].start()
-    for copy in sum(spec_copies, []) + out_copies:
+    for p in range(8):
+        last_block(p)
+    out_copy.start()
+    for copy in sum(spec_copies, []):
         copy.wait()
+    out_copy.wait()
 
 
 def filter_grad_kernel(
@@ -411,33 +383,33 @@
     return call(
         filter_kernel,
         (laid, t["one"], t["two"]),
-        jax.ShapeDtypeStruct((OUTER, PAIR, LANES), F32),
+        jax.ShapeDtypeStruct((OUTER, PAIR, LANES), BF16),
         [pltpu.VMEM((OUTER, PAIR, LANES), BF16)],
         4 << 30, 24 << 20,
     )
 
 
 def main_path(t, moved, kernel_spec, gains):
-    operands = (moved, gains, t["one"], t["three"], kernel_spec, t["two"], t["last"])
+    near = (moved, gains, t["one"], t["three"])
+    far = (kernel_spec, t["two"], t["last"])
     return pl.pallas_call(
         main_kernel,
         out_shape=(MOVED, HELD),
-        in_specs=[IN_HBM] * len(operands),
+        in_specs=[IN_VMEM] * len(near) + [IN_HBM] * len(far),
         out_specs=(IN_HBM, IN_HBM),
-        scratch_shapes=[pltpu.VMEM(o.shape, o.dtype) for o in operands]
+        scratch_shapes=[pltpu.VMEM(o.shape, o.dtype) for o in far]
         + [
             pltpu.VMEM(MOVED.shape, BF16),
             pltpu.VMEM(HELD.shape, BF16),
             pltpu.VMEM(HELD.shape, F32),
-            DMA((len(OUTER_ENDS),)), DMA, DMA, DMA, DMA((len(SLAB_ENDS),)),
-            DMA((len(SLAB_ENDS),)), DMA((len(LAST_ENDS),)), DMA((len(LAST_ENDS),)),
+            DMA((len(SLAB_ENDS),)), DMA((len(SLAB_ENDS),)), DMA((1,)), DMA,
             DMA((len(SLAB_ENDS),)),
         ],
         compiler_params=pltpu.CompilerParams(vmem_limit_bytes=60 << 20),
         cost_estimate=pl.CostEstimate(
             flops=6 << 30, bytes_accessed=20 << 20, transcendentals=0
         ),
-    )(*operands)
+    )(*near, *far)
 
 
 def filter_gradient(t, spec):

time: 86.7 us -> 86.5 us (level)
  no operation moved by 1% of the time
where the time goes in v6:
time: 86.5 us; the launch traced here: 86 us
  waiting for transfers between devices  34.5 us (40%)
  Pallas kernels  24.4 us (28%)
  starting transfers between devices  20.1 us (23%)
  local copies, waits for them, and re-layouts  5.02 us (6%)
    all_to_all x2, waiting for transfers between devices, exchange(): lax.all_to_all(blocks, 'ctx', split_axis=0, concat_axis=0, tiled=True)  34.5 us
    all_to_all x2, starting transfers between devices, exchange(): lax.all_to_all(blocks, 'ctx', split_axis=0, concat_axis=0, tiled=True)  14.2 us
    pallas_call x2, Pallas kernels, call(): pl.pallas_call(kernel, out_shape=outs, in_specs=[space] * len(operands),...  10.9 us
    pallas_call x1, Pallas kernels, main_path(): pl.pallas_call(main_kernel, out_shape=(MOVED, HELD), in_specs=[IN_VMEM] *...  9.14 us
    ppermute x3, starting transfers between devices, shares(): lax.ppermute(share((place + hop) % count), 'dp', [(i, (i + hop) % count)...  5.93 us
    unnamed x12, local copies, waits for them, and re-layouts  3.54 us
    pallas_call x1, Pallas kernels, gather(): pl.pallas_call(gather_kernel, out_shape=MOVED, in_specs=[IN_HBM] * 3, out...  2.91 us
  transfers between devices with their start and end apart: 5, of which 2 were waited for; matrix products, arithmetic and copies ran while one was open for 2% of the time, Pallas kernels for 14%

profile of v6, /device:TPU:0, one launch (start us, length us, event | category | flops | bytes accessed | tf_op | source)
XLA Modules:
  0.0 86.0 jit_solution(15036206145347584327)
XLA Ops:
  0.6 0.0 copy-start
  0.6 2.9 %shard_map.157 = bf16[32,2,128,128]{3,2,1,0:T(8,128)(2,1)} custom-call(bf16[128,4096]{1,0:T(8,128)(2,1)} %bitcast.22, bf16[128,4096]{1,0:T(8,128)(2,1)} %bitcast.23, bf16[128,4096]{1,0:T(8,128)(2,1)} %bitcast.19), custom_call_target="tpu_custom_call" | custom-call | tf_op jit(solution)/shard_map/pallas_call | solution.py:346
  3.6 0.0 copy-start.5
  3.6 9.4 %all-to-all-start = ((bf16[32,2,128,128]{3,2,1,0:T(8,128)(2,1)}), bf16[32,2,128,128]{3,2,1,0:T(8,128)(2,1)}, u32[]{:S(2)}, u32[]{:S(2)}) async-start(bf16[32,2,128,128]{3,2,1,0:T(8,128)(2,1)} %shard_map.157), calls=%async_computation | async-start | bytes 4194304 | tf_op jit(solution)/shard_map/all_to_all | solution.py:434
  13.0 0.0 copy-done
  13.0 0.0 copy-done.5
  13.0 0.0 copy-start.3
  13.0 0.5 fusion
  13.5 0.7 copy.17
  14.2 0.0 copy-done.3
  14.2 0.0 copy-start.2
  14.2 2.2 %copy-done.2 = bf16[32,256,256]{2,1,0:T(8,128)(2,1)S(1)} copy-done((bf16[32,256,256]{2,1,0:T(8,128)(2,1)S(1)}, bf16[32,256,256]{2,1,0:T(8,128)(2,1)}, u32[]{:S(2)}) %copy-start.2) | copy-done | bytes 4194328
  16.4 4.7 %shard_map.158.h_hbm = bf16[32,256,128]{2,1,0:T(8,128)(2,1)S(1)} custom-call(bf16[32,128,128]{2,1,0:T(8,128)(2,1)S(1)} %bitcast.21, bf16[512,256]{1,0:T(8,128)(2,1)S(1)} %copy-done.3, bf16[32,256,256]{2,1,0:T(8,128)(2,1)S(1)} %copy-done.2), custom_call_target="tpu_custom_call" | custom-call | flops 4294967296 | bytes 16777216 | tf_op jit(solution)/shard_map/pallas_call | solution.py:371
  21.1 0.0 copy-start.4
  21.1 1.3 %copy-done.4 = bf16[32,256,128]{2,1,0:T(8,128)(2,1)} copy-done((bf16[32,256,128]{2,1,0:T(8,128)(2,1)}, bf16[32,256,128]{2,1,0:T(8,128)(2,1)S(1)}, u32[]{:S(2)}) %copy-start.4) | copy-done | bytes 2097176
  22.4 19.0 %all-to-all-done.v_ref = bf16[32,2,128,128]{3,2,1,0:T(8,128)(2,1)} async-done(((bf16[32,2,128,128]{3,2,1,0:T(8,128)(2,1)}), bf16[32,2,128,128]{3,2,1,0:T(8,128)(2,1)}, u32[]{:S(2)}, u32[]{:S(2)}) %all-to-all-start) | async-done | bytes 2097184 | tf_op jit(solution)/shard_map/all_to_all | solution.py:434
  41.4 9.1 %shard_map.159 = (bf16[32,2,128,128]{3,2,1,0:T(8,128)(2,1)}, bf16[32,256,256]{2,1,0:T(8,128)(2,1)}) custom-call(bf16[32,2,128,128]{3,2,1,0:T(8,128)(2,1)} %all-to-all-done.v_ref, f32[1,128]{1,0:T(1,128)} %bitcast.26, bf16[512,256]{1,0:T(8,128)(2,1)} %constant.60.clone.one_ref, bf16[2,256,256]{2,1,0:T(8,128)(2,1)} %constant.63.clone.three_ref, ...), custom_call_target="tpu_custom_call" | custom-call | flops 6442450944 | bytes 20971520 | tf_op jit(solution)/shard_map/pallas_call | solution.py:395
  50.5 4.8 %all-to-all-start.1 = ((bf16[32,2,128,128]{3,2,1,0:T(8,128)(2,1)}), bf16[32,2,128,128]{3,2,1,0:T(8,128)(2,1)S(1)}, u32[]{:S(2)}, u32[]{:S(2)}) async-start(bf16[32,2,128,128]{3,2,1,0:T(8,128)(2,1)} %get-tuple-element.13), calls=%async_computation.1 | async-start | bytes 4194304 | tf_op jit(solution)/shard_map/all_to_all | solution.py:434
  55.4 0.0 copy-start.1
  55.4 6.2 %shard_map.161 = f32[4,8,1024]{2,1,0:T(8,128)} custom-call(bf16[32,256,256]{2,1,0:T(8,128)(2,1)} %get-tuple-element.16.spec_ref, bf16[2,256,256]{2,1,0:T(8,128)(2,1)} %constant.63.clone.three_ref, bf16[8,256,128]{2,1,0:T(8,128)(2,1)} %constant.64.clone.member_ref, f32[128,256]{1,0:T(8,128)} %constant.65.clone.turn_cos_ref, ...), custom_call_target="tpu_custom_call" | custom-call | flops 2147483648 | bytes 16777216 | tf_op jit(solution)/shard_map/pallas_call | solution.py:371
  61.6 0.8 dynamic-slice_bitcast_fusion
  62.4 0.1 collective-permute-start
  62.5 3.0 %collective-permute-start.1 = (f32[8,1024]{1,0:T(8,128)S(1)}, f32[8,1024]{1,0:T(8,128)S(1)}, u32[]{:S(2)}, u32[]{:S(2)}) collective-permute-start(f32[8,1024]{1,0:T(8,128)S(1)} %get-tuple-element.24), channel_id=1, source_target_pairs={{0,64},{32,96},{64,0},{96,32},{1,65},{33,97},{65,1},{97,33},{2,66}... | collective-permute-start | bytes 98312 | tf_op jit(solution)/shard_map/ppermute | solution.py:445
  65.5 2.9 %collective-permute-start.2 = (f32[8,1024]{1,0:T(8,128)S(1)}, f32[8,1024]{1,0:T(8,128)S(1)}, u32[]{:S(2)}, u32[]{:S(2)}) collective-permute-start(f32[8,1024]{1,0:T(8,128)S(1)} %get-tuple-element.23), channel_id=1, source_target_pairs={{0,96},{32,0},{64,32},{96,64},{1,97},{33,1},{65,33},{97,65},{2,98}... | collective-permute-start | bytes 98312 | tf_op jit(solution)/shard_map/ppermute | solution.py:445
  68.4 15.6 %all-to-all-done.1.back_ref = bf16[32,2,128,128]{3,2,1,0:T(8,128)(2,1)S(1)} async-done(((bf16[32,2,128,128]{3,2,1,0:T(8,128)(2,1)}), bf16[32,2,128,128]{3,2,1,0:T(8,128)(2,1)S(1)}, u32[]{:S(2)}, u32[]{:S(2)}) %all-to-all-start.1) | async-done | bytes 2097184 | tf_op jit(solution)/shard_map/all_to_all | solution.py:434
  83.9 0.0 copy-done.1
  83.9 1.4 %shard_map.160 = (bf16[128,4096]{1,0:T(8,128)(2,1)}, bf16[128,4096]{1,0:T(8,128)(2,1)}) custom-call(bf16[32,2,128,128]{3,2,1,0:T(8,128)(2,1)S(1)} %all-to-all-done.1.back_ref, bf16[128,4096]{1,0:T(8,128)(2,1)S(1)} %bitcast.20), custom_call_target="tpu_custom_call" | custom-call | tf_op jit(solution)/shard_map/pallas_call | solution.py:359
  85.4 0.0 collective-permute-done
  85.4 0.0 collective-permute-done.1
  85.4 0.0 collective-permute-done.2
  85.4 0.6 add_add_fusion
Async XLA Ops:
  0.6 12.4 %copy-start = (bf16[8,4096]{1,0:T(8,128)(2,1)S(1)}, bf16[8,4096]{1,0:T(8,128)(2,1)}, u32[]{:S(2)}) copy-start(bf16[8,4096]{1,0:T(8,128)(2,1)} %param.17) | copy-start | bytes 196612
  3.6 9.4 %copy-start.5 = (bf16[8,128]{1,0:T(8,128)(2,1)S(1)}, bf16[8,128]{1,0:T(8,128)(2,1)}, u32[]{:S(2)}) copy-start(bf16[8,128]{1,0:T(8,128)(2,1)} %constant.68.clone) | copy-start | bytes 6148
  3.6 37.8 %all-to-all-start = ((bf16[32,2,128,128]{3,2,1,0:T(8,128)(2,1)}), bf16[32,2,128,128]{3,2,1,0:T(8,128)(2,1)}, u32[]{:S(2)}, u32[]{:S(2)}) async-start(bf16[32,2,128,128]{3,2,1,0:T(8,128)(2,1)} %shard_map.157), calls=%async_computation | async-start | bytes 4194304 | tf_op jit(solution)/shard_map/all_to_all | solution.py:434
  13.0 1.2 %copy-start.3 = (bf16[512,256]{1,0:T(8,128)(2,1)S(1)}, bf16[512,256]{1,0:T(8,128)(2,1)}, u32[]{:S(2)}) copy-start(bf16[512,256]{1,0:T(8,128)(2,1)} %constant.60.clone.one_ref) | copy-start | bytes 786436
  14.2 2.2 %copy-start.2 = (bf16[32,256,256]{2,1,0:T(8,128)(2,1)S(1)}, bf16[32,256,256]{2,1,0:T(8,128)(2,1)}, u32[]{:S(2)}) copy-start(bf16[32,256,256]{2,1,0:T(8,128)(2,1)} %constant.62.clone.two_ref.two_hbm) | copy-start | bytes 12582916
  21.1 1.3 %copy-start.4 = (bf16[32,256,128]{2,1,0:T(8,128)(2,1)}, bf16[32,256,128]{2,1,0:T(8,128)(2,1)S(1)}, u32[]{:S(2)}) copy-start(bf16[32,256,128]{2,1,0:T(8,128)(2,1)S(1)} %shard_map.158.h_hbm) | copy-start | bytes 6291460
  50.5 33.4 %all-to-all-start.1 = ((bf16[32,2,128,128]{3,2,1,0:T(8,128)(2,1)}), bf16[32,2,128,128]{3,2,1,0:T(8,128)(2,1)S(1)}, u32[]{:S(2)}, u32[]{:S(2)}) async-start(bf16[32,2,128,128]{3,2,1,0:T(8,128)(2,1)} %get-tuple-element.13), calls=%async_computation.1 | async-start | bytes 4194304 | tf_op jit(solution)/shard_map/all_to_all | solution.py:434
  55.4 28.6 %copy-start.1 = (bf16[1,128,4096]{2,1,0:T(8,128)(2,1)S(1)}, bf16[1,128,4096]{2,1,0:T(8,128)(2,1)}, u32[]{:S(2)}) copy-start(bf16[1,128,4096]{2,1,0:T(8,128)(2,1)} %param.16) | copy-start | bytes 3145732
  62.4 23.0 %collective-permute-start = (f32[8,1024]{1,0:T(8,128)S(1)}, f32[8,1024]{1,0:T(8,128)S(1)}, u32[]{:S(2)}, u32[]{:S(2)}) collective-permute-start(f32[8,1024]{1,0:T(8,128)S(1)} %get-tuple-element.25), channel_id=1, source_target_pairs={{0,32},{32,64},{64,96},{96,0},{1,33},{33,65},{65,97},{97,1},{2,34}... | collective-permute-start | bytes 98312 | tf_op jit(solution)/shard_map/ppermute | solution.py:445
  62.5 22.9 %collective-permute-start.1 = (f32[8,1024]{1,0:T(8,128)S(1)}, f32[8,1024]{1,0:T(8,128)S(1)}, u32[]{:S(2)}, u32[]{:S(2)}) collective-permute-start(f32[8,1024]{1,0:T(8,128)S(1)} %get-tuple-element.24), channel_id=1, source_target_pairs={{0,64},{32,96},{64,0},{96,32},{1,65},{33,97},{65,1},{97,33},{2,66}... | collective-permute-start | bytes 98312 | tf_op jit(solution)/shard_map/ppermute | solution.py:445
  65.5 19.9 %collective-permute-start.2 = (f32[8,1024]{1,0:T(8,128)S(1)}, f32[8,1024]{1,0:T(8,128)S(1)}, u32[]{:S(2)}, u32[]{:S(2)}) collective-permute-start(f32[8,1024]{1,0:T(8,128)S(1)} %get-tuple-element.23), channel_id=1, source_target_pairs={{0,96},{32,0},{64,32},{96,64},{1,97},{33,1},{65,33},{97,65},{2,98}... | collective-permute-start | bytes 98312 | tf_op jit(solution)/shard_map/ppermute | solution.py:445

commit v7 on v6

--- a/solution.py
+++ b/solution.py
@@ -134,10 +134,6 @@
         real = jnp.where(edge, ar * br, real)
         imag = jnp.where(edge, cross, imag)
     return real, imag
-
-
-def lane_cut(values, k, width):
-    return values[:, width * k : width * k + width]
 
 
 def slabs(body, count):
@@ -449,13 +445,6 @@
     ]
 
 
-def unit(moved_input, moved_grad, filters, gains):
-    t = build_tables(1.0 / (8192 * 512))
-    moved = jnp.stack([moved_input, moved_grad], 1)
-    out, spec = main_path(t, moved, filter_spectrum(t, lay_filters(filters)), gains)
-    return out[:, 0], out[:, 1], filter_gradient(t, spec)
-
-
 def on_device(gate_values, conv_input, cotangent, filters, direct_scale):
     replica_count = lax.axis_size("dp")
     grad_scale = 1.0 / (POINTS * math.sqrt(GROUP_WIDTH * replica_count * POINTS // 2))

time: 86.5 us -> 86.5 us (level)
  no operation moved by 1% of the time
where the time goes in v7:
time: 86.5 us; the launch traced here: 86 us
  waiting for transfers between devices  34.5 us (40%)
  Pallas kernels  24.4 us (28%)
  starting transfers between devices  20.1 us (23%)
  local copies, waits for them, and re-layouts  5.02 us (6%)
    all_to_all x2, waiting for transfers between devices, exchange(): lax.all_to_all(blocks, 'ctx', split_axis=0, concat_axis=0, tiled=True)  34.5 us
    all_to_all x2, starting transfers between devices, exchange(): lax.all_to_all(blocks, 'ctx', split_axis=0, concat_axis=0, tiled=True)  14.2 us
    pallas_call x2, Pallas kernels, call(): pl.pallas_call(kernel, out_shape=outs, in_specs=[space] * len(operands),...  10.9 us
    pallas_call x1, Pallas kernels, main_path(): pl.pallas_call(main_kernel, out_shape=(MOVED, HELD), in_specs=[IN_VMEM] *...  9.14 us
    ppermute x3, starting transfers between devices, shares(): lax.ppermute(share((place + hop) % count), 'dp', [(i, (i + hop) % count)...  5.93 us
    unnamed x12, local copies, waits for them, and re-layouts  3.54 us
    pallas_call x1, Pallas kernels, gather(): pl.pallas_call(gather_kernel, out_shape=MOVED, in_specs=[IN_HBM] * 3, out...  2.91 us
  transfers between devices with their start and end apart: 5, of which 2 were waited for; matrix products, arithmetic and copies ran while one was open for 2% of the time, Pallas kernels for 14%

profile of v7, /device:TPU:0, one launch (start us, length us, event | category | flops | bytes accessed | tf_op | source)
XLA Modules:
  0.0 86.0 jit_solution(15036206145347584327)
XLA Ops:
  0.6 0.0 copy-start
  0.6 2.9 %shard_map.157 = bf16[32,2,128,128]{3,2,1,0:T(8,128)(2,1)} custom-call(bf16[128,4096]{1,0:T(8,128)(2,1)} %bitcast.22, bf16[128,4096]{1,0:T(8,128)(2,1)} %bitcast.23, bf16[128,4096]{1,0:T(8,128)(2,1)} %bitcast.19), custom_call_target="tpu_custom_call" | custom-call | tf_op jit(solution)/shard_map/pallas_call | solution.py:342
  3.6 0.0 copy-start.5
  3.6 9.4 %all-to-all-start = ((bf16[32,2,128,128]{3,2,1,0:T(8,128)(2,1)}), bf16[32,2,128,128]{3,2,1,0:T(8,128)(2,1)}, u32[]{:S(2)}, u32[]{:S(2)}) async-start(bf16[32,2,128,128]{3,2,1,0:T(8,128)(2,1)} %shard_map.157), calls=%async_computation | async-start | bytes 4194304 | tf_op jit(solution)/shard_map/all_to_all | solution.py:430
  13.0 0.0 copy-done
  13.0 0.0 copy-done.5
  13.0 0.0 copy-start.3
  13.0 0.5 fusion
  13.5 0.7 copy.17
  14.2 0.0 copy-done.3
  14.2 0.0 copy-start.2
  14.2 2.2 %copy-done.2 = bf16[32,256,256]{2,1,0:T(8,128)(2,1)S(1)} copy-done((bf16[32,256,256]{2,1,0:T(8,128)(2,1)S(1)}, bf16[32,256,256]{2,1,0:T(8,128)(2,1)}, u32[]{:S(2)}) %copy-start.2) | copy-done | bytes 4194328
  16.4 4.7 %shard_map.158.h_hbm = bf16[32,256,128]{2,1,0:T(8,128)(2,1)S(1)} custom-call(bf16[32,128,128]{2,1,0:T(8,128)(2,1)S(1)} %bitcast.21, bf16[512,256]{1,0:T(8,128)(2,1)S(1)} %copy-done.3, bf16[32,256,256]{2,1,0:T(8,128)(2,1)S(1)} %copy-done.2), custom_call_target="tpu_custom_call" | custom-call | flops 4294967296 | bytes 16777216 | tf_op jit(solution)/shard_map/pallas_call | solution.py:367
  21.1 0.0 copy-start.4
  21.1 1.3 %copy-done.4 = bf16[32,256,128]{2,1,0:T(8,128)(2,1)} copy-done((bf16[32,256,128]{2,1,0:T(8,128)(2,1)}, bf16[32,256,128]{2,1,0:T(8,128)(2,1)S(1)}, u32[]{:S(2)}) %copy-start.4) | copy-done | bytes 2097176
  22.4 19.0 %all-to-all-done.v_ref = bf16[32,2,128,128]{3,2,1,0:T(8,128)(2,1)} async-done(((bf16[32,2,128,128]{3,2,1,0:T(8,128)(2,1)}), bf16[32,2,128,128]{3,2,1,0:T(8,128)(2,1)}, u32[]{:S(2)}, u32[]{:S(2)}) %all-to-all-start) | async-done | bytes 2097184 | tf_op jit(solution)/shard_map/all_to_all | solution.py:430
  41.4 9.1 %shard_map.159 = (bf16[32,2,128,128]{3,2,1,0:T(8,128)(2,1)}, bf16[32,256,256]{2,1,0:T(8,128)(2,1)}) custom-call(bf16[32,2,128,128]{3,2,1,0:T(8,128)(2,1)} %all-to-all-done.v_ref, f32[1,128]{1,0:T(1,128)} %bitcast.26, bf16[512,256]{1,0:T(8,128)(2,1)} %constant.60.clone.one_ref, bf16[2,256,256]{2,1,0:T(8,128)(2,1)} %constant.63.clone.three_ref, ...), custom_call_target="tpu_custom_call" | custom-call | flops 6442450944 | bytes 20971520 | tf_op jit(solution)/shard_map/pallas_call | solution.py:391
  50.5 4.8 %all-to-all-start.1 = ((bf16[32,2,128,128]{3,2,1,0:T(8,128)(2,1)}), bf16[32,2,128,128]{3,2,1,0:T(8,128)(2,1)S(1)}, u32[]{:S(2)}, u32[]{:S(2)}) async-start(bf16[32,2,128,128]{3,2,1,0:T(8,128)(2,1)} %get-tuple-element.13), calls=%async_computation.1 | async-start | bytes 4194304 | tf_op jit(solution)/shard_map/all_to_all | solution.py:430
  55.4 0.0 copy-start.1
  55.4 6.2 %shard_map.161 = f32[4,8,1024]{2,1,0:T(8,128)} custom-call(bf16[32,256,256]{2,1,0:T(8,128)(2,1)} %get-tuple-element.16.spec_ref, bf16[2,256,256]{2,1,0:T(8,128)(2,1)} %constant.63.clone.three_ref, bf16[8,256,128]{2,1,0:T(8,128)(2,1)} %constant.64.clone.member_ref, f32[128,256]{1,0:T(8,128)} %constant.65.clone.turn_cos_ref, ...), custom_call_target="tpu_custom_call" | custom-call | flops 2147483648 | bytes 16777216 | tf_op jit(solution)/shard_map/pallas_call | solution.py:367
  61.6 0.8 dynamic-slice_bitcast_fusion
  62.4 0.1 collective-permute-start
  62.5 3.0 %collective-permute-start.1 = (f32[8,1024]{1,0:T(8,128)S(1)}, f32[8,1024]{1,0:T(8,128)S(1)}, u32[]{:S(2)}, u32[]{:S(2)}) collective-permute-start(f32[8,1024]{1,0:T(8,128)S(1)} %get-tuple-element.24), channel_id=1, source_target_pairs={{0,64},{32,96},{64,0},{96,32},{1,65},{33,97},{65,1},{97,33},{2,66}... | collective-permute-start | bytes 98312 | tf_op jit(solution)/shard_map/ppermute | solution.py:441
  65.5 2.9 %collective-permute-start.2 = (f32[8,1024]{1,0:T(8,128)S(1)}, f32[8,1024]{1,0:T(8,128)S(1)}, u32[]{:S(2)}, u32[]{:S(2)}) collective-permute-start(f32[8,1024]{1,0:T(8,128)S(1)} %get-tuple-element.23), channel_id=1, source_target_pairs={{0,96},{32,0},{64,32},{96,64},{1,97},{33,1},{65,33},{97,65},{2,98}... | collective-permute-start | bytes 98312 | tf_op jit(solution)/shard_map/ppermute | solution.py:441
  68.4 15.6 %all-to-all-done.1.back_ref = bf16[32,2,128,128]{3,2,1,0:T(8,128)(2,1)S(1)} async-done(((bf16[32,2,128,128]{3,2,1,0:T(8,128)(2,1)}), bf16[32,2,128,128]{3,2,1,0:T(8,128)(2,1)S(1)}, u32[]{:S(2)}, u32[]{:S(2)}) %all-to-all-start.1) | async-done | bytes 2097184 | tf_op jit(solution)/shard_map/all_to_all | solution.py:430
  83.9 0.0 copy-done.1
  83.9 1.4 %shard_map.160 = (bf16[128,4096]{1,0:T(8,128)(2,1)}, bf16[128,4096]{1,0:T(8,128)(2,1)}) custom-call(bf16[32,2,128,128]{3,2,1,0:T(8,128)(2,1)S(1)} %all-to-all-done.1.back_ref, bf16[128,4096]{1,0:T(8,128)(2,1)S(1)} %bitcast.20), custom_call_target="tpu_custom_call" | custom-call | tf_op jit(solution)/shard_map/pallas_call | solution.py:355
  85.4 0.0 collective-permute-done
  85.4 0.0 collective-permute-done.1
  85.4 0.0 collective-permute-done.2
  85.4 0.6 add_add_fusion
Async XLA Ops:
  0.6 12.4 %copy-start = (bf16[8,4096]{1,0:T(8,128)(2,1)S(1)}, bf16[8,4096]{1,0:T(8,128)(2,1)}, u32[]{:S(2)}) copy-start(bf16[8,4096]{1,0:T(8,128)(2,1)} %param.17) | copy-start | bytes 196612
  3.6 9.4 %copy-start.5 = (bf16[8,128]{1,0:T(8,128)(2,1)S(1)}, bf16[8,128]{1,0:T(8,128)(2,1)}, u32[]{:S(2)}) copy-start(bf16[8,128]{1,0:T(8,128)(2,1)} %constant.68.clone) | copy-start | bytes 6148
  3.6 37.8 %all-to-all-start = ((bf16[32,2,128,128]{3,2,1,0:T(8,128)(2,1)}), bf16[32,2,128,128]{3,2,1,0:T(8,128)(2,1)}, u32[]{:S(2)}, u32[]{:S(2)}) async-start(bf16[32,2,128,128]{3,2,1,0:T(8,128)(2,1)} %shard_map.157), calls=%async_computation | async-start | bytes 4194304 | tf_op jit(solution)/shard_map/all_to_all | solution.py:430
  13.0 1.2 %copy-start.3 = (bf16[512,256]{1,0:T(8,128)(2,1)S(1)}, bf16[512,256]{1,0:T(8,128)(2,1)}, u32[]{:S(2)}) copy-start(bf16[512,256]{1,0:T(8,128)(2,1)} %constant.60.clone.one_ref) | copy-start | bytes 786436
  14.2 2.2 %copy-start.2 = (bf16[32,256,256]{2,1,0:T(8,128)(2,1)S(1)}, bf16[32,256,256]{2,1,0:T(8,128)(2,1)}, u32[]{:S(2)}) copy-start(bf16[32,256,256]{2,1,0:T(8,128)(2,1)} %constant.62.clone.two_ref.two_hbm) | copy-start | bytes 12582916
  21.1 1.3 %copy-start.4 = (bf16[32,256,128]{2,1,0:T(8,128)(2,1)}, bf16[32,256,128]{2,1,0:T(8,128)(2,1)S(1)}, u32[]{:S(2)}) copy-start(bf16[32,256,128]{2,1,0:T(8,128)(2,1)S(1)} %shard_map.158.h_hbm) | copy-start | bytes 6291460
  50.5 33.4 %all-to-all-start.1 = ((bf16[32,2,128,128]{3,2,1,0:T(8,128)(2,1)}), bf16[32,2,128,128]{3,2,1,0:T(8,128)(2,1)S(1)}, u32[]{:S(2)}, u32[]{:S(2)}) async-start(bf16[32,2,128,128]{3,2,1,0:T(8,128)(2,1)} %get-tuple-element.13), calls=%async_computation.1 | async-start | bytes 4194304 | tf_op jit(solution)/shard_map/all_to_all | solution.py:430
  55.4 28.6 %copy-start.1 = (bf16[1,128,4096]{2,1,0:T(8,128)(2,1)S(1)}, bf16[1,128,4096]{2,1,0:T(8,128)(2,1)}, u32[]{:S(2)}) copy-start(bf16[1,128,4096]{2,1,0:T(8,128)(2,1)} %param.16) | copy-start | bytes 3145732
  62.4 23.0 %collective-permute-start = (f32[8,1024]{1,0:T(8,128)S(1)}, f32[8,1024]{1,0:T(8,128)S(1)}, u32[]{:S(2)}, u32[]{:S(2)}) collective-permute-start(f32[8,1024]{1,0:T(8,128)S(1)} %get-tuple-element.25), channel_id=1, source_target_pairs={{0,32},{32,64},{64,96},{96,0},{1,33},{33,65},{65,97},{97,1},{2,34}... | collective-permute-start | bytes 98312 | tf_op jit(solution)/shard_map/ppermute | solution.py:441
  62.5 22.9 %collective-permute-start.1 = (f32[8,1024]{1,0:T(8,128)S(1)}, f32[8,1024]{1,0:T(8,128)S(1)}, u32[]{:S(2)}, u32[]{:S(2)}) collective-permute-start(f32[8,1024]{1,0:T(8,128)S(1)} %get-tuple-element.24), channel_id=1, source_target_pairs={{0,64},{32,96},{64,0},{96,32},{1,65},{33,97},{65,1},{97,33},{2,66}... | collective-permute-start | bytes 98312 | tf_op jit(solution)/shard_map/ppermute | solution.py:441
  65.5 19.9 %collective-permute-start.2 = (f32[8,1024]{1,0:T(8,128)S(1)}, f32[8,1024]{1,0:T(8,128)S(1)}, u32[]{:S(2)}, u32[]{:S(2)}) collective-permute-start(f32[8,1024]{1,0:T(8,128)S(1)} %get-tuple-element.23), channel_id=1, source_target_pairs={{0,96},{32,0},{64,32},{96,64},{1,97},{33,1},{65,33},{97,65},{2,98}... | collective-permute-start | bytes 98312 | tf_op jit(solution)/shard_map/ppermute | solution.py:441

commit v8 on v5

--- a/solution.py
+++ b/solution.py
@@ -167,7 +167,8 @@
     @pl.loop(0, OUTER // 4)
     def _(m):
         for k in range(4):
-            spec_ref[4 * m + k] = dot(two_ref[4 * m + k], u_ref[4 * m + k])
+            spec = dot(two_ref[4 * m + k], u_ref[4 * m + k])
+            spec_ref[4 * m + k] = spec.astype(spec_ref.dtype)
 
 
 def main_kernel(
@@ -209,12 +210,11 @@
     three_copy.start()
     gain_copy.start()
 
+    for copy in sum(slab_copies + last_copies, []):
+        copy.start()
     one_copy.wait()
     for g, group in enumerate(groups(OUTER_ENDS)):
         v_copies[g].wait()
-        if g == len(OUTER_ENDS) - 1:
-            for copy in sum(slab_copies + last_copies, []):
-                copy.start()
         for p in group:
             both = v_ref[:, :, pl.ds(16 * p, 16), :].astype(F32)
             outer_block(jnp.concatenate([both[:, 0], both[:, 1]], 2), one_ref, p, u_ref)
@@ -223,7 +223,7 @@
     def slab(j):
         spec = dot(two_ref[j], u_ref[j])
         real, imag = apart(spec)
-        hr, hi = apart(h_ref[j])
+        hr, hi = apart(h_ref[j].astype(F32))
         pr, pi = times(hr, hi, real[..., :LANES], imag[..., :LANES], False, j == 0)
         ar, ai = times(hr, hi, real[..., LANES:], imag[..., LANES:], True, j == 0)
         product = together(jnp.concatenate([pr, ar], 2), jnp.concatenate([pi, ai], 2))
@@ -411,7 +411,7 @@
     return call(
         filter_kernel,
         (laid, t["one"], t["two"]),
-        jax.ShapeDtypeStruct((OUTER, PAIR, LANES), F32),
+        jax.ShapeDtypeStruct((OUTER, PAIR, LANES), BF16),
         [pltpu.VMEM((OUTER, PAIR, LANES), BF16)],
         4 << 30, 24 << 20,
     )
@@ -477,13 +477,6 @@
     ]
 
 
-def unit(moved_input, moved_grad, filters, gains):
-    t = build_tables(1.0 / (8192 * 512))
-    moved = jnp.stack([moved_input, moved_grad], 1)
-    out, spec = main_path(t, moved, filter_spectrum(t, lay_filters(filters)), gains)
-    return out[:, 0], out[:, 1], filter_gradient(t, spec)
-
-
 def on_device(gate_values, conv_input, cotangent, filters, direct_scale):
     replica_count = lax.axis_size("dp")
     grad_scale = 1.0 / (POINTS * math.sqrt(GROUP_WIDTH * replica_count * POINTS // 2))

time: 86.7 us -> 86.8 us (level)
  no operation moved by 1% of the time
where the time goes in v8:
time: 86.8 us; the launch traced here: 86.4 us
  waiting for transfers between devices  34.6 us (40%)
  Pallas kernels  24.7 us (28%)
  starting transfers between devices  20.1 us (23%)
  local copies, waits for them, and re-layouts  5.02 us (6%)
    all_to_all x2, waiting for transfers between devices, exchange(): lax.all_to_all(blocks, 'ctx', split_axis=0, concat_axis=0, tiled=True)  34.6 us
    all_to_all x2, starting transfers between devices, exchange(): lax.all_to_all(blocks, 'ctx', split_axis=0, concat_axis=0, tiled=True)  14.2 us
    pallas_call x2, Pallas kernels, call(): pl.pallas_call(kernel, out_shape=outs, in_specs=[space] * len(operands),...  10.9 us
    pallas_call x1, Pallas kernels, main_path(): pl.pallas_call(main_kernel, out_shape=(MOVED, HELD), in_specs=[IN_HBM] *...  9.46 us
    ppermute x3, starting transfers between devices, shares(): lax.ppermute(share((place + hop) % count), 'dp', [(i, (i + hop) % count)...  5.93 us
    unnamed x12, local copies, waits for them, and re-layouts  3.54 us
    pallas_call x1, Pallas kernels, gather(): pl.pallas_call(gather_kernel, out_shape=MOVED, in_specs=[IN_HBM] * 3, out...  2.91 us
  transfers between devices with their start and end apart: 5, of which 2 were waited for; matrix products, arithmetic and copies ran while one was open for 2% of the time, Pallas kernels for 14%

profile of v8, /device:TPU:0, one launch (start us, length us, event | category | flops | bytes accessed | tf_op | source)
XLA Modules:
  0.0 86.4 jit_solution(13267674295563180290)
XLA Ops:
  0.6 0.0 copy-start
  0.6 2.9 %shard_map.157 = bf16[32,2,128,128]{3,2,1,0:T(8,128)(2,1)} custom-call(bf16[128,4096]{1,0:T(8,128)(2,1)} %bitcast.22, bf16[128,4096]{1,0:T(8,128)(2,1)} %bitcast.23, bf16[128,4096]{1,0:T(8,128)(2,1)} %bitcast.19), custom_call_target="tpu_custom_call" | custom-call | tf_op jit(solution)/shard_map/pallas_call | solution.py:374
  3.6 0.0 copy-start.5
  3.6 9.4 %all-to-all-start = ((bf16[32,2,128,128]{3,2,1,0:T(8,128)(2,1)}), bf16[32,2,128,128]{3,2,1,0:T(8,128)(2,1)}, u32[]{:S(2)}, u32[]{:S(2)}) async-start(bf16[32,2,128,128]{3,2,1,0:T(8,128)(2,1)} %shard_map.157), calls=%async_computation | async-start | bytes 4194304 | tf_op jit(solution)/shard_map/all_to_all | solution.py:462
  13.0 0.0 copy-done
  13.0 0.0 copy-done.5
  13.0 0.0 copy-start.3
  13.0 0.5 fusion
  13.5 0.7 copy.17
  14.2 0.0 copy-done.3
  14.2 0.0 copy-start.2
  14.2 2.2 %copy-done.2 = bf16[32,256,256]{2,1,0:T(8,128)(2,1)S(1)} copy-done((bf16[32,256,256]{2,1,0:T(8,128)(2,1)S(1)}, bf16[32,256,256]{2,1,0:T(8,128)(2,1)}, u32[]{:S(2)}) %copy-start.2) | copy-done | bytes 4194328
  16.4 4.7 %shard_map.158.h_hbm = bf16[32,256,128]{2,1,0:T(8,128)(2,1)S(1)} custom-call(bf16[32,128,128]{2,1,0:T(8,128)(2,1)S(1)} %bitcast.21, bf16[512,256]{1,0:T(8,128)(2,1)S(1)} %copy-done.3, bf16[32,256,256]{2,1,0:T(8,128)(2,1)S(1)} %copy-done.2), custom_call_target="tpu_custom_call" | custom-call | flops 4294967296 | bytes 16777216 | tf_op jit(solution)/shard_map/pallas_call | solution.py:399
  21.1 0.0 copy-start.4
  21.1 1.3 %copy-done.4 = bf16[32,256,128]{2,1,0:T(8,128)(2,1)} copy-done((bf16[32,256,128]{2,1,0:T(8,128)(2,1)}, bf16[32,256,128]{2,1,0:T(8,128)(2,1)S(1)}, u32[]{:S(2)}) %copy-start.4) | copy-done | bytes 2097176
  22.4 19.0 %all-to-all-done.v_hbm = bf16[32,2,128,128]{3,2,1,0:T(8,128)(2,1)} async-done(((bf16[32,2,128,128]{3,2,1,0:T(8,128)(2,1)}), bf16[32,2,128,128]{3,2,1,0:T(8,128)(2,1)}, u32[]{:S(2)}, u32[]{:S(2)}) %all-to-all-start) | async-done | bytes 2097184 | tf_op jit(solution)/shard_map/all_to_all | solution.py:462
  41.4 9.5 %shard_map.159 = (bf16[32,2,128,128]{3,2,1,0:T(8,128)(2,1)}, bf16[32,256,256]{2,1,0:T(8,128)(2,1)}) custom-call(bf16[32,2,128,128]{3,2,1,0:T(8,128)(2,1)} %all-to-all-done.v_hbm, f32[1,128]{1,0:T(1,128)} %bitcast.26, bf16[512,256]{1,0:T(8,128)(2,1)} %constant.60.clone.one_ref.one_hbm, bf16[2,256,256]{2,1,0:T(8,128)(2,1)} %constant.63.clone.three_hbm.three_ref, ...), custom_call_target="tpu_custom_call" | custom-call | flops 6442450944 | bytes 20971520 | tf_op jit(solution)/shard_map/pallas_call | solution.py:422
  50.8 4.8 %all-to-all-start.1 = ((bf16[32,2,128,128]{3,2,1,0:T(8,128)(2,1)}), bf16[32,2,128,128]{3,2,1,0:T(8,128)(2,1)S(1)}, u32[]{:S(2)}, u32[]{:S(2)}) async-start(bf16[32,2,128,128]{3,2,1,0:T(8,128)(2,1)} %get-tuple-element.13), calls=%async_computation.1 | async-start | bytes 4194304 | tf_op jit(solution)/shard_map/all_to_all | solution.py:462
  55.7 0.0 copy-start.1
  55.7 6.2 %shard_map.161 = f32[4,8,1024]{2,1,0:T(8,128)} custom-call(bf16[32,256,256]{2,1,0:T(8,128)(2,1)} %get-tuple-element.16.spec_ref, bf16[2,256,256]{2,1,0:T(8,128)(2,1)} %constant.63.clone.three_hbm.three_ref, bf16[8,256,128]{2,1,0:T(8,128)(2,1)} %constant.64.clone.member_ref, f32[128,256]{1,0:T(8,128)} %constant.65.clone.turn_cos_ref, ...), custom_call_target="tpu_custom_call" | custom-call | flops 2147483648 | bytes 16777216 | tf_op jit(solution)/shard_map/pallas_call | solution.py:399
  61.9 0.8 dynamic-slice_bitcast_fusion
  62.7 0.1 collective-permute-start
  62.8 3.0 %collective-permute-start.1 = (f32[8,1024]{1,0:T(8,128)S(1)}, f32[8,1024]{1,0:T(8,128)S(1)}, u32[]{:S(2)}, u32[]{:S(2)}) collective-permute-start(f32[8,1024]{1,0:T(8,128)S(1)} %get-tuple-element.24), channel_id=1, source_target_pairs={{0,64},{32,96},{64,0},{96,32},{1,65},{33,97},{65,1},{97,33},{2,66}... | collective-permute-start | bytes 98312 | tf_op jit(solution)/shard_map/ppermute | solution.py:473
  65.8 2.9 %collective-permute-start.2 = (f32[8,1024]{1,0:T(8,128)S(1)}, f32[8,1024]{1,0:T(8,128)S(1)}, u32[]{:S(2)}, u32[]{:S(2)}) collective-permute-start(f32[8,1024]{1,0:T(8,128)S(1)} %get-tuple-element.23), channel_id=1, source_target_pairs={{0,96},{32,0},{64,32},{96,64},{1,97},{33,1},{65,33},{97,65},{2,98}... | collective-permute-start | bytes 98312 | tf_op jit(solution)/shard_map/ppermute | solution.py:473
  68.7 15.6 %all-to-all-done.1.back_ref = bf16[32,2,128,128]{3,2,1,0:T(8,128)(2,1)S(1)} async-done(((bf16[32,2,128,128]{3,2,1,0:T(8,128)(2,1)}), bf16[32,2,128,128]{3,2,1,0:T(8,128)(2,1)S(1)}, u32[]{:S(2)}, u32[]{:S(2)}) %all-to-all-start.1) | async-done | bytes 2097184 | tf_op jit(solution)/shard_map/all_to_all | solution.py:462
  84.3 0.0 copy-done.1
  84.3 1.4 %shard_map.160 = (bf16[128,4096]{1,0:T(8,128)(2,1)}, bf16[128,4096]{1,0:T(8,128)(2,1)}) custom-call(bf16[32,2,128,128]{3,2,1,0:T(8,128)(2,1)S(1)} %all-to-all-done.1.back_ref, bf16[128,4096]{1,0:T(8,128)(2,1)S(1)} %bitcast.20), custom_call_target="tpu_custom_call" | custom-call | tf_op jit(solution)/shard_map/pallas_call | solution.py:387
  85.7 0.0 collective-permute-done
  85.7 0.0 collective-permute-done.1
  85.8 0.0 collective-permute-done.2
  85.8 0.6 add_add_fusion
Async XLA Ops:
  0.6 12.4 %copy-start = (bf16[8,4096]{1,0:T(8,128)(2,1)S(1)}, bf16[8,4096]{1,0:T(8,128)(2,1)}, u32[]{:S(2)}) copy-start(bf16[8,4096]{1,0:T(8,128)(2,1)} %param.17) | copy-start | bytes 196612
  3.6 9.4 %copy-start.5 = (bf16[8,128]{1,0:T(8,128)(2,1)S(1)}, bf16[8,128]{1,0:T(8,128)(2,1)}, u32[]{:S(2)}) copy-start(bf16[8,128]{1,0:T(8,128)(2,1)} %constant.68.clone) | copy-start | bytes 6148
  3.6 37.8 %all-to-all-start = ((bf16[32,2,128,128]{3,2,1,0:T(8,128)(2,1)}), bf16[32,2,128,128]{3,2,1,0:T(8,128)(2,1)}, u32[]{:S(2)}, u32[]{:S(2)}) async-start(bf16[32,2,128,128]{3,2,1,0:T(8,128)(2,1)} %shard_map.157), calls=%async_computation | async-start | bytes 4194304 | tf_op jit(solution)/shard_map/all_to_all | solution.py:462
  13.0 1.2 %copy-start.3 = (bf16[512,256]{1,0:T(8,128)(2,1)S(1)}, bf16[512,256]{1,0:T(8,128)(2,1)}, u32[]{:S(2)}) copy-start(bf16[512,256]{1,0:T(8,128)(2,1)} %constant.60.clone.one_ref.one_hbm) | copy-start | bytes 786436
  14.2 2.2 %copy-start.2 = (bf16[32,256,256]{2,1,0:T(8,128)(2,1)S(1)}, bf16[32,256,256]{2,1,0:T(8,128)(2,1)}, u32[]{:S(2)}) copy-start(bf16[32,256,256]{2,1,0:T(8,128)(2,1)} %constant.62.clone.two_ref.two_hbm) | copy-start | bytes 12582916
  21.1 1.3 %copy-start.4 = (bf16[32,256,128]{2,1,0:T(8,128)(2,1)}, bf16[32,256,128]{2,1,0:T(8,128)(2,1)S(1)}, u32[]{:S(2)}) copy-start(bf16[32,256,128]{2,1,0:T(8,128)(2,1)S(1)} %shard_map.158.h_hbm) | copy-start | bytes 6291460
  50.8 33.4 %all-to-all-start.1 = ((bf16[32,2,128,128]{3,2,1,0:T(8,128)(2,1)}), bf16[32,2,128,128]{3,2,1,0:T(8,128)(2,1)S(1)}, u32[]{:S(2)}, u32[]{:S(2)}) async-start(bf16[32,2,128,128]{3,2,1,0:T(8,128)(2,1)} %get-tuple-element.13), calls=%async_computation.1 | async-start | bytes 4194304 | tf_op jit(solution)/shard_map/all_to_all | solution.py:462
  55.7 28.6 %copy-start.1 = (bf16[1,128,4096]{2,1,0:T(8,128)(2,1)S(1)}, bf16[1,128,4096]{2,1,0:T(8,128)(2,1)}, u32[]{:S(2)}) copy-start(bf16[1,128,4096]{2,1,0:T(8,128)(2,1)} %param.16) | copy-start | bytes 3145732
  62.7 23.0 %collective-permute-start = (f32[8,1024]{1,0:T(8,128)S(1)}, f32[8,1024]{1,0:T(8,128)S(1)}, u32[]{:S(2)}, u32[]{:S(2)}) collective-permute-start(f32[8,1024]{1,0:T(8,128)S(1)} %get-tuple-element.25), channel_id=1, source_target_pairs={{0,32},{32,64},{64,96},{96,0},{1,33},{33,65},{65,97},{97,1},{2,34}... | collective-permute-start | bytes 98312 | tf_op jit(solution)/shard_map/ppermute | solution.py:473
  62.8 22.9 %collective-permute-start.1 = (f32[8,1024]{1,0:T(8,128)S(1)}, f32[8,1024]{1,0:T(8,128)S(1)}, u32[]{:S(2)}, u32[]{:S(2)}) collective-permute-start(f32[8,1024]{1,0:T(8,128)S(1)} %get-tuple-element.24), channel_id=1, source_target_pairs={{0,64},{32,96},{64,0},{96,32},{1,65},{33,97},{65,1},{97,33},{2,66}... | collective-permute-start | bytes 98312 | tf_op jit(solution)/shard_map/ppermute | solution.py:473
  65.8 20.0 %collective-permute-start.2 = (f32[8,1024]{1,0:T(8,128)S(1)}, f32[8,1024]{1,0:T(8,128)S(1)}, u32[]{:S(2)}, u32[]{:S(2)}) collective-permute-start(f32[8,1024]{1,0:T(8,128)S(1)} %get-tuple-element.23), channel_id=1, source_target_pairs={{0,96},{32,0},{64,32},{96,64},{1,97},{33,1},{65,33},{97,65},{2,98}... | collective-permute-start | bytes 98312 | tf_op jit(solution)/shard_map/ppermute | solution.py:473
